TPU v7x, 32 devices: a whole 2x2x4 slice. The times are simulated.
32 devices in a mesh: groups: 2 (over y), tx: 16 (over z, x, core).
Axes of the slice: x: 2, y: 2, z: 4, core: 2. Of those that a mesh axis runs over, the one named last changes fastest.
Arguments:
- mask: bfloat16 [8192, 1024], P(('groups', 'tx')), parts along dimension 0, may hold values from -1 to 1
- kernel_spectra: float32 [2, 96, 12, 128], replicated, may hold values from -3 to 3
- kernel_weights: float32 [12], replicated, may hold values from 0.1 to 1
- threshold: float32 [1], replicated, may hold values from 0.4 to 1.2
- eval_tile: int32 [16384], P(('groups', 'tx')), parts along dimension 0, may hold values from 0 to 15, as said below
- site_coords: float32 [2, 16, 16384], P(None, None, ('groups', 'tx')), parts along dimension 2, may hold values from 0 to 1
- bias_steps: int32 [16384], P(('groups', 'tx')), parts along dimension 0, may hold values from -4 to 4
Outputs:
- resist: float32 [8192, 1024], P(('groups', 'tx')), parts along dimension 0
- new_bias: float32 [16384], P(('groups', 'tx')), parts along dimension 0
There are 2 independent parts, one for each index of `groups`. A program takes and returns all parts, laid end to end along the dimension named above; an argument that names none is the same for every part. Nothing has to cross between parts.
Inputs may be any that keep to these rules, and one draw needn't show every extreme that they name: `eval_tile`: the evaluating tile of a fragment owned by tile t is t - 1, t or t + 1. One owning tile sends at most 256 fragments to each evaluating tile and exactly 256 to at least one of them; in every draw some tile receives exactly 256 fragments from each of the three owners beside it or itself.
All inputs are finite; a program needn't handle non-finite values.
Results may differ from a plain program's by a relative error of at most 0.0019.
Values may be sent and summed in bfloat16 or wider, within the bound.
No kernel may reach another device: no remote copies, remote signals or barrier semaphores. Data moves between devices by JAX's collectives and lax.ppermute only.
A program may use at most 64 MiB of HBM per device.

v0:
```python
import math

import jax
import jax.numpy as jnp
from jax import lax
from jax.sharding import PartitionSpec as P

HALO = 256
BLUR_REACH = 8
SITES = 16


blur_sigma = 3.0
bias_step = 0.5
bias_gain = 2.0


def padded(block, sides, width):
    for axis, dim in sides:
        count = lax.axis_size(axis)
        forward = [(i, i + 1) for i in range(count - 1)]
        backward = [(target, source) for source, target in forward]
        low = lax.ppermute(
            lax.slice_in_dim(block, block.shape[dim] - width, None, axis=dim), axis, forward
        )
        high = lax.ppermute(lax.slice_in_dim(block, 0, width, axis=dim), axis, backward)
        block = jnp.concatenate([low, block, high], axis=dim)
    return block


def twiddle(position, frequency, period, amplitude):
    phase_index = position[:, None] * frequency[None, :] % period
    phase_angle = phase_index.astype(jnp.float32) * (2.0 * math.pi / period)
    return (jnp.cos(phase_angle) * amplitude, jnp.sin(phase_angle) * amplitude)


def centered(count):
    return jnp.arange(count, dtype=jnp.int32) - count // 2


def imaging_tables(tile_rows, tile_cols, window_rows, row_freqs, col_freqs, halo_rows):
    col_cos, col_sin = twiddle(
        jnp.arange(tile_cols, dtype=jnp.int32),
        centered(col_freqs),
        tile_cols,
        1.0 / math.sqrt(tile_cols),
    )
    col_forward = jnp.concatenate([col_cos, -col_sin], axis=1).astype(jnp.bfloat16)
    row_cos, row_sin = twiddle(
        centered(row_freqs),
        jnp.arange(window_rows, dtype=jnp.int32),
        window_rows,
        1.0 / math.sqrt(window_rows),
    )
    row_forward = jnp.concatenate([row_cos, -row_sin], axis=0).astype(jnp.bfloat16)
    back_cos, back_sin = twiddle(
        jnp.arange(tile_rows, dtype=jnp.int32) + halo_rows,
        centered(row_freqs),
        window_rows,
        1.0 / math.sqrt(row_freqs),
    )
    row_inverse = jnp.concatenate([back_cos, back_sin], axis=0).astype(jnp.bfloat16)
    out_cos, out_sin = twiddle(
        centered(col_freqs),
        jnp.arange(tile_cols, dtype=jnp.int32),
        tile_cols,
        1.0 / math.sqrt(col_freqs),
    )
    upper_half = jnp.concatenate([out_cos, out_sin], axis=1)
    lower_half = jnp.concatenate([-out_sin, out_cos], axis=1)
    col_inverse = jnp.concatenate([upper_half, lower_half], axis=0).astype(jnp.bfloat16)
    return (col_forward, row_forward, row_inverse, col_inverse)


def tile_intensity(col_spectra, tables, kernel_spectra, kernel_weights):
    row_forward = tables[1]
    row_inverse = tables[2]
    col_inverse = tables[3]
    row_freqs = kernel_spectra.shape[1]
    kernel_count = kernel_spectra.shape[2]
    col_freqs = kernel_spectra.shape[3]
    tile_rows = row_inverse.shape[0] // 2
    tile_cols = col_inverse.shape[1] // 2
    row_product = jnp.dot(row_forward, col_spectra, preferred_element_type=jnp.float32)
    spec_real = row_product[:row_freqs, :col_freqs] - row_product[row_freqs:, col_freqs:]
    spec_imag = row_product[:row_freqs, col_freqs:] + row_product[row_freqs:, :col_freqs]
    kern_real = kernel_spectra[0]
    kern_imag = kernel_spectra[1]
    prod_real = (kern_real * spec_real[:, None, :] - kern_imag * spec_imag[:, None, :]).astype(
        jnp.bfloat16
    )
    prod_imag = (kern_real * spec_imag[:, None, :] + kern_imag * spec_real[:, None, :]).astype(
        jnp.bfloat16
    )
    flat_width = kernel_count * col_freqs
    joined = jnp.concatenate(
        [prod_real.reshape(row_freqs, flat_width), prod_imag.reshape(row_freqs, flat_width)], axis=1
    )
    back_product = jnp.dot(row_inverse, joined, preferred_element_type=jnp.float32)
    half_real = (
        back_product[:tile_rows, :flat_width] - back_product[tile_rows:, flat_width:]
    ).astype(jnp.bfloat16)
    half_imag = (
        back_product[:tile_rows, flat_width:] + back_product[tile_rows:, :flat_width]
    ).astype(jnp.bfloat16)
    stacked = jnp.concatenate(
        [
            half_real.reshape(tile_rows, kernel_count, col_freqs),
            half_imag.reshape(tile_rows, kernel_count, col_freqs),
        ],
        axis=2,
    )
    stacked = jnp.transpose(stacked, (1, 0, 2))

    def add_kernel(intensity_sum, inputs):
        kernel_block, kernel_weight = inputs
        field_pair = jnp.dot(kernel_block, col_inverse, preferred_element_type=jnp.float32)
        field_real = field_pair[:, :tile_cols]
        field_imag = field_pair[:, tile_cols:]
        return (
            intensity_sum + kernel_weight * (field_real * field_real + field_imag * field_imag),
            None,
        )

    start_sum = jnp.zeros((tile_rows, tile_cols), jnp.float32)
    intensity_sum, unused_out = lax.scan(add_kernel, start_sum, (stacked, kernel_weights))
    return intensity_sum.astype(jnp.bfloat16)


def blur_weight(offset, reach):
    offset_value = offset.astype(jnp.float32)
    all_offsets = jnp.arange(-reach, reach + 1, dtype=jnp.int32).astype(jnp.float32)
    norm_sum = jnp.sum(jnp.exp(-all_offsets * all_offsets / (2.0 * blur_sigma * blur_sigma)))
    inside = jnp.abs(offset) <= reach
    return jnp.where(
        inside,
        jnp.exp(-offset_value * offset_value / (2.0 * blur_sigma * blur_sigma)) / norm_sum,
        jnp.float32(0.0),
    )


def blur_tables(tile_rows, tile_cols, reach):
    col_diff = (
        jnp.arange(tile_cols, dtype=jnp.int32)[None, :]
        - jnp.arange(tile_cols, dtype=jnp.int32)[:, None]
    )
    col_blur = blur_weight(col_diff, reach).astype(jnp.bfloat16)
    row_diff = (
        jnp.arange(tile_rows + 2 * reach, dtype=jnp.int32)[None, :]
        - reach
        - jnp.arange(tile_rows, dtype=jnp.int32)[:, None]
    )
    row_blur = blur_weight(row_diff, reach).astype(jnp.bfloat16)
    return (col_blur, row_blur)


def interp_weights(frac, extent):
    position = frac * (extent - 1)
    low_index = jnp.minimum(jnp.floor(position), extent - 2)
    part = position - low_index
    grid_line = jnp.arange(extent, dtype=jnp.int32).astype(jnp.float32)
    low_hit = (grid_line[None, :] == low_index[:, None]).astype(jnp.float32)
    high_hit = (grid_line[None, :] == low_index[:, None] + 1.0).astype(jnp.float32)
    return low_hit * (1.0 - part)[:, None] + high_hit * part[:, None]


def sample_block(resist, row_frac, col_frac):
    tile_rows, tile_cols = resist.shape
    row_weight = interp_weights(row_frac, tile_rows)
    col_weight = interp_weights(col_frac, tile_cols)
    picked = jnp.dot(
        row_weight, resist, preferred_element_type=jnp.float32, precision=lax.Precision.HIGHEST
    )
    return jnp.sum(picked * col_weight, axis=1)


def slot_ranks(target, target_count):
    frag_count = target.shape[0]
    member = (target[None, :] == jnp.arange(target_count, dtype=jnp.int32)[:, None]).astype(
        jnp.float32
    )
    line = jnp.arange(frag_count, dtype=jnp.int32)
    upper = (line[:, None] <= line[None, :]).astype(jnp.float32)
    inclusive = jnp.dot(
        member, upper, preferred_element_type=jnp.float32, precision=lax.Precision.HIGHEST
    )
    return jnp.sum(member * (inclusive - 1.0), axis=0).astype(jnp.int32)


def shards(mask, kernel_spectra, kernel_weights, threshold, eval_tile, site_coords, bias_steps):
    tile_rows, tile_cols = mask.shape
    window_rows = tile_rows + 2 * HALO
    row_freqs = kernel_spectra.shape[1]
    col_freqs = kernel_spectra.shape[3]
    tables = imaging_tables(tile_rows, tile_cols, window_rows, row_freqs, col_freqs, HALO)
    window = padded(mask, (("tx", 0),), HALO)
    col_spectra = jnp.dot(window, tables[0], preferred_element_type=jnp.float32).astype(
        jnp.bfloat16
    )
    intensity = tile_intensity(col_spectra, tables, kernel_spectra, kernel_weights)
    col_blur, row_blur = blur_tables(tile_rows, tile_cols, BLUR_REACH)
    extended = padded(intensity, (("tx", 0),), BLUR_REACH)
    col_blurred = jnp.dot(extended, col_blur, preferred_element_type=jnp.float32).astype(
        jnp.bfloat16
    )
    resist = jnp.dot(row_blur, col_blurred, preferred_element_type=jnp.float32)
    frag_count = eval_tile.shape[0]
    capacity = frag_count // 2
    records = site_coords.reshape(2 * SITES, frag_count)
    offset_index = eval_tile - lax.axis_index("tx") + 1
    slot_rank = slot_ranks(offset_index, 3)
    target_slot = offset_index * capacity + slot_rank
    slot_line = jnp.arange(3 * capacity, dtype=jnp.int32)
    selector = (target_slot[:, None] == slot_line[None, :]).astype(jnp.float32)
    packed = jnp.dot(
        records, selector, preferred_element_type=jnp.float32, precision=lax.Precision.HIGHEST
    )
    buffer = jnp.transpose(packed.reshape(2 * SITES, 3, capacity), (1, 0, 2))
    arrived = padded(buffer, (("tx", 0),), 1)
    arrived_blocks = arrived[0::2]
    block_means = []
    for block_number in range(3):
        block = arrived_blocks[block_number]
        values = sample_block(resist, block[:SITES].reshape(-1), block[SITES:].reshape(-1))
        block_means.append(jnp.mean(values.reshape(SITES, capacity), axis=0))
    site_means = jnp.stack(block_means, axis=0)
    returned = padded(site_means, (("tx", 0),), 1)[0::2]
    site_mean = jnp.sum(selector * returned.reshape(-1)[None, :], axis=1)
    new_bias = bias_step * bias_steps.astype(jnp.float32) - bias_gain * (site_mean - threshold[0])
    return (resist, new_bias)


def solution(mesh):
    placed = (
        P(("groups", "tx"), None),
        P(),
        P(),
        P(),
        P(("groups", "tx")),
        P(None, None, ("groups", "tx")),
        P(("groups", "tx")),
    )
    return jax.shard_map(
        shards,
        mesh=mesh,
        in_specs=placed,
        out_specs=(P(("groups", "tx"), None), P(("groups", "tx"))),
        check_vma=False,
    )
```

profile of v0, /device:TPU:24, one launch (start us, length us, event | category | flops | bytes accessed | tf_op | source)
XLA Modules:
  0.0 174.5 jit_solution(9952004148682430072)
XLA Ops:
  0.6 2.1 %collective-permute-start = (bf16[256,1024]{1,0:T(8,128)(2,1)}, bf16[256,1024]{1,0:T(8,128)(2,1)}, u32[]{:S(2)}, u32[]{:S(2)}) collective-permute-start(bf16[256,1024]{1,0:T(8,128)(2,1)} %param.9), channel_id=1, source_target_pairs={{0,1},{1,2},{2,3},{3,4},{4,5},{5,6},{6,7},{7,8},{8,9},{9,10},{10,1... | collective-permute-start | bytes 1572872 | tf_op jit(solution)/shard_map/ppermute | solution.py:23
  2.7 4.5 %collective-permute-start.1 = (bf16[256,1024]{1,0:T(8,128)(2,1)}, bf16[256,1024]{1,0:T(8,128)(2,1)}, u32[]{:S(2)}, u32[]{:S(2)}) collective-permute-start(bf16[256,1024]{1,0:T(8,128)(2,1)} %param.9), channel_id=1, source_target_pairs={{1,0},{2,1},{3,2},{4,3},{5,4},{6,5},{7,6},{8,7},{9,8},{10,9},{11,1... | collective-permute-start | bytes 1572872 | tf_op jit(solution)/shard_map/ppermute | solution.py:26
  10.8 1.9 %collective-permute-start.4 = (f32[1,32,256]{2,0,1:T(1,128)}, f32[1,32,256]{2,0,1:T(1,128)}, u32[]{:S(2)}, u32[]{:S(2)}) collective-permute-start(f32[1,32,256]{2,0,1:T(1,128)} %get-tuple-element.84), channel_id=1, source_target_pairs={{0,1},{1,2},{2,3},{3,4},{4,5},{5,6},{6,7},{7,8},{8,9},{9,10},{10,1... | collective-permute-start | bytes 98312 | tf_op jit(solution)/shard_map/ppermute | solution.py:23
  12.7 4.5 %collective-permute-start.5 = (f32[1,32,256]{2,0,1:T(1,128)}, f32[1,32,256]{2,0,1:T(1,128)}, u32[]{:S(2)}, u32[]{:S(2)}) collective-permute-start(f32[1,32,256]{2,0,1:T(1,128)} %get-tuple-element.85), channel_id=1, source_target_pairs={{1,0},{2,1},{3,2},{4,3},{5,4},{6,5},{7,6},{8,7},{9,8},{10,9},{11,1... | collective-permute-start | bytes 98312 | tf_op jit(solution)/shard_map/ppermute | solution.py:26
  17.3 3.0 %multiply_convert_fusion.1 = (bf16[1024,128]{1,0:T(8,128)(2,1)}, bf16[1024,128]{1,0:T(8,128)(2,1)}) fusion(s32[128]{0:T(128)S(1)} %iota_add_fusion.2), kind=kLoop, calls=%fused_computation.121 | loop fusion | flops 2490368 | bytes 524800 | tf_op jit(solution)/shard_map/convert.6
  20.3 2.5 %fusion.112 = (bf16[128,1024]{1,0:T(8,128)(2,1)S(1)}, bf16[128,1024]{1,0:T(8,128)(2,1)S(1)}, bf16[128,1024]{1,0:T(8,128)(2,1)S(1)}) fusion(s32[128]{0:T(128)S(1)} %iota_add_fusion.2), kind=kLoop, calls=%fused_computation.126 | loop fusion | flops 2621440 | bytes 786944 | tf_op jit(solution)/shard_map/convert.5
  24.0 2.1 %multiply_convert_fusion.2 = (bf16[96,768]{1,0:T(8,128)(2,1)}, bf16[96,768]{1,0:T(8,128)(2,1)}) fusion(s32[96]{0:T(128)S(1)} %iota_add_fusion.3), kind=kLoop, calls=%fused_computation.140 | loop fusion | flops 1032192 | bytes 295296 | tf_op jit(solution)/shard_map/convert.8
  34.2 2.5 %fusion.70 = f32[192,256]{1,0:T(8,128)S(1)} fusion(bf16[256,1024]{1,0:T(8,128)(2,1)} %collective-permute-done.1, bf16[256,1024]{1,0:T(8,128)(2,1)} %param.9, bf16[256,1024]{1,0:T(8,128)(2,1)} %collective-permute-done, bf16[1024,128]{1,0:T(8,128)(2,1)} %get-tuple-element.118, bf16[1024,128]{1,0:T(8,128)(2,1)} %get-tuple-element.117, ...), kind=kOutput, calls=%fused_computation.74 | convolution fusion | flops 484704256 | bytes 2588672 | tf_op jit(solution)/shard_map/dot_general | solution.py:84
  41.2 52.7 %while.11 = (s32[]{:T(128)}, f32[256,1024]{1,0:T(8,128)S(1)}, f32[12]{0:T(128)}, bf16[12,256,256]{1,2,0:T(8,128)(2,1)}, bf16[256,2048]{1,0:T(8,128)(2,1)}, /*index=5*/s32[]{:T(128)}, s32[]{:T(128)}) while((s32[]{:T(128)}, f32[256,1024]{1,0:T(8,128)S(1)}, f32[12]{0:T(128)}, bf16[12,256,256]{1,2,0:T(8,128)(2,1)}, ...), condition=%wide.region_2.3_spmd.clone, body=%wide.region_1.2_spmd.clone.sunk | while | flops 270008320 | bytes 7471719 | solution.py:126
  41.2 1.8 %fusion.178 = f32[256,2048]{1,0:T(8,128)S(1)} fusion(bf16[256,2048]{1,0:T(8,128)(2,1)} %get-tuple-element.180, bf16[12,256,256]{1,2,0:T(8,128)(2,1)} %get-tuple-element.179, s32[]{:T(128)} %get-tuple-element.169), kind=kOutput, calls=%fused_computation.5.clone.1 | convolution fusion | flops 268435456 | bytes 3277312 | tf_op jit(solution)/shard_map/while/body/eval_jaxpr/dot_general | solution.py:117
  45.6 1.8 %fusion.178 = f32[256,2048]{1,0:T(8,128)S(1)} fusion(bf16[256,2048]{1,0:T(8,128)(2,1)} %get-tuple-element.180, bf16[12,256,256]{1,2,0:T(8,128)(2,1)} %get-tuple-element.179, s32[]{:T(128)} %get-tuple-element.169), kind=kOutput, calls=%fused_computation.5.clone.1 | convolution fusion | flops 268435456 | bytes 3277312 | tf_op jit(solution)/shard_map/while/body/eval_jaxpr/dot_general | solution.py:117
  47.4 1.3 dynamic_slice.17
  50.0 1.8 %fusion.178 = f32[256,2048]{1,0:T(8,128)S(1)} fusion(bf16[256,2048]{1,0:T(8,128)(2,1)} %get-tuple-element.180, bf16[12,256,256]{1,2,0:T(8,128)(2,1)} %get-tuple-element.179, s32[]{:T(128)} %get-tuple-element.169), kind=kOutput, calls=%fused_computation.5.clone.1 | convolution fusion | flops 268435456 | bytes 3277312 | tf_op jit(solution)/shard_map/while/body/eval_jaxpr/dot_general | solution.py:117
  54.4 1.8 %fusion.178 = f32[256,2048]{1,0:T(8,128)S(1)} fusion(bf16[256,2048]{1,0:T(8,128)(2,1)} %get-tuple-element.180, bf16[12,256,256]{1,2,0:T(8,128)(2,1)} %get-tuple-element.179, s32[]{:T(128)} %get-tuple-element.169), kind=kOutput, calls=%fused_computation.5.clone.1 | convolution fusion | flops 268435456 | bytes 3277312 | tf_op jit(solution)/shard_map/while/body/eval_jaxpr/dot_general | solution.py:117
  58.8 1.8 %fusion.178 = f32[256,2048]{1,0:T(8,128)S(1)} fusion(bf16[256,2048]{1,0:T(8,128)(2,1)} %get-tuple-element.180, bf16[12,256,256]{1,2,0:T(8,128)(2,1)} %get-tuple-element.179, s32[]{:T(128)} %get-tuple-element.169), kind=kOutput, calls=%fused_computation.5.clone.1 | convolution fusion | flops 268435456 | bytes 3277312 | tf_op jit(solution)/shard_map/while/body/eval_jaxpr/dot_general | solution.py:117
  60.5 1.3 dynamic_slice.17
  63.2 1.8 %fusion.178 = f32[256,2048]{1,0:T(8,128)S(1)} fusion(bf16[256,2048]{1,0:T(8,128)(2,1)} %get-tuple-element.180, bf16[12,256,256]{1,2,0:T(8,128)(2,1)} %get-tuple-element.179, s32[]{:T(128)} %get-tuple-element.169), kind=kOutput, calls=%fused_computation.5.clone.1 | convolution fusion | flops 268435456 | bytes 3277312 | tf_op jit(solution)/shard_map/while/body/eval_jaxpr/dot_general | solution.py:117
  67.5 1.8 %fusion.178 = f32[256,2048]{1,0:T(8,128)S(1)} fusion(bf16[256,2048]{1,0:T(8,128)(2,1)} %get-tuple-element.180, bf16[12,256,256]{1,2,0:T(8,128)(2,1)} %get-tuple-element.179, s32[]{:T(128)} %get-tuple-element.169), kind=kOutput, calls=%fused_computation.5.clone.1 | convolution fusion | flops 268435456 | bytes 3277312 | tf_op jit(solution)/shard_map/while/body/eval_jaxpr/dot_general | solution.py:117
  71.9 1.8 %fusion.178 = f32[256,2048]{1,0:T(8,128)S(1)} fusion(bf16[256,2048]{1,0:T(8,128)(2,1)} %get-tuple-element.180, bf16[12,256,256]{1,2,0:T(8,128)(2,1)} %get-tuple-element.179, s32[]{:T(128)} %get-tuple-element.169), kind=kOutput, calls=%fused_computation.5.clone.1 | convolution fusion | flops 268435456 | bytes 3277312 | tf_op jit(solution)/shard_map/while/body/eval_jaxpr/dot_general | solution.py:117
  76.3 1.8 %fusion.178 = f32[256,2048]{1,0:T(8,128)S(1)} fusion(bf16[256,2048]{1,0:T(8,128)(2,1)} %get-tuple-element.180, bf16[12,256,256]{1,2,0:T(8,128)(2,1)} %get-tuple-element.179, s32[]{:T(128)} %get-tuple-element.169), kind=kOutput, calls=%fused_computation.5.clone.1 | convolution fusion | flops 268435456 | bytes 3277312 | tf_op jit(solution)/shard_map/while/body/eval_jaxpr/dot_general | solution.py:117
  80.7 1.8 %fusion.178 = f32[256,2048]{1,0:T(8,128)S(1)} fusion(bf16[256,2048]{1,0:T(8,128)(2,1)} %get-tuple-element.180, bf16[12,256,256]{1,2,0:T(8,128)(2,1)} %get-tuple-element.179, s32[]{:T(128)} %get-tuple-element.169), kind=kOutput, calls=%fused_computation.5.clone.1 | convolution fusion | flops 268435456 | bytes 3277312 | tf_op jit(solution)/shard_map/while/body/eval_jaxpr/dot_general | solution.py:117
  85.1 1.8 %fusion.178 = f32[256,2048]{1,0:T(8,128)S(1)} fusion(bf16[256,2048]{1,0:T(8,128)(2,1)} %get-tuple-element.180, bf16[12,256,256]{1,2,0:T(8,128)(2,1)} %get-tuple-element.179, s32[]{:T(128)} %get-tuple-element.169), kind=kOutput, calls=%fused_computation.5.clone.1 | convolution fusion | flops 268435456 | bytes 3277312 | tf_op jit(solution)/shard_map/while/body/eval_jaxpr/dot_general | solution.py:117
  89.5 1.8 %fusion.178 = f32[256,2048]{1,0:T(8,128)S(1)} fusion(bf16[256,2048]{1,0:T(8,128)(2,1)} %get-tuple-element.180, bf16[12,256,256]{1,2,0:T(8,128)(2,1)} %get-tuple-element.179, s32[]{:T(128)} %get-tuple-element.169), kind=kOutput, calls=%fused_computation.5.clone.1 | convolution fusion | flops 268435456 | bytes 3277312 | tf_op jit(solution)/shard_map/while/body/eval_jaxpr/dot_general | solution.py:117
  94.0 1.9 %collective-permute-start.2 = (bf16[8,1024]{1,0:T(8,128)(2,1)S(1)}, bf16[8,1024]{1,0:T(8,128)(2,1)S(1)}, u32[]{:S(2)}, u32[]{:S(2)}) collective-permute-start(bf16[8,1024]{1,0:T(8,128)(2,1)S(1)} %get-tuple-element.74), channel_id=1, source_target_pairs={{0,1},{1,2},{2,3},{3,4},{4,5},{5,6},{6,7},{7,8},{8,9},{9,10},{10,1... | collective-permute-start | bytes 49160 | tf_op jit(solution)/shard_map/ppermute | solution.py:23
  95.9 4.7 %collective-permute-start.3 = (bf16[8,1024]{1,0:T(8,128)(2,1)S(1)}, bf16[8,1024]{1,0:T(8,128)(2,1)S(1)}, u32[]{:S(2)}, u32[]{:S(2)}) collective-permute-start(bf16[8,1024]{1,0:T(8,128)(2,1)S(1)} %get-tuple-element.75), channel_id=1, source_target_pairs={{1,0},{2,1},{3,2},{4,3},{5,4},{6,5},{7,6},{8,7},{9,8},{10,9},{11,1... | collective-permute-start | bytes 49160 | tf_op jit(solution)/shard_map/ppermute | solution.py:26
  101.9 1.6 fusion.64
  103.7 19.7 %multiply_reduce_fusion = f32[4096]{0:T(1024)S(1)} fusion(f32[256,1024]{1,0:T(8,128)S(1)} %fusion.64, f32[4096]{0:T(1024)S(1)} %copy-done.9, f32[4096]{0:T(1024)S(1)} %copy-done.8, f32[4096]{0:T(1024)S(1)} %copy-done.7, f32[4096]{0:T(1024)S(1)} %copy-done.6, f32[1024]{0:T(1024)S(1)} %copy-done.16, f32[4096]{0:T(1024)S(1)} %copy-done.10, ...), kind=kOutput, calls=%fused_computation.9 | convolution fusion | flops 12919500800 | bytes 1201152 | tf_op jit(solution)/shard_map/dot_general | solution.py:171
  123.4 19.7 %multiply_reduce_fusion.1 = f32[4096]{0:T(1024)S(1)} fusion(f32[256,1024]{1,0:T(8,128)S(1)} %fusion.64, f32[4096]{0:T(1024)S(1)} %copy-done.1, f32[4096]{0:T(1024)S(1)} %get-tuple-element.100, f32[4096]{0:T(1024)S(1)} %get-tuple-element.99, f32[4096]{0:T(1024)S(1)} %get-tuple-element.98, f32[1024]{0:T(1024)S(1)} %copy-done.16, f32[4096]{0:T(1024)S(1)} %copy-done.2, ...), kind=kOutput, calls=%fused_computation.10 | convolution fusion | flops 12919500800 | bytes 1201152 | tf_op jit(solution)/shard_map/dot_general | solution.py:171
  143.2 4.7 %collective-permute-start.7 = (f32[1,256]{1,0:T(1,128)S(1)}, f32[1,256]{1,0:T(1,128)S(1)}, u32[]{:S(2)}, u32[]{:S(2)}) collective-permute-start(f32[1,256]{1,0:T(1,128)S(1)} %bitcast.80), channel_id=1, source_target_pairs={{1,0},{2,1},{3,2},{4,3},{5,4},{6,5},{7,6},{8,7},{9,8},{10,9},{11,1... | collective-permute-start | bytes 3080 | tf_op jit(solution)/shard_map/ppermute | solution.py:26
  148.0 19.7 %multiply_reduce_fusion.2 = f32[4096]{0:T(1024)S(1)} fusion(f32[256,1024]{1,0:T(8,128)S(1)} %fusion.64, f32[4096]{0:T(1024)S(1)} %get-tuple-element.109, f32[4096]{0:T(1024)S(1)} %get-tuple-element.108, f32[4096]{0:T(1024)S(1)} %get-tuple-element.107, f32[4096]{0:T(1024)S(1)} %get-tuple-element.106, f32[1024]{0:T(1024)S(1)} %copy-done.16, ...), kind=kOutput, calls=%fused_computation.11 | convolution fusion | flops 12919500800 | bytes 1201152 | tf_op jit(solution)/shard_map/dot_general | solution.py:171
  167.7 1.9 %collective-permute-start.6 = (f32[1,256]{1,0:T(1,128)S(1)}, f32[1,256]{1,0:T(1,128)S(1)}, u32[]{:S(2)}, u32[]{:S(2)}) collective-permute-start(f32[1,256]{1,0:T(1,128)S(1)} %bitcast.82), channel_id=1, source_target_pairs={{0,1},{1,2},{2,3},{3,4},{4,5},{5,6},{6,7},{7,8},{8,9},{9,10},{10,1... | collective-permute-start | bytes 3080 | tf_op jit(solution)/shard_map/ppermute | solution.py:23
  169.7 3.8 %collective-permute-done.6 = f32[1,256]{1,0:T(1,128)S(1)} collective-permute-done((f32[1,256]{1,0:T(1,128)S(1)}, f32[1,256]{1,0:T(1,128)S(1)}, u32[]{:S(2)}, u32[]{:S(2)}) %collective-permute-start.6) | collective-permute-done | bytes 1056 | tf_op jit(solution)/shard_map/ppermute | solution.py:23
  (121 shorter events, 47.6 us)
Async XLA Ops:
  0.6 8.2 %copy-start = (f32[2,16,512]{2,1,0:T(8,128)S(1)}, f32[2,16,512]{2,1,0:T(8,128)}, u32[]{:S(2)}) copy-start(f32[2,16,512]{2,1,0:T(8,128)} %param.14) | copy-start | bytes 196612
  0.6 33.5 %collective-permute-start = (bf16[256,1024]{1,0:T(8,128)(2,1)}, bf16[256,1024]{1,0:T(8,128)(2,1)}, u32[]{:S(2)}, u32[]{:S(2)}) collective-permute-start(bf16[256,1024]{1,0:T(8,128)(2,1)} %param.9), channel_id=1, source_target_pairs={{0,1},{1,2},{2,3},{3,4},{4,5},{5,6},{6,7},{7,8},{8,9},{9,10},{10,1... | collective-permute-start | bytes 1572872 | tf_op jit(solution)/shard_map/ppermute | solution.py:23
  2.7 31.5 %collective-permute-start.1 = (bf16[256,1024]{1,0:T(8,128)(2,1)}, bf16[256,1024]{1,0:T(8,128)(2,1)}, u32[]{:S(2)}, u32[]{:S(2)}) collective-permute-start(bf16[256,1024]{1,0:T(8,128)(2,1)} %param.9), channel_id=1, source_target_pairs={{1,0},{2,1},{3,2},{4,3},{5,4},{6,5},{7,6},{8,7},{9,8},{10,9},{11,1... | collective-permute-start | bytes 1572872 | tf_op jit(solution)/shard_map/ppermute | solution.py:26
  8.8 0.6 copy-start.14
  10.8 20.7 %collective-permute-start.4 = (f32[1,32,256]{2,0,1:T(1,128)}, f32[1,32,256]{2,0,1:T(1,128)}, u32[]{:S(2)}, u32[]{:S(2)}) collective-permute-start(f32[1,32,256]{2,0,1:T(1,128)} %get-tuple-element.84), channel_id=1, source_target_pairs={{0,1},{1,2},{2,3},{3,4},{4,5},{5,6},{6,7},{7,8},{8,9},{9,10},{10,1... | collective-permute-start | bytes 98312 | tf_op jit(solution)/shard_map/ppermute | solution.py:23
  12.7 18.8 %collective-permute-start.5 = (f32[1,32,256]{2,0,1:T(1,128)}, f32[1,32,256]{2,0,1:T(1,128)}, u32[]{:S(2)}, u32[]{:S(2)}) collective-permute-start(f32[1,32,256]{2,0,1:T(1,128)} %get-tuple-element.85), channel_id=1, source_target_pairs={{1,0},{2,1},{3,2},{4,3},{5,4},{6,5},{7,6},{8,7},{9,8},{10,9},{11,1... | collective-permute-start | bytes 98312 | tf_op jit(solution)/shard_map/ppermute | solution.py:26
  41.2 60.7 %copy-start.18 = (s32[272]{0:T(512)S(1)}, s32[272]{0:T(512)}, u32[]{:S(2)}) copy-start(s32[272]{0:T(512)} %iota_add_fusion) | copy-start | bytes 3268
  94.0 6.8 %collective-permute-start.2 = (bf16[8,1024]{1,0:T(8,128)(2,1)S(1)}, bf16[8,1024]{1,0:T(8,128)(2,1)S(1)}, u32[]{:S(2)}, u32[]{:S(2)}) collective-permute-start(bf16[8,1024]{1,0:T(8,128)(2,1)S(1)} %get-tuple-element.74), channel_id=1, source_target_pairs={{0,1},{1,2},{2,3},{3,4},{4,5},{5,6},{6,7},{7,8},{8,9},{9,10},{10,1... | collective-permute-start | bytes 49160 | tf_op jit(solution)/shard_map/ppermute | solution.py:23
  95.9 6.0 %collective-permute-start.3 = (bf16[8,1024]{1,0:T(8,128)(2,1)S(1)}, bf16[8,1024]{1,0:T(8,128)(2,1)S(1)}, u32[]{:S(2)}, u32[]{:S(2)}) collective-permute-start(bf16[8,1024]{1,0:T(8,128)(2,1)S(1)} %get-tuple-element.75), channel_id=1, source_target_pairs={{1,0},{2,1},{3,2},{4,3},{5,4},{6,5},{7,6},{8,7},{9,8},{10,9},{11,1... | collective-permute-start | bytes 49160 | tf_op jit(solution)/shard_map/ppermute | solution.py:26
  100.6 2.9 %copy-start.6 = (f32[4096]{0:T(1024)S(1)}, f32[4096]{0:T(1024)}, u32[]{:S(2)}) copy-start(f32[4096]{0:T(1024)} %get-tuple-element.90) | copy-start | bytes 49156
  100.7 2.9 %copy-start.7 = (f32[4096]{0:T(1024)S(1)}, f32[4096]{0:T(1024)}, u32[]{:S(2)}) copy-start(f32[4096]{0:T(1024)} %get-tuple-element.91) | copy-start | bytes 49156
  100.7 2.9 %copy-start.8 = (f32[4096]{0:T(1024)S(1)}, f32[4096]{0:T(1024)}, u32[]{:S(2)}) copy-start(f32[4096]{0:T(1024)} %get-tuple-element.92) | copy-start | bytes 49156
  100.7 2.9 %copy-start.9 = (f32[4096]{0:T(1024)S(1)}, f32[4096]{0:T(1024)}, u32[]{:S(2)}) copy-start(f32[4096]{0:T(1024)} %get-tuple-element.93) | copy-start | bytes 49156
  100.7 2.9 %copy-start.10 = (f32[4096]{0:T(1024)S(1)}, f32[4096]{0:T(1024)}, u32[]{:S(2)}) copy-start(f32[4096]{0:T(1024)} %get-tuple-element.127) | copy-start | bytes 49156
  100.7 2.9 %copy-start.11 = (f32[4096]{0:T(1024)S(1)}, f32[4096]{0:T(1024)}, u32[]{:S(2)}) copy-start(f32[4096]{0:T(1024)} %get-tuple-element.128) | copy-start | bytes 49156
  100.7 2.9 %copy-start.12 = (f32[4096]{0:T(1024)S(1)}, f32[4096]{0:T(1024)}, u32[]{:S(2)}) copy-start(f32[4096]{0:T(1024)} %get-tuple-element.129) | copy-start | bytes 49156
  100.7 2.9 %copy-start.13 = (f32[4096]{0:T(1024)S(1)}, f32[4096]{0:T(1024)}, u32[]{:S(2)}) copy-start(f32[4096]{0:T(1024)} %get-tuple-element.130) | copy-start | bytes 49156
  100.7 2.9 %copy-start.16 = (f32[1024]{0:T(1024)S(1)}, f32[1024]{0:T(1024)}, u32[]{:S(2)}) copy-start(f32[1024]{0:T(1024)} %iota_convert_fusion) | copy-start | bytes 12292
  100.7 2.9 %copy-start.20 = (f32[256]{0:T(256)S(1)}, f32[256]{0:T(256)}, u32[]{:S(2)}) copy-start(f32[256]{0:T(256)} %iota_convert_fusion.1) | copy-start | bytes 3076
  103.5 44.5 %copy-start.19 = (f32[256,1024]{1,0:T(8,128)}, f32[256,1024]{1,0:T(8,128)S(1)}, u32[]{:S(2)}) copy-start(f32[256,1024]{1,0:T(8,128)S(1)} %fusion.64) | copy-start | bytes 3145732
  103.6 19.8 %copy-start.1 = (f32[4096]{0:T(1024)S(1)}, f32[4096]{0:T(1024)}, u32[]{:S(2)}) copy-start(f32[4096]{0:T(1024)} %get-tuple-element.101) | copy-start | bytes 49156
  103.6 19.8 %copy-start.2 = (f32[4096]{0:T(1024)S(1)}, f32[4096]{0:T(1024)}, u32[]{:S(2)}) copy-start(f32[4096]{0:T(1024)} %get-tuple-element.123) | copy-start | bytes 49156
  103.6 19.8 %copy-start.3 = (f32[4096]{0:T(1024)S(1)}, f32[4096]{0:T(1024)}, u32[]{:S(2)}) copy-start(f32[4096]{0:T(1024)} %get-tuple-element.124) | copy-start | bytes 49156
  103.6 19.8 %copy-start.4 = (f32[4096]{0:T(1024)S(1)}, f32[4096]{0:T(1024)}, u32[]{:S(2)}) copy-start(f32[4096]{0:T(1024)} %get-tuple-element.125) | copy-start | bytes 49156
  103.7 19.8 %copy-start.5 = (f32[4096]{0:T(1024)S(1)}, f32[4096]{0:T(1024)}, u32[]{:S(2)}) copy-start(f32[4096]{0:T(1024)} %get-tuple-element.126) | copy-start | bytes 49156
  143.2 26.5 %collective-permute-start.7 = (f32[1,256]{1,0:T(1,128)S(1)}, f32[1,256]{1,0:T(1,128)S(1)}, u32[]{:S(2)}, u32[]{:S(2)}) collective-permute-start(f32[1,256]{1,0:T(1,128)S(1)} %bitcast.80), channel_id=1, source_target_pairs={{1,0},{2,1},{3,2},{4,3},{5,4},{6,5},{7,6},{8,7},{9,8},{10,9},{11,1... | collective-permute-start | bytes 3080 | tf_op jit(solution)/shard_map/ppermute | solution.py:26
  148.0 25.6 %copy-start.15 = (s32[512]{0:T(512)S(1)}, s32[512]{0:T(512)}, u32[]{:S(2)}) copy-start(s32[512]{0:T(512)} %copy-done.14) | copy-start | bytes 6148
  148.0 25.9 %copy-start.17 = (s32[512]{0:T(512)S(1)}, s32[512]{0:T(512)}, u32[]{:S(2)}) copy-start(s32[512]{0:T(512)} %param.15) | copy-start | bytes 6148
  167.7 5.8 %collective-permute-start.6 = (f32[1,256]{1,0:T(1,128)S(1)}, f32[1,256]{1,0:T(1,128)S(1)}, u32[]{:S(2)}, u32[]{:S(2)}) collective-permute-start(f32[1,256]{1,0:T(1,128)S(1)} %bitcast.82), channel_id=1, source_target_pairs={{0,1},{1,2},{2,3},{3,4},{4,5},{5,6},{6,7},{7,8},{8,9},{9,10},{10,1... | collective-permute-start | bytes 3080 | tf_op jit(solution)/shard_map/ppermute | solution.py:23
where the time goes:
time: 176 us; the launch traced here: 174 us
  matrix products  86.1 us (49%)
  other arithmetic  34.5 us (20%)
  starting transfers between devices  26.4 us (15%)
  local copies, waits for them, and re-layouts  20.3 us (12%)
  waiting for transfers between devices  4.96 us (3%)
  between operations  1.91 us (1%)
    dot_general x3, matrix products, sample_block(): jnp.dot(row_weight, resist, preferred_element_type=jnp.float32, precision...  59.1 us
    dot_general x12, matrix products, add_kernel(): jnp.dot(kernel_block, col_inverse, preferred_element_type=jnp.float32)  21.2 us
    ppermute x4, starting transfers between devices, padded(): lax.ppermute(lax.slice_in_dim(block, 0, width, axis=dim), axis, backward)  18.6 us
    dynamic_slice x12, local copies, waits for them, and re-layouts, tile_intensity(): lax.scan(add_kernel, start_sum, (stacked, kernel_weights))  15.9 us
    add x12, other arithmetic, add_kernel(): intensity_sum + kernel_weight * (field_real * field_real + field_imag * f...  15.4 us
    another operation x4, other arithmetic  8.14 us
    ppermute x4, starting transfers between devices, padded(): lax.ppermute(lax.slice_in_dim(block, block.shape[dim] - width, None, axis...  7.81 us
    ppermute x4, waiting for transfers between devices, padded(): lax.ppermute(lax.slice_in_dim(block, block.shape[dim] - width, None, axis...  3.84 us
  transfers between devices with their start and end apart: 8, of which 2 were waited for; matrix products, arithmetic and copies ran while one was open for 22% of the time, Pallas kernels for 0%

commit v1 on v0

v1 whole, which is shorter than its diff:
```python
import math

import jax
import jax.numpy as jnp
import ml_dtypes
import numpy as np
from jax import lax
from jax.experimental import pallas as pl
from jax.experimental.pallas import tpu as pltpu
from jax.sharding import PartitionSpec as P

HALO = 256
BLUR_REACH = 8
SITES = 16

blur_sigma = 3.0
bias_step = 0.5
bias_gain = 2.0

F32 = jnp.float32
BF16 = jnp.bfloat16
BLOCK = 64
VMEM_BYTES = 48 * 1024 * 1024


def rounded(table):
    return np.asarray(table, np.float32).astype(ml_dtypes.bfloat16)


def halves(table):
    high = rounded(table)
    low = rounded(np.asarray(table, np.float64) - high.astype(np.float64))
    return high, low


def twiddle(position, frequency, period, amplitude):
    phase_index = (position[:, None] * frequency[None, :]) % period
    phase_angle = phase_index * (2.0 * math.pi / period)
    return np.cos(phase_angle) * amplitude, np.sin(phase_angle) * amplitude


def centered(count):
    return np.arange(count) - count // 2


def imaging_tables(tile_rows, tile_cols, row_freqs, col_freqs):
    window_rows = tile_rows + 2 * HALO
    col_cos, col_sin = twiddle(
        np.arange(tile_cols), centered(col_freqs), tile_cols, 1.0 / math.sqrt(tile_cols)
    )
    col_forward = rounded(np.concatenate([col_cos, -col_sin], axis=1))
    row_cos, row_sin = twiddle(
        centered(row_freqs), np.arange(window_rows), window_rows, 1.0 / math.sqrt(window_rows)
    )
    row_forward = rounded(np.concatenate([row_cos, -row_sin], axis=0))
    row_blocks = np.stack(
        [row_forward[:, i * tile_rows : (i + 1) * tile_rows] for i in range(3)]
    )
    back_cos, back_sin = twiddle(
        np.arange(tile_rows) + HALO, centered(row_freqs), window_rows, 1.0 / math.sqrt(row_freqs)
    )
    row_inverse = rounded(
        np.block([[back_cos, -back_sin], [back_sin, back_cos]])
    )
    samples = 2 * col_freqs
    step = tile_cols // samples
    out_cos, out_sin = twiddle(
        centered(col_freqs), np.arange(samples) * step, tile_cols, 1.0 / math.sqrt(col_freqs)
    )
    col_inverse = rounded(np.block([[out_cos, out_sin], [-out_sin, out_cos]]))
    return col_forward, row_blocks, row_inverse, col_inverse


def blur_weight(offset, reach):
    every = np.arange(-reach, reach + 1).astype(np.float64)
    norm = np.sum(np.exp(-every * every / (2.0 * blur_sigma * blur_sigma)))
    weight = np.exp(-offset.astype(np.float64) ** 2 / (2.0 * blur_sigma * blur_sigma)) / norm
    return np.where(np.abs(offset) <= reach, weight, 0.0)


def blur_tables(tile_rows, tile_cols, col_freqs, reach):
    line = np.arange(tile_cols)
    col_blur = rounded(blur_weight(line[None, :] - line[:, None], reach))
    samples = 2 * col_freqs
    step = tile_cols // samples
    offset = (line[None, :] - step * np.arange(samples)[:, None]).astype(np.float64)
    half = np.where(offset == 0, 1.0, np.sin(math.pi * offset / tile_cols))
    spread = np.where(
        offset == 0,
        (samples - 1) / samples,
        np.sin((samples - 1) * math.pi * offset / tile_cols) / (samples * half),
    )
    spread_blur = spread @ col_blur.astype(np.float64)
    row_diff = (
        np.arange(tile_rows + 2 * reach)[None, :] - reach - np.arange(tile_rows)[:, None]
    )
    row_blur = rounded(blur_weight(row_diff, reach))
    inner = row_blur[:, reach : reach + tile_rows]
    outer = np.concatenate([row_blur[:, :reach], row_blur[:, reach + tile_rows :]], axis=1)
    return halves(spread_blur), np.ascontiguousarray(inner), np.ascontiguousarray(outer)


def parity():
    return lax.rem(lax.axis_index("tx"), 2)


def spectra_kernel(mask_ref, forward_ref, rows_ref, own_ref, core_ref, chip_ref):
    col_spectra = jnp.dot(mask_ref[...], forward_ref[...], preferred_element_type=F32).astype(BF16)
    freqs, cols = own_ref.shape[0] // 2, own_ref.shape[1]
    odd = parity()

    def partial(block, out_ref):
        product = jnp.dot(rows_ref[block], col_spectra, preferred_element_type=F32)
        out_ref[:freqs, :] = product[:freqs, :cols] - product[freqs:, cols:]
        out_ref[freqs:, :] = product[:freqs, cols:] + product[freqs:, :cols]

    partial(1, own_ref)
    partial(2 * odd, core_ref)
    partial(2 - 2 * odd, chip_ref)


def pack_kernel(eval_ref, records_ref, core_ref, chip_ref, own_ref, code_ref):
    frags = eval_ref.shape[1]
    capacity = frags // 2
    me = lax.axis_index("tx")
    odd = parity()
    offset = eval_ref[...] - me + 1
    member = (
        lax.broadcasted_iota(jnp.int32, (8, frags), 0) == offset
    )
    before = lax.broadcasted_iota(jnp.int32, (frags, frags), 0)
    after = lax.broadcasted_iota(jnp.int32, (frags, frags), 1)
    upper = (before <= after).astype(F32).astype(BF16)
    counts = jnp.dot(member.astype(F32).astype(BF16), upper, preferred_element_type=F32)
    code_ref[...] = jnp.where(member, counts - 1.0, -1.0)
    records = records_ref[...]
    first = records.astype(BF16)
    rest = records - first.astype(F32)
    second = rest.astype(BF16)
    third = (rest - second.astype(F32)).astype(BF16)
    pieces = jnp.concatenate([first, second, third], axis=0)
    slots = lax.broadcasted_iota(jnp.int32, (capacity, frags), 0).astype(F32)
    count = records.shape[0]

    def packed(side, out_ref):
        chosen = (slots == code_ref[pl.ds(side, 1), :]).astype(F32).astype(BF16)
        got = lax.dot_general(
            pieces, chosen, (((1,), (1,)), ((), ())), preferred_element_type=F32
        )
        out_ref[...] = got[:count] + got[count : 2 * count] + got[2 * count :]

    packed(2 - 2 * odd, core_ref)
    packed(2 * odd, chip_ref)
    packed(1, own_ref)


def has_chip_side():
    me = lax.axis_index("tx")
    return jnp.logical_and(me != 0, me != lax.axis_size("tx") - 1)


def across():
    rest = lax.rem(lax.axis_index("tx"), 4)
    return jnp.logical_or(rest == 1, rest == 2)


def imaging_kernel(
    weights_ref, own_ref, core_ref, near_ref, far_ref, kern_ref, inverse_ref, spread_ref,
    packed_core_ref, packed_chip_ref,
    intensity_ref, pay_core_ref, pay_chip_ref,
    product_ref, half_ref,
):
    freqs, cols = own_ref.shape[0] // 2, own_ref.shape[1]
    rows = intensity_ref.shape[0]
    kernels = kern_ref.shape[1]
    odd = parity()
    chip = jnp.where(across(), near_ref[...], far_ref[...])
    chip = jnp.where(has_chip_side(), chip, 0.0)
    spectrum = own_ref[...] + core_ref[...] + chip
    spec_real, spec_imag = spectrum[:freqs], spectrum[freqs:]
    for k in range(kernels):
        kern_real, kern_imag = kern_ref[0, k], kern_ref[1, k]
        lanes = slice(k * cols, (k + 1) * cols)
        product_ref[:freqs, lanes] = (kern_real * spec_real - kern_imag * spec_imag).astype(BF16)
        product_ref[freqs:, lanes] = (kern_real * spec_imag + kern_imag * spec_real).astype(BF16)
    half_ref[...] = jnp.dot(
        inverse_ref[...], product_ref[...], preferred_element_type=F32
    ).astype(BF16)
    total = None
    for k in range(kernels):
        lanes = slice(k * cols, (k + 1) * cols)
        pair = jnp.concatenate([half_ref[:rows, lanes], half_ref[rows:, lanes]], axis=1)
        field = jnp.dot(pair, spread_ref[...], preferred_element_type=F32)
        real, imag = field[:, : 2 * cols], field[:, 2 * cols :]
        term = weights_ref[0, k] * (real * real + imag * imag)
        total = term if total is None else total + term
    rounded_total = total.astype(BF16)
    intensity_ref[...] = rounded_total
    values = rounded_total.astype(F32)
    top, bottom = values[:BLUR_REACH], values[rows - BLUR_REACH :]
    count = packed_core_ref.shape[0]
    pay_core_ref[:count] = packed_core_ref[...]
    pay_chip_ref[:count] = packed_chip_ref[...]
    pay_core_ref[count:] = jnp.where(odd == 1, top, bottom)
    pay_chip_ref[count:] = jnp.where(odd == 1, bottom, top)


def site_means(table_ref, fetch):
    tile_cols, tile_rows = table_ref.shape
    slots = fetch(0).shape[1]
    grid_rows = lax.broadcasted_iota(jnp.int32, (tile_rows, slots), 0).astype(F32)
    eight = lax.broadcasted_iota(jnp.int32, (8, slots), 0).astype(F32)
    groups = BLOCK // 8
    blocks = tile_cols // BLOCK

    def one_site(site, total):
        row_pos = fetch(site) * (tile_rows - 1)
        tent = jnp.maximum(1.0 - jnp.abs(row_pos - grid_rows), 0.0).astype(BF16)
        picked = jnp.dot(table_ref[...], tent, preferred_element_type=F32)
        col_pos = fetch(SITES + site) * (tile_cols - 1)
        block = jnp.minimum(jnp.floor(col_pos * (1.0 / BLOCK)), blocks - 1.0)
        within = jnp.broadcast_to(col_pos - block * BLOCK, (8, slots))
        block = jnp.broadcast_to(block, (8, slots))
        held = [jnp.zeros((8, slots), F32) for _ in range(groups + 1)]
        for b in range(blocks):
            hit = block == float(b)
            start = b * BLOCK
            last = groups + 1 if b < blocks - 1 else groups
            for g in range(last):
                held[g] = jnp.where(hit, picked[start + 8 * g : start + 8 * g + 8], held[g])
        for g in range(groups + 1):
            weight = jnp.maximum(1.0 - jnp.abs(within - (eight + 8.0 * g)), 0.0)
            total = total + held[g] * weight
        return total

    total = lax.fori_loop(0, SITES, one_site, jnp.zeros((8, slots), F32))
    return jnp.broadcast_to(jnp.sum(total, axis=0, keepdims=True) * (1.0 / SITES), (8, slots))


def resist_kernel(
    intensity_ref, core_ref, near_ref, far_ref, inner_ref, outer_ref,
    high_ref, low_ref, high_t_ref, low_t_ref,
    resist_ref, table_ref, coords_core_ref, mean_chip_ref, coords_ref,
):
    odd = parity()
    count = coords_ref.shape[0]
    chip = jnp.where(across(), near_ref[...], far_ref[...])
    coords_ref[...] = chip[:count]
    core = core_ref[...]
    coords_core_ref[...] = core[:count]
    chip_edge = jnp.where(has_chip_side(), chip[count:], 0.0)
    core_edge = core[count:]
    above = jnp.where(odd == 1, core_edge, chip_edge)
    below = jnp.where(odd == 1, chip_edge, core_edge)
    edges = jnp.concatenate([above, below], axis=0).astype(BF16)
    blurred = jnp.dot(inner_ref[...], intensity_ref[...], preferred_element_type=F32)
    blurred += jnp.dot(outer_ref[...], edges, preferred_element_type=F32)
    high = blurred.astype(BF16)
    low = (blurred - high.astype(F32)).astype(BF16)

    resist_ref[...] = (
        jnp.dot(high, high_ref[...], preferred_element_type=F32)
        + jnp.dot(low, high_ref[...], preferred_element_type=F32)
        + jnp.dot(high, low_ref[...], preferred_element_type=F32)
    )

    def crossed(left, right):
        return lax.dot_general(left, right, (((1,), (1,)), ((), ())), preferred_element_type=F32)

    table_ref[...] = (
        crossed(high_t_ref[...], high)
        + crossed(high_t_ref[...], low)
        + crossed(low_t_ref[...], high)
    ).astype(BF16)
    mean_chip_ref[...] = site_means(table_ref, lambda i: coords_ref[pl.ds(i, 1), :])


def mean_kernel(table_ref, coords_ref, mean_ref):
    mean_ref[...] = site_means(table_ref, lambda i: coords_ref[pl.ds(i, 1), :])


def bias_kernel(threshold_ref, code_ref, own_ref, core_ref, near_ref, far_ref, steps_ref, out_ref):
    frags = code_ref.shape[1]
    capacity = frags // 2
    odd = parity()
    chip = jnp.where(across(), near_ref[...], far_ref[...])
    slots = lax.broadcasted_iota(jnp.int32, (capacity, frags), 0).astype(F32)
    lanes = lax.broadcasted_iota(jnp.int32, (8, capacity), 0)
    total = jnp.zeros((1, frags), F32)
    for side, mean in ((1, own_ref[...]), (2 - 2 * odd, core_ref[...]), (2 * odd, chip)):
        first = mean.astype(BF16)
        rest = mean - first.astype(F32)
        second = rest.astype(BF16)
        third = (rest - second.astype(F32)).astype(BF16)
        parts = jnp.where(
            lanes == 0, first.astype(F32),
            jnp.where(lanes == 1, second.astype(F32), jnp.where(lanes == 2, third.astype(F32), 0.0)),
        ).astype(BF16)
        chosen = (slots == code_ref[pl.ds(side, 1), :]).astype(F32).astype(BF16)
        got = jnp.dot(parts, chosen, preferred_element_type=F32)
        total = total + jnp.sum(got, axis=0, keepdims=True)
    out_ref[...] = bias_step * steps_ref[...].astype(F32) - bias_gain * (total - threshold_ref[0])


def swaps(count):
    core = [(i, i ^ 1) for i in range(count)]
    near = [(i, i ^ 3) for i in range(count)]
    partner = {0: 1, 1: 0, count - 1: count - 2, count - 2: count - 1}
    for low in range(0, count - 4, 4):
        for a, b in ((low + 3, low + 4), (low + 2, low + 5)):
            partner[a], partner[b] = b, a
    far = [(i, partner[i]) for i in range(count)]
    return core, near, far


def exchange(to_core, to_chip):
    core, near, far = swaps(lax.axis_size("tx"))
    got_far = lax.ppermute(to_chip, "tx", far)
    got_near = lax.ppermute(to_chip, "tx", near)
    got_core = lax.ppermute(to_core, "tx", core)
    return got_core, got_near, got_far


def call(kernel, outs, args, smem=(), scratch=(), name=None):
    specs = [
        pl.BlockSpec(memory_space=pltpu.SMEM if i in smem else pltpu.VMEM) for i in range(len(args))
    ]
    return pl.pallas_call(
        kernel,
        out_shape=[jax.ShapeDtypeStruct(s, d) for s, d in outs],
        in_specs=specs,
        out_specs=[pl.BlockSpec(memory_space=pltpu.VMEM) for _ in outs],
        scratch_shapes=list(scratch),
        compiler_params=pltpu.CompilerParams(vmem_limit_bytes=VMEM_BYTES),
        name=name,
    )(*args)


def shards(mask, kernel_spectra, kernel_weights, threshold, eval_tile, site_coords, bias_steps):
    tile_rows, tile_cols = mask.shape
    _, row_freqs, kernels, col_freqs = kernel_spectra.shape
    frags = eval_tile.shape[0]
    capacity = frags // 2
    samples = 2 * col_freqs
    flat = kernels * col_freqs
    records = 2 * SITES
    col_forward, row_blocks, row_inverse, col_inverse = imaging_tables(
        tile_rows, tile_cols, row_freqs, col_freqs
    )
    (high, low), inner, outer = blur_tables(tile_rows, tile_cols, col_freqs, BLUR_REACH)
    spectrum = ((2 * row_freqs, col_freqs), F32)
    packed = ((records, capacity), F32)
    payload = ((records + BLUR_REACH, capacity), F32)
    means = ((8, capacity), F32)

    own, to_core, to_chip = call(
        spectra_kernel, [spectrum] * 3, (mask, col_forward, row_blocks), name="spectra"
    )
    from_core, from_near, from_far = exchange(to_core, to_chip)
    packed_core, packed_chip, packed_own, code = call(
        pack_kernel,
        [packed] * 3 + [((8, frags), F32)],
        (eval_tile.reshape(1, frags), site_coords.reshape(records, frags)),
        name="pack",
    )
    kern = jnp.transpose(kernel_spectra, (0, 2, 1, 3))
    intensity, pay_core, pay_chip = call(
        imaging_kernel,
        [((tile_rows, samples), BF16), payload, payload],
        (
            kernel_weights.reshape(1, kernels), own, from_core, from_near, from_far,
            kern, row_inverse, col_inverse, packed_core, packed_chip,
        ),
        smem=(0,),
        scratch=[
            pltpu.VMEM((2 * row_freqs, flat), BF16),
            pltpu.VMEM((2 * tile_rows, flat), BF16),
        ],
        name="imaging",
    )
    edge_core, edge_near, edge_far = exchange(pay_core, pay_chip)
    resist, table, coords_core, mean_chip = call(
        resist_kernel,
        [
            ((tile_rows, tile_cols), F32),
            ((tile_cols, tile_rows), BF16),
            packed,
            means,
        ],
        (
            intensity, edge_core, edge_near, edge_far, inner, outer,
            high, low, np.ascontiguousarray(high.T), np.ascontiguousarray(low.T),
        ),
        scratch=[pltpu.VMEM((records, capacity), F32)],
        name="resist",
    )
    core, near, far = swaps(lax.axis_size("tx"))
    back_far = lax.ppermute(mean_chip, "tx", far)
    back_near = lax.ppermute(mean_chip, "tx", near)
    (mean_core,) = call(mean_kernel, [means], (table, coords_core), name="mean_core")
    back_core = lax.ppermute(mean_core, "tx", core)
    (mean_own,) = call(mean_kernel, [means], (table, packed_own), name="mean_own")
    (new_bias,) = call(
        bias_kernel,
        [((1, frags), F32)],
        (threshold, code, mean_own, back_core, back_near, back_far, bias_steps.reshape(1, frags)),
        smem=(0,),
        name="bias",
    )
    return resist, new_bias.reshape(frags)


def solution(mesh):
    placed = (
        P(("groups", "tx"), None),
        P(),
        P(),
        P(),
        P(("groups", "tx")),
        P(None, None, ("groups", "tx")),
        P(("groups", "tx")),
    )
    return jax.shard_map(
        shards,
        mesh=mesh,
        in_specs=placed,
        out_specs=(P(("groups", "tx"), None), P(("groups", "tx"))),
        check_vma=False,
    )
```

time: 176 us -> 43.9 us (0.25)
  the two profiles are of different devices: /device:TPU:24 before, /device:TPU:0 now
where the time goes in v1:
time: 43.9 us; the launch traced here: 43.3 us
  Pallas kernels  22.2 us (51%)
  starting transfers between devices  9.31 us (21%)
  local copies, waits for them, and re-layouts  5.92 us (13%)
  waiting for transfers between devices  4.42 us (10%)
  between operations  1.47 us (3%)
    pallas_call x7, Pallas kernels, call(): pl.pallas_call(kernel, out_shape=[jax.ShapeDtypeStruct(s, d) for s, d in...  22.2 us
    unnamed x32, local copies, waits for them, and re-layouts  5.92 us
    ppermute x2, starting transfers between devices, exchange(): got_near = lax.ppermute(to_chip, 'tx', near)  4.68 us
    ppermute x2, waiting for transfers between devices, exchange(): got_near = lax.ppermute(to_chip, 'tx', near)  4.4 us
    ppermute x1, starting transfers between devices, shards(): back_near = lax.ppermute(mean_chip, 'tx', near)  2.9 us
    ppermute x2, starting transfers between devices, exchange(): got_far = lax.ppermute(to_chip, 'tx', far)  1.07 us
  transfers between devices with their start and end apart: 9, of which 2 were waited for; matrix products, arithmetic and copies ran while one was open for 0% of the time, Pallas kernels for 14%

profile of v1, /device:TPU:0, one launch (start us, length us, event | category | flops | bytes accessed | tf_op | source)
XLA Modules:
  0.0 43.3 jit_solution(18396052801990661684)
XLA Ops:
  0.7 1.1 %copy-done.5 = bf16[256,1024]{1,0:T(8,128)(2,1)S(1)} copy-done((bf16[256,1024]{1,0:T(8,128)(2,1)S(1)}, bf16[256,1024]{1,0:T(8,128)(2,1)}, u32[]{:S(2)}) %copy-start.5) | copy-done | bytes 524312
  1.8 1.0 %copy-done.6 = bf16[1024,256]{1,0:T(8,128)(2,1)S(1)} copy-done((bf16[1024,256]{1,0:T(8,128)(2,1)S(1)}, bf16[1024,256]{1,0:T(8,128)(2,1)}, u32[]{:S(2)}) %copy-start.6) | copy-done | bytes 524312
  2.8 1.0 %copy-done.7 = bf16[3,192,256]{2,1,0:T(8,128)(2,1)S(1)} copy-done((bf16[3,192,256]{2,1,0:T(8,128)(2,1)S(1)}, bf16[3,192,256]{2,1,0:T(8,128)(2,1)}, u32[]{:S(2)}) %copy-start.7) | copy-done | bytes 294936
  3.8 0.7 %spectra.1 = (f32[192,128]{1,0:T(8,128)S(1)}, f32[192,128]{1,0:T(8,128)S(1)}, f32[192,128]{1,0:T(8,128)S(1)}) custom-call(bf16[256,1024]{1,0:T(8,128)(2,1)S(1)} %copy-done.5, bf16[1024,256]{1,0:T(8,128)(2,1)S(1)} %copy-done.6, bf16[3,192,256]{2,1,0:T(8,128)(2,1)S(1)} %copy-done.7), custom_call_target="tpu_custom_call" | custom-call | tf_op jit(solution)/shard_map/spectra/pallas_call | solution.py:328
  4.5 0.0 copy-start.1
  4.5 0.0 copy-start.2
  4.5 0.0 copy-start.3
  4.5 0.0 copy-start.4
  4.5 2.4 %collective-permute-start.1 = (f32[192,128]{1,0:T(8,128)S(1)}, f32[192,128]{1,0:T(8,128)S(1)}, u32[]{:S(2)}, u32[]{:S(2)}) collective-permute-start(f32[192,128]{1,0:T(8,128)S(1)} %get-tuple-element.18), channel_id=1, source_target_pairs={{0,3},{1,2},{2,1},{3,0},{4,7},{5,6},{6,5},{7,4},{8,11},{9,10},{10,... | collective-permute-start | bytes 294920 | tf_op jit(solution)/shard_map/ppermute | solution.py:319
  6.9 0.7 %collective-permute-start.2 = (f32[192,128]{1,0:T(8,128)S(1)}, f32[192,128]{1,0:T(8,128)S(1)}, u32[]{:S(2)}, u32[]{:S(2)}) collective-permute-start(f32[192,128]{1,0:T(8,128)S(1)} %get-tuple-element.18), channel_id=1, source_target_pairs={{0,1},{1,0},{2,5},{3,4},{4,3},{5,2},{6,9},{7,8},{8,7},{9,6},{10,13... | collective-permute-start | bytes 294920 | tf_op jit(solution)/shard_map/ppermute | solution.py:318
  7.6 0.8 %copy-done.12 = f32[2,16,512]{2,1,0:T(8,128)S(1)} copy-done((f32[2,16,512]{2,1,0:T(8,128)S(1)}, f32[2,16,512]{2,1,0:T(8,128)}, u32[]{:S(2)}) %copy-start.12) | copy-done | bytes 65560
  8.5 0.5 %pack.1 = (f32[32,256]{1,0:T(8,128)S(1)}, f32[32,256]{1,0:T(8,128)S(1)}, f32[32,256]{1,0:T(8,128)S(1)}, f32[8,512]{1,0:T(8,128)S(1)}) custom-call(s32[1,512]{1,0:T(1,128)S(1)} %bitcast.8, f32[32,512]{1,0:T(8,128)S(1)} %bitcast.7), custom_call_target="tpu_custom_call" | custom-call | tf_op jit(solution)/shard_map/pack/pallas_call | solution.py:328
  9.0 3.2 %collective-permute-done.1.near_ref = f32[192,128]{1,0:T(8,128)S(1)} collective-permute-done((f32[192,128]{1,0:T(8,128)S(1)}, f32[192,128]{1,0:T(8,128)S(1)}, u32[]{:S(2)}, u32[]{:S(2)}) %collective-permute-start.1) | collective-permute-done | bytes 98336 | tf_op jit(solution)/shard_map/ppermute | solution.py:319
  12.3 0.0 copy-start.8
  12.3 0.9 %copy-done.8 = bf16[512,192]{1,0:T(8,128)(2,1)S(1)} copy-done((bf16[512,192]{1,0:T(8,128)(2,1)S(1)}, bf16[512,192]{1,0:T(8,128)(2,1)}, u32[]{:S(2)}) %copy-start.8) | copy-done | bytes 196632
  13.2 0.9 %copy-done.9 = bf16[256,512]{1,0:T(8,128)(2,1)S(1)} copy-done((bf16[256,512]{1,0:T(8,128)(2,1)S(1)}, bf16[256,512]{1,0:T(8,128)(2,1)}, u32[]{:S(2)}) %copy-start.9) | copy-done | bytes 262168
  14.2 2.1 %imaging.1 = (bf16[256,256]{1,0:T(8,128)(2,1)S(1)}, f32[40,256]{1,0:T(8,128)S(1)}, f32[40,256]{1,0:T(8,128)S(1)}) custom-call(f32[1,12]{1,0:T(1,128)S(1)} %bitcast.10, f32[192,128]{1,0:T(8,128)S(1)} %get-tuple-element.16.own_ref, f32[192,128]{1,0:T(8,128)S(1)} %collective-permute-done.core_ref, f32[192,128]{1,0:T(8,128)S(1)} %collective-permute-done.1.near_ref, ...), custom_call_target="tpu_custom_call" | custom-call | tf_op jit(solution)/shard_map/imaging/pallas_call | solution.py:328
  16.3 2.2 %collective-permute-start.4 = (f32[40,256]{1,0:T(8,128)S(1)}, f32[40,256]{1,0:T(8,128)S(1)}, u32[]{:S(2)}, u32[]{:S(2)}) collective-permute-start(f32[40,256]{1,0:T(8,128)S(1)} %get-tuple-element.23), channel_id=1, source_target_pairs={{0,3},{1,2},{2,1},{3,0},{4,7},{5,6},{6,5},{7,4},{8,11},{9,10},{10,... | collective-permute-start | bytes 122888 | tf_op jit(solution)/shard_map/ppermute | solution.py:319
  18.5 0.4 collective-permute-start.5
  18.9 0.1 collective-permute-start.3
  19.0 1.2 %collective-permute-done.4.near_ref = f32[40,256]{1,0:T(8,128)S(1)} collective-permute-done((f32[40,256]{1,0:T(8,128)S(1)}, f32[40,256]{1,0:T(8,128)S(1)}, u32[]{:S(2)}, u32[]{:S(2)}) %collective-permute-start.4) | collective-permute-done | bytes 40992 | tf_op jit(solution)/shard_map/ppermute | solution.py:319
  20.2 0.0 collective-permute-done.5.far_ref
  20.2 0.0 collective-permute-done.3.core_ref
  20.3 0.0 copy-start.14
  20.3 7.2 %resist.1 = (f32[256,1024]{1,0:T(8,128)}, bf16[1024,256]{1,0:T(8,128)(2,1)S(1)}, f32[32,256]{1,0:T(8,128)S(1)}, f32[8,256]{1,0:T(8,128)S(1)}) custom-call(bf16[256,256]{1,0:T(8,128)(2,1)S(1)} %get-tuple-element.21.intensity_ref, f32[40,256]{1,0:T(8,128)S(1)} %collective-permute-done.3.core_ref, f32[40,256]{1,0:T(8,128)S(1)} %collective-permute-done.4.near_ref, ...), custom_call_target="tpu_custom_call" | custom-call | tf_op jit(solution)/shard_map/resist/pallas_call | solution.py:328
  27.5 5.4 %mean_core.1 = f32[8,256]{1,0:T(8,128)S(1)} custom-call(bf16[1024,256]{1,0:T(8,128)(2,1)S(1)} %get-tuple-element.26.table_ref, f32[32,256]{1,0:T(8,128)S(1)} %get-tuple-element.28.coords_ref), custom_call_target="tpu_custom_call" | custom-call | tf_op jit(solution)/shard_map/mean_core/pallas_call | solution.py:328
  32.9 0.5 %collective-permute-start.6 = (f32[8,256]{1,0:T(8,128)S(1)}, f32[8,256]{1,0:T(8,128)S(1)}, u32[]{:S(2)}, u32[]{:S(2)}) collective-permute-start(f32[8,256]{1,0:T(8,128)S(1)} %mean_core.1), channel_id=1, source_target_pairs={{0,1},{1,0},{2,3},{3,2},{4,5},{5,4},{6,7},{7,6},{8,9},{9,8},{10,11... | collective-permute-start | bytes 24584 | tf_op jit(solution)/shard_map/ppermute | solution.py:401
  33.4 2.9 %collective-permute-start.7 = (f32[8,256]{1,0:T(8,128)S(1)}, f32[8,256]{1,0:T(8,128)S(1)}, u32[]{:S(2)}, u32[]{:S(2)}) collective-permute-start(f32[8,256]{1,0:T(8,128)S(1)} %get-tuple-element.29), channel_id=1, source_target_pairs={{0,3},{1,2},{2,1},{3,0},{4,7},{5,6},{6,5},{7,4},{8,11},{9,10},{10,... | collective-permute-start | bytes 24584 | tf_op jit(solution)/shard_map/ppermute | solution.py:399
  36.3 0.1 collective-permute-start.8
  37.0 5.4 %mean_own.1.own_ref = f32[8,256]{1,0:T(8,128)S(1)} custom-call(bf16[1024,256]{1,0:T(8,128)(2,1)S(1)} %get-tuple-element.26.table_ref, f32[32,256]{1,0:T(8,128)S(1)} %get-tuple-element.27.coords_ref), custom_call_target="tpu_custom_call" | custom-call | tf_op jit(solution)/shard_map/mean_own/pallas_call | solution.py:328
  42.4 0.0 collective-permute-done.7.near_ref
  42.5 0.8 %bias.1 = f32[1,512]{1,0:T(1,128)} custom-call(f32[1]{0:T(128)S(6)} %copy.19.threshold_ref, f32[8,512]{1,0:T(8,128)S(1)} %get-tuple-element.25.code_ref, f32[8,256]{1,0:T(8,128)S(1)} %mean_own.1.own_ref, f32[8,256]{1,0:T(8,128)S(1)} %collective-permute-done.6.core_ref, f32[8,256]{1,0:T(8,128)S(1)} %collective-permute-done.7.near_ref, ...), custom_call_target="tpu_custom_call" | custom-call | tf_op jit(solution)/shard_map/bias/pallas_call | solution.py:328
  (25 shorter events, 0.1 us)
Async XLA Ops:
  0.6 11.6 %copy-start = (f32[2,96,12,128]{3,1,2,0:T(8,128)S(1)}, f32[2,96,12,128]{3,1,2,0:T(8,128)}, u32[]{:S(2)}) copy-start(f32[2,96,12,128]{3,1,2,0:T(8,128)} %param.18) | copy-start | bytes 3538948
  0.6 1.1 %copy-start.5 = (bf16[256,1024]{1,0:T(8,128)(2,1)S(1)}, bf16[256,1024]{1,0:T(8,128)(2,1)}, u32[]{:S(2)}) copy-start(bf16[256,1024]{1,0:T(8,128)(2,1)} %mask_ref.1) | copy-start | bytes 1572868
  1.8 1.0 %copy-start.6 = (bf16[1024,256]{1,0:T(8,128)(2,1)S(1)}, bf16[1024,256]{1,0:T(8,128)(2,1)}, u32[]{:S(2)}) copy-start(bf16[1024,256]{1,0:T(8,128)(2,1)} %constant.20.clone.forward_ref) | copy-start | bytes 1572868
  2.8 1.0 %copy-start.7 = (bf16[3,192,256]{2,1,0:T(8,128)(2,1)S(1)}, bf16[3,192,256]{2,1,0:T(8,128)(2,1)}, u32[]{:S(2)}) copy-start(bf16[3,192,256]{2,1,0:T(8,128)(2,1)} %constant.21.clone.rows_ref) | copy-start | bytes 884740
  3.8 3.8 %copy-start.13 = (s32[512]{0:T(512)S(1)}, s32[512]{0:T(512)}, u32[]{:S(2)}) copy-start(s32[512]{0:T(512)} %param.21) | copy-start | bytes 6148
  3.8 8.5 %copy-start.15 = (f32[12]{0:T(128)S(1)}, f32[12]{0:T(128)}, u32[]{:S(2)}) copy-start(f32[12]{0:T(128)} %param.19) | copy-start | bytes 148
  3.8 16.4 %copy-start.10 = (bf16[256,256]{1,0:T(8,128)(2,1)S(1)}, bf16[256,256]{1,0:T(8,128)(2,1)}, u32[]{:S(2)}) copy-start(bf16[256,256]{1,0:T(8,128)(2,1)} %constant.24.clone.inner_ref) | copy-start | bytes 393220
  4.5 15.8 %copy-start.1 = (bf16[256,1024]{1,0:T(8,128)(2,1)S(1)}, bf16[256,1024]{1,0:T(8,128)(2,1)}, u32[]{:S(2)}) copy-start(bf16[256,1024]{1,0:T(8,128)(2,1)} %constant.26.clone.high_ref) | copy-start | bytes 1572868
  4.5 15.8 %copy-start.2 = (bf16[256,1024]{1,0:T(8,128)(2,1)S(1)}, bf16[256,1024]{1,0:T(8,128)(2,1)}, u32[]{:S(2)}) copy-start(bf16[256,1024]{1,0:T(8,128)(2,1)} %constant.27.clone.low_ref) | copy-start | bytes 1572868
  4.5 15.8 %copy-start.3 = (bf16[1024,256]{1,0:T(8,128)(2,1)S(1)}, bf16[1024,256]{1,0:T(8,128)(2,1)}, u32[]{:S(2)}) copy-start(bf16[1024,256]{1,0:T(8,128)(2,1)} %constant.28.clone.high_t_ref) | copy-start | bytes 1572868
  4.5 15.8 %copy-start.4 = (bf16[1024,256]{1,0:T(8,128)(2,1)S(1)}, bf16[1024,256]{1,0:T(8,128)(2,1)}, u32[]{:S(2)}) copy-start(bf16[1024,256]{1,0:T(8,128)(2,1)} %constant.29.clone.low_t_ref) | copy-start | bytes 1572868
  4.5 7.7 %collective-permute-start.1 = (f32[192,128]{1,0:T(8,128)S(1)}, f32[192,128]{1,0:T(8,128)S(1)}, u32[]{:S(2)}, u32[]{:S(2)}) collective-permute-start(f32[192,128]{1,0:T(8,128)S(1)} %get-tuple-element.18), channel_id=1, source_target_pairs={{0,3},{1,2},{2,1},{3,0},{4,7},{5,6},{6,5},{7,4},{8,11},{9,10},{10,... | collective-permute-start | bytes 294920 | tf_op jit(solution)/shard_map/ppermute | solution.py:319
  6.9 5.3 %collective-permute-start.2 = (f32[192,128]{1,0:T(8,128)S(1)}, f32[192,128]{1,0:T(8,128)S(1)}, u32[]{:S(2)}, u32[]{:S(2)}) collective-permute-start(f32[192,128]{1,0:T(8,128)S(1)} %get-tuple-element.18), channel_id=1, source_target_pairs={{0,1},{1,0},{2,5},{3,4},{4,3},{5,2},{6,9},{7,8},{8,7},{9,6},{10,13... | collective-permute-start | bytes 294920 | tf_op jit(solution)/shard_map/ppermute | solution.py:318
  7.6 4.6 %collective-permute-start = (f32[192,128]{1,0:T(8,128)S(1)}, f32[192,128]{1,0:T(8,128)S(1)}, u32[]{:S(2)}, u32[]{:S(2)}) collective-permute-start(f32[192,128]{1,0:T(8,128)S(1)} %get-tuple-element.17), channel_id=1, source_target_pairs={{0,1},{1,0},{2,3},{3,2},{4,5},{5,4},{6,7},{7,6},{8,9},{9,8},{10,11... | collective-permute-start | bytes 294920 | tf_op jit(solution)/shard_map/ppermute | solution.py:320
  7.6 0.8 %copy-start.12 = (f32[2,16,512]{2,1,0:T(8,128)S(1)}, f32[2,16,512]{2,1,0:T(8,128)}, u32[]{:S(2)}) copy-start(f32[2,16,512]{2,1,0:T(8,128)} %param.22) | copy-start | bytes 196612
  12.3 1.0 %copy-start.8 = (bf16[512,192]{1,0:T(8,128)(2,1)S(1)}, bf16[512,192]{1,0:T(8,128)(2,1)}, u32[]{:S(2)}) copy-start(bf16[512,192]{1,0:T(8,128)(2,1)} %constant.22.clone.inverse_ref) | copy-start | bytes 589828
  13.2 0.9 %copy-start.9 = (bf16[256,512]{1,0:T(8,128)(2,1)S(1)}, bf16[256,512]{1,0:T(8,128)(2,1)}, u32[]{:S(2)}) copy-start(bf16[256,512]{1,0:T(8,128)(2,1)} %constant.23.clone.spread_ref) | copy-start | bytes 786436
  14.2 6.1 %copy-start.11 = (bf16[256,16]{1,0:T(8,128)(2,1)S(1)}, bf16[256,16]{1,0:T(8,128)(2,1)}, u32[]{:S(2)}) copy-start(bf16[256,16]{1,0:T(8,128)(2,1)} %constant.25.clone.outer_ref) | copy-start | bytes 24580
  16.3 3.9 %collective-permute-start.4 = (f32[40,256]{1,0:T(8,128)S(1)}, f32[40,256]{1,0:T(8,128)S(1)}, u32[]{:S(2)}, u32[]{:S(2)}) collective-permute-start(f32[40,256]{1,0:T(8,128)S(1)} %get-tuple-element.23), channel_id=1, source_target_pairs={{0,3},{1,2},{2,1},{3,0},{4,7},{5,6},{6,5},{7,4},{8,11},{9,10},{10,... | collective-permute-start | bytes 122888 | tf_op jit(solution)/shard_map/ppermute | solution.py:319
  18.5 1.7 %collective-permute-start.5 = (f32[40,256]{1,0:T(8,128)S(1)}, f32[40,256]{1,0:T(8,128)S(1)}, u32[]{:S(2)}, u32[]{:S(2)}) collective-permute-start(f32[40,256]{1,0:T(8,128)S(1)} %get-tuple-element.23), channel_id=1, source_target_pairs={{0,1},{1,0},{2,5},{3,4},{4,3},{5,2},{6,9},{7,8},{8,7},{9,6},{10,13... | collective-permute-start | bytes 122888 | tf_op jit(solution)/shard_map/ppermute | solution.py:318
  18.9 1.3 %collective-permute-start.3 = (f32[40,256]{1,0:T(8,128)S(1)}, f32[40,256]{1,0:T(8,128)S(1)}, u32[]{:S(2)}, u32[]{:S(2)}) collective-permute-start(f32[40,256]{1,0:T(8,128)S(1)} %get-tuple-element.22), channel_id=1, source_target_pairs={{0,1},{1,0},{2,3},{3,2},{4,5},{5,4},{6,7},{7,6},{8,9},{9,8},{10,11... | collective-permute-start | bytes 122888 | tf_op jit(solution)/shard_map/ppermute | solution.py:320
  20.3 22.2 %copy-start.14 = (s32[512]{0:T(512)S(1)}, s32[512]{0:T(512)}, u32[]{:S(2)}) copy-start(s32[512]{0:T(512)} %param.23) | copy-start | bytes 6148
  32.9 9.5 %collective-permute-start.6 = (f32[8,256]{1,0:T(8,128)S(1)}, f32[8,256]{1,0:T(8,128)S(1)}, u32[]{:S(2)}, u32[]{:S(2)}) collective-permute-start(f32[8,256]{1,0:T(8,128)S(1)} %mean_core.1), channel_id=1, source_target_pairs={{0,1},{1,0},{2,3},{3,2},{4,5},{5,4},{6,7},{7,6},{8,9},{9,8},{10,11... | collective-permute-start | bytes 24584 | tf_op jit(solution)/shard_map/ppermute | solution.py:401
  33.4 9.1 %collective-permute-start.7 = (f32[8,256]{1,0:T(8,128)S(1)}, f32[8,256]{1,0:T(8,128)S(1)}, u32[]{:S(2)}, u32[]{:S(2)}) collective-permute-start(f32[8,256]{1,0:T(8,128)S(1)} %get-tuple-element.29), channel_id=1, source_target_pairs={{0,3},{1,2},{2,1},{3,0},{4,7},{5,6},{6,5},{7,4},{8,11},{9,10},{10,... | collective-permute-start | bytes 24584 | tf_op jit(solution)/shard_map/ppermute | solution.py:399
  36.3 6.2 %collective-permute-start.8 = (f32[8,256]{1,0:T(8,128)S(1)}, f32[8,256]{1,0:T(8,128)S(1)}, u32[]{:S(2)}, u32[]{:S(2)}) collective-permute-start(f32[8,256]{1,0:T(8,128)S(1)} %get-tuple-element.29), channel_id=1, source_target_pairs={{0,1},{1,0},{2,5},{3,4},{4,3},{5,2},{6,9},{7,8},{8,7},{9,6},{10,13... | collective-permute-start | bytes 24584 | tf_op jit(solution)/shard_map/ppermute | solution.py:398

commit v2 on v1

v2 whole, which is shorter than its diff:
```python
import math

import jax
import jax.numpy as jnp
import ml_dtypes
import numpy as np
from jax import lax
from jax.experimental import pallas as pl
from jax.experimental.pallas import tpu as pltpu
from jax.sharding import PartitionSpec as P

HALO = 256
BLUR_REACH = 8
SITES = 16

blur_sigma = 3.0
bias_step = 0.5
bias_gain = 2.0

F32 = jnp.float32
BF16 = jnp.bfloat16
BLOCK = 64
VMEM_BYTES = 48 * 1024 * 1024


def rounded(table):
    return np.asarray(table, np.float32).astype(ml_dtypes.bfloat16)


def halves(table):
    high = rounded(table)
    low = rounded(np.asarray(table, np.float64) - high.astype(np.float64))
    return high, low


def twiddle(position, frequency, period, amplitude):
    phase_index = (position[:, None] * frequency[None, :]) % period
    phase_angle = phase_index * (2.0 * math.pi / period)
    return np.cos(phase_angle) * amplitude, np.sin(phase_angle) * amplitude


def centered(count):
    return np.arange(count) - count // 2


def imaging_tables(tile_rows, tile_cols, row_freqs, col_freqs):
    window_rows = tile_rows + 2 * HALO
    col_cos, col_sin = twiddle(
        np.arange(tile_cols), centered(col_freqs), tile_cols, 1.0 / math.sqrt(tile_cols)
    )
    col_forward = rounded(np.concatenate([col_cos, -col_sin], axis=1))
    row_cos, row_sin = twiddle(
        centered(row_freqs), np.arange(window_rows), window_rows, 1.0 / math.sqrt(window_rows)
    )
    row_forward = rounded(np.concatenate([row_cos, -row_sin], axis=0))
    row_blocks = np.stack(
        [row_forward[:, i * tile_rows : (i + 1) * tile_rows] for i in range(3)]
    )
    back_cos, back_sin = twiddle(
        np.arange(tile_rows) + HALO, centered(row_freqs), window_rows, 1.0 / math.sqrt(row_freqs)
    )
    row_inverse = rounded(
        np.block([[back_cos, -back_sin], [back_sin, back_cos]])
    )
    samples = 2 * col_freqs
    step = tile_cols // samples
    out_cos, out_sin = twiddle(
        centered(col_freqs), np.arange(samples) * step, tile_cols, 1.0 / math.sqrt(col_freqs)
    )
    col_inverse = rounded(np.block([[out_cos, out_sin], [-out_sin, out_cos]]))
    return col_forward, row_blocks, row_inverse, col_inverse


def blur_weight(offset, reach):
    every = np.arange(-reach, reach + 1).astype(np.float64)
    norm = np.sum(np.exp(-every * every / (2.0 * blur_sigma * blur_sigma)))
    weight = np.exp(-offset.astype(np.float64) ** 2 / (2.0 * blur_sigma * blur_sigma)) / norm
    return np.where(np.abs(offset) <= reach, weight, 0.0)


def blur_tables(tile_rows, tile_cols, col_freqs, reach):
    line = np.arange(tile_cols)
    col_blur = rounded(blur_weight(line[None, :] - line[:, None], reach))
    samples = 2 * col_freqs
    step = tile_cols // samples
    offset = (line[None, :] - step * np.arange(samples)[:, None]).astype(np.float64)
    half = np.where(offset == 0, 1.0, np.sin(math.pi * offset / tile_cols))
    spread = np.where(
        offset == 0,
        (samples - 1) / samples,
        np.sin((samples - 1) * math.pi * offset / tile_cols) / (samples * half),
    )
    spread_blur = spread @ col_blur.astype(np.float64)
    row_diff = (
        np.arange(tile_rows + 2 * reach)[None, :] - reach - np.arange(tile_rows)[:, None]
    )
    row_blur = rounded(blur_weight(row_diff, reach))
    inner = row_blur[:, reach : reach + tile_rows]
    outer = np.concatenate([row_blur[:, :reach], row_blur[:, reach + tile_rows :]], axis=1)
    return halves(spread_blur), np.ascontiguousarray(inner), np.ascontiguousarray(outer)


def parity():
    return lax.rem(lax.axis_index("tx"), 2)


def has_chip_side():
    me = lax.axis_index("tx")
    return jnp.logical_and(me != 0, me != lax.axis_size("tx") - 1)


def across():
    rest = lax.rem(lax.axis_index("tx"), 4)
    return jnp.logical_or(rest == 1, rest == 2)


def from_chip(near_ref, far_ref):
    return jnp.where(across(), near_ref[...], far_ref[...])


def three_parts(values):
    first = values.astype(BF16)
    rest = values - first.astype(F32)
    second = rest.astype(BF16)
    third = (rest - second.astype(F32)).astype(BF16)
    return first, second, third


def transposed_dot(left, right):
    return lax.dot_general(left, right, (((1,), (1,)), ((), ())), preferred_element_type=F32)


def front_kernel(
    eval_hbm, records_hbm, mask_hbm, forward_hbm, rows_hbm,
    own_ref, core_ref, chip_ref, packed_core_ref, packed_chip_ref, packed_own_ref, chosen_ref,
    eval_ref, records_ref, mask_ref, forward_ref, rows_ref, sems,
):
    copies = [
        pltpu.make_async_copy(source, target, sems.at[i])
        for i, (source, target) in enumerate(
            (
                (eval_hbm, eval_ref),
                (records_hbm, records_ref),
                (mask_hbm, mask_ref),
                (forward_hbm, forward_ref),
                (rows_hbm, rows_ref),
            )
        )
    ]
    for copy in copies:
        copy.start()
    me = lax.axis_index("tx")
    odd = parity()
    frags = eval_ref.shape[1]
    capacity = frags // 2
    count = records_ref.shape[0]
    before = lax.broadcasted_iota(jnp.int32, (frags, frags), 0)
    after = lax.broadcasted_iota(jnp.int32, (frags, frags), 1)
    upper = (before <= after).astype(F32).astype(BF16)
    slots = lax.broadcasted_iota(jnp.int32, (capacity, frags), 0).astype(F32).astype(BF16)
    copies[0].wait()
    copies[1].wait()
    member = lax.broadcasted_iota(jnp.int32, (8, frags), 0) == eval_ref[...] - me + 1
    counts = jnp.dot(member.astype(F32).astype(BF16), upper, preferred_element_type=F32)
    code = jnp.where(member, counts - 1.0, -1.0)
    for side in range(3):
        row = jnp.broadcast_to(code[side : side + 1].astype(BF16), (capacity, frags))
        chosen_ref[side] = jnp.where(slots == row, jnp.ones_like(slots), jnp.zeros_like(slots))
    pieces = jnp.concatenate(three_parts(records_ref[...]), axis=0)

    def packed(side, out_ref):
        got = transposed_dot(pieces, chosen_ref[side])
        out_ref[...] = got[:count] + got[count : 2 * count] + got[2 * count :]

    packed(2 - 2 * odd, packed_core_ref)
    packed(2 * odd, packed_chip_ref)
    packed(1, packed_own_ref)

    for copy in copies[2:]:
        copy.wait()
    col_spectra = jnp.dot(mask_ref[...], forward_ref[...], preferred_element_type=F32).astype(BF16)
    freqs, cols = own_ref.shape[0] // 2, own_ref.shape[1]

    def partial(block, out_ref):
        product = jnp.dot(rows_ref[block], col_spectra, preferred_element_type=F32)
        out_ref[:freqs, :] = product[:freqs, :cols] - product[freqs:, cols:]
        out_ref[freqs:, :] = product[:freqs, cols:] + product[freqs:, :cols]

    partial(2 - 2 * odd, chip_ref)
    partial(2 * odd, core_ref)
    partial(1, own_ref)


def load_kernel(after_ref, *refs):
    count = (len(refs) - 1) // 2
    sems = refs[-1]
    copies = [
        pltpu.make_async_copy(refs[i], refs[count + i], sems.at[i]) for i in range(count)
    ]
    for copy in copies:
        copy.start()
    for copy in copies:
        copy.wait()


def summed_intensity(half, rows, kernels, cols, spread, weights_ref):
    total = None
    for k in range(kernels):
        lanes = slice(k * cols, (k + 1) * cols)
        pair = jnp.concatenate([half[:rows, lanes], half[rows:, lanes]], axis=1)
        field = jnp.dot(pair, spread, preferred_element_type=F32)
        real, imag = field[:, : 2 * cols], field[:, 2 * cols :]
        term = weights_ref[0, k] * (real * real + imag * imag)
        total = term if total is None else total + term
    return total


def edge_kernel(
    weights_ref, own_ref, core_ref, near_ref, far_ref, kern_ref, inverse_ref, spread_ref,
    product_ref, edge_core_ref, edge_chip_ref,
):
    freqs, cols = own_ref.shape[0] // 2, own_ref.shape[1]
    rows = inverse_ref.shape[0] // 2
    kernels = kern_ref.shape[1]
    odd = parity()
    chip = jnp.where(has_chip_side(), from_chip(near_ref, far_ref), 0.0)
    spectrum = own_ref[...] + core_ref[...] + chip
    spec_real, spec_imag = spectrum[:freqs], spectrum[freqs:]
    for k in range(kernels):
        kern_real, kern_imag = kern_ref[0, k], kern_ref[1, k]
        lanes = slice(k * cols, (k + 1) * cols)
        product_ref[:freqs, lanes] = (kern_real * spec_real - kern_imag * spec_imag).astype(BF16)
        product_ref[freqs:, lanes] = (kern_real * spec_imag + kern_imag * spec_real).astype(BF16)
    reach = BLUR_REACH
    lines = jnp.concatenate(
        [
            inverse_ref[:reach], inverse_ref[rows - reach : rows],
            inverse_ref[rows : rows + reach], inverse_ref[2 * rows - reach :],
        ],
        axis=0,
    )
    half = jnp.dot(lines, product_ref[...], preferred_element_type=F32).astype(BF16)
    total = summed_intensity(half, 2 * reach, kernels, cols, spread_ref[...], weights_ref)
    values = total.astype(BF16).astype(F32)
    top, bottom = values[:reach], values[reach:]
    edge_core_ref[...] = jnp.where(odd == 1, top, bottom)
    edge_chip_ref[...] = jnp.where(odd == 1, bottom, top)


def imaging_kernel(weights_ref, product_ref, inverse_ref, spread_ref, intensity_ref, half_ref):
    rows, samples = intensity_ref.shape
    cols = samples // 2
    kernels = product_ref.shape[1] // cols
    half_ref[...] = jnp.dot(
        inverse_ref[...], product_ref[...], preferred_element_type=F32
    ).astype(BF16)
    total = summed_intensity(half_ref, rows, kernels, cols, spread_ref[...], weights_ref)
    intensity_ref[...] = total.astype(BF16)


def site_means(table, coords):
    tile_rows, tile_cols = table.shape
    slots = coords.shape[1]
    width = 256
    low_line = lax.broadcasted_iota(jnp.int32, (width, slots), 0).astype(F32).astype(BF16)
    none = jnp.zeros((width, slots), BF16)
    eight = lax.broadcasted_iota(jnp.int32, (8, slots), 0).astype(F32)
    groups = BLOCK // 8
    blocks = tile_rows // BLOCK
    total = jnp.zeros((8, slots), F32)
    for site in range(SITES):
        col_pos = coords[SITES + site : SITES + site + 1] * (tile_cols - 1)
        low = jnp.minimum(jnp.floor(col_pos), tile_cols - 2.0)
        part = col_pos - low
        low_weight = jnp.broadcast_to((1.0 - part).astype(BF16), (width, slots))
        high_weight = jnp.broadcast_to(part.astype(BF16), (width, slots))
        tents = []
        for start in range(0, tile_cols, width):
            hits = []
            for index in (low - start, low + (1.0 - start)):
                inside = jnp.logical_and(index >= 0.0, index < width)
                index = jnp.where(inside, index, -1.0).astype(BF16)
                hits.append(low_line == jnp.broadcast_to(index, (width, slots)))
            tents.append(jnp.where(hits[0], low_weight, jnp.where(hits[1], high_weight, none)))
        picked = jnp.dot(table, jnp.concatenate(tents, axis=0), preferred_element_type=F32)
        row_pos = coords[site : site + 1] * (tile_rows - 1)
        block = jnp.minimum(jnp.floor(row_pos * (1.0 / BLOCK)), blocks - 1.0)
        within = jnp.broadcast_to(row_pos - block * BLOCK, (8, slots))
        block = jnp.broadcast_to(block, (8, slots))
        held = [jnp.zeros((8, slots), F32) for _ in range(groups + 1)]
        for b in range(blocks):
            hit = block == float(b)
            for g in range(groups + 1 if b < blocks - 1 else groups):
                first = b * BLOCK + 8 * g
                held[g] = jnp.where(hit, picked[first : first + 8], held[g])
        for g in range(groups + 1):
            weight = jnp.maximum(1.0 - jnp.abs(within - (eight + 8.0 * g)), 0.0)
            total = total + held[g] * weight
    return jnp.broadcast_to(jnp.sum(total, axis=0, keepdims=True) * (1.0 / SITES), (8, slots))


def resist_kernel(
    intensity_ref, core_ref, near_ref, far_ref, inner_ref, outer_ref, high_ref, low_ref,
    coords_near_ref, coords_far_ref,
    resist_ref, table_ref, mean_chip_ref,
):
    odd = parity()
    chip_edge = jnp.where(has_chip_side(), from_chip(near_ref, far_ref), 0.0)
    core_edge = core_ref[...]
    above = jnp.where(odd == 1, core_edge, chip_edge)
    below = jnp.where(odd == 1, chip_edge, core_edge)
    edges = jnp.concatenate([above, below], axis=0).astype(BF16)
    blurred = jnp.dot(inner_ref[...], intensity_ref[...], preferred_element_type=F32)
    blurred += jnp.dot(outer_ref[...], edges, preferred_element_type=F32)
    high = blurred.astype(BF16)
    low = (blurred - high.astype(F32)).astype(BF16)
    resist = (
        jnp.dot(high, high_ref[...], preferred_element_type=F32)
        + jnp.dot(low, high_ref[...], preferred_element_type=F32)
        + jnp.dot(high, low_ref[...], preferred_element_type=F32)
    )
    resist_ref[...] = resist
    table_ref[...] = resist.astype(BF16)
    mean_chip_ref[...] = site_means(table_ref[...], from_chip(coords_near_ref, coords_far_ref))


def mean_kernel(table_ref, coords_ref, mean_ref):
    mean_ref[...] = site_means(table_ref[...], coords_ref[...])


def bias_kernel(threshold_ref, chosen_ref, own_ref, core_ref, near_ref, far_ref, steps_ref, out_ref):
    frags = steps_ref.shape[1]
    odd = parity()
    lanes = lax.broadcasted_iota(jnp.int32, own_ref.shape, 0)
    total = jnp.zeros((8, frags), F32)
    for side, mean in (
        (1, own_ref[...]), (2 - 2 * odd, core_ref[...]), (2 * odd, from_chip(near_ref, far_ref))
    ):
        first, second, third = (part.astype(F32) for part in three_parts(mean))
        parts = jnp.where(
            lanes == 0, first, jnp.where(lanes == 1, second, jnp.where(lanes == 2, third, 0.0))
        ).astype(BF16)
        total = total + jnp.dot(parts, chosen_ref[side], preferred_element_type=F32)
    site_mean = jnp.sum(total, axis=0, keepdims=True)
    out_ref[...] = bias_step * steps_ref[...].astype(F32) - bias_gain * (
        site_mean - threshold_ref[0]
    )


def swaps(count):
    def whole(pairs):
        partner = {}
        for a, b in pairs:
            partner[a], partner[b] = b, a
        return [(i, partner[i]) for i in range(count)]

    quads = count // 4
    core = [(i, i + 1) for i in range(0, count, 2)]
    near = [(i + 1, i + 2) for i in range(0, count, 4)]
    for quad in range(0, quads - 1, 2):
        near += [(4 * quad + i, 4 * quad + 4 + i) for i in (0, 3)]
    if quads % 2:
        near.append((count - 4, count - 1))
    far = [(0, 1), (count - 2, count - 1)] + [(i + 3, i + 4) for i in range(0, count - 4, 4)]
    far += [(i + 2, i + 5) for i in range(0, count - 4, 4)]
    return whole(core), whole(near), whole(far)


def exchange_chip(to_chip):
    _, near, far = swaps(lax.axis_size("tx"))
    return lax.ppermute(to_chip, "tx", near), lax.ppermute(to_chip, "tx", far)


def exchange_core(to_core):
    return lax.ppermute(to_core, "tx", swaps(lax.axis_size("tx"))[0])


def call(kernel, outs, args, smem=(), hbm=(), scratch=(), name=None):
    specs = [
        pl.BlockSpec(
            memory_space=pltpu.SMEM if i in smem else pltpu.HBM if i in hbm else pltpu.VMEM
        )
        for i in range(len(args))
    ]
    args = [
        pltpu.with_memory_space_constraint(arg, pltpu.HBM) if i in hbm else arg
        for i, arg in enumerate(args)
    ]
    return pl.pallas_call(
        kernel,
        out_shape=[jax.ShapeDtypeStruct(s, d) for s, d in outs],
        in_specs=specs,
        out_specs=[pl.BlockSpec(memory_space=pltpu.VMEM) for _ in outs],
        scratch_shapes=list(scratch),
        compiler_params=pltpu.CompilerParams(vmem_limit_bytes=VMEM_BYTES),
        name=name,
    )(*args)


def shards(mask, kernel_spectra, kernel_weights, threshold, eval_tile, site_coords, bias_steps):
    tile_rows, tile_cols = mask.shape
    _, row_freqs, kernels, col_freqs = kernel_spectra.shape
    frags = eval_tile.shape[0]
    capacity = frags // 2
    samples = 2 * col_freqs
    flat = kernels * col_freqs
    records = 2 * SITES
    col_forward, row_blocks, row_inverse, col_inverse = imaging_tables(
        tile_rows, tile_cols, row_freqs, col_freqs
    )
    (high, low), inner, outer = blur_tables(tile_rows, tile_cols, col_freqs, BLUR_REACH)
    spectrum = ((2 * row_freqs, col_freqs), F32)
    packed = ((records, capacity), F32)
    edge = ((BLUR_REACH, samples), F32)
    means = ((8, capacity), F32)
    weights = kernel_weights.reshape(1, kernels)

    own, to_core, to_chip, packed_core, packed_chip, packed_own, chosen = call(
        front_kernel,
        [spectrum] * 3 + [packed] * 3 + [((3, capacity, frags), BF16)],
        (
            eval_tile.reshape(1, frags), site_coords.reshape(records, frags),
            mask, col_forward, row_blocks,
        ),
        hbm=range(5),
        scratch=[
            pltpu.VMEM((1, frags), jnp.int32),
            pltpu.VMEM((records, frags), F32),
            pltpu.VMEM(mask.shape, BF16),
            pltpu.VMEM(col_forward.shape, BF16),
            pltpu.VMEM(row_blocks.shape, BF16),
            pltpu.SemaphoreType.DMA((5,)),
        ],
        name="front",
    )
    got_near, got_far = exchange_chip(to_chip)
    got_core = exchange_core(to_core)
    coords_near, coords_far = exchange_chip(packed_chip)
    coords_core = exchange_core(packed_core)
    inverse, spread = call(
        load_kernel,
        [(row_inverse.shape, BF16), (col_inverse.shape, BF16)],
        (own, row_inverse, col_inverse),
        hbm=(1, 2),
        scratch=[pltpu.SemaphoreType.DMA((2,))],
        name="load",
    )
    product, edge_core, edge_chip = call(
        edge_kernel,
        [((2 * row_freqs, flat), BF16), edge, edge],
        (
            weights, own, got_core, got_near, got_far,
            jnp.transpose(kernel_spectra, (0, 2, 1, 3)), inverse, spread,
        ),
        smem=(0,),
        name="edges",
    )
    edge_near, edge_far = exchange_chip(edge_chip)
    edge_core = exchange_core(edge_core)
    (intensity,) = call(
        imaging_kernel,
        [((tile_rows, samples), BF16)],
        (weights, product, inverse, spread),
        smem=(0,),
        scratch=[pltpu.VMEM((2 * tile_rows, flat), BF16)],
        name="imaging",
    )
    resist, table, mean_chip = call(
        resist_kernel,
        [((tile_rows, tile_cols), F32), ((tile_rows, tile_cols), BF16), means],
        (
            intensity, edge_core, edge_near, edge_far, inner, outer, high, low,
            coords_near, coords_far,
        ),
        name="resist",
    )
    back_near, back_far = exchange_chip(mean_chip)
    (mean_core,) = call(mean_kernel, [means], (table, coords_core), name="mean_core")
    back_core = exchange_core(mean_core)
    (mean_own,) = call(mean_kernel, [means], (table, packed_own), name="mean_own")
    (new_bias,) = call(
        bias_kernel,
        [((1, frags), F32)],
        (
            threshold, chosen, mean_own, back_core, back_near, back_far,
            bias_steps.reshape(1, frags),
        ),
        smem=(0,),
        name="bias",
    )
    return resist, new_bias.reshape(frags)


def solution(mesh):
    placed = (
        P(("groups", "tx"), None),
        P(),
        P(),
        P(),
        P(("groups", "tx")),
        P(None, None, ("groups", "tx")),
        P(("groups", "tx")),
    )
    return jax.shard_map(
        shards,
        mesh=mesh,
        in_specs=placed,
        out_specs=(P(("groups", "tx"), None), P(("groups", "tx"))),
        check_vma=False,
    )
```

time: 43.9 us -> 29.9 us (0.68); the launches traced: 43.3 us -> 29.8 us
  Pallas kernels: 22.2 us -> 15.6 us
  local copies, waits for them, and re-layouts: 5.92 us -> 0.04 us
  waiting for transfers between devices: 4.42 us -> 0.03 us
  starting transfers between devices: 9.31 us -> 12.5 us
    pallas_call x7 -> x8, Pallas kernels: 22.2 us -> 15.6 us  [call(): pl.pallas_call(kernel, out_shape=[jax.ShapeDtypeStruct(s, d) for s, d in...]
    unnamed x32 -> x14, local copies, waits for them, and re-layouts: 5.92 us -> 0.04 us
    ppermute x9 -> x12, waiting for transfers between devices: 4.42 us -> 0.03 us  [the longest x8 0.02 us: exchange_chip(): return (lax.ppermute(to_chip, 'tx', near), lax.ppermute(to_chip, 'tx', far))]
    ppermute x9 -> x12, starting transfers between devices: 9.31 us -> 12.5 us  [the longest x8 11.5 us: exchange_chip(): return (lax.ppermute(to_chip, 'tx', near), lax.ppermute(to_chip, 'tx', far))]
  transfers between devices with their start and end apart: 9 -> 12, of which waited for: 2 -> 0; matrix products, arithmetic and copies ran while one was open for 0% -> 0% of each run, Pallas kernels for 14% -> 34%
where the time goes in v2:
time: 29.9 us; the launch traced here: 29.8 us
  Pallas kernels  15.6 us (52%)
  starting transfers between devices  12.5 us (42%)
  between operations  1.52 us (5%)
    pallas_call x8, Pallas kernels, call(): pl.pallas_call(kernel, out_shape=[jax.ShapeDtypeStruct(s, d) for s, d in...  15.6 us
    ppermute x8, starting transfers between devices, exchange_chip(): return (lax.ppermute(to_chip, 'tx', near), lax.ppermute(to_chip, 'tx', far))  11.5 us
    ppermute x4, starting transfers between devices, exchange_core(): return lax.ppermute(to_core, 'tx', swaps(lax.axis_size('tx'))[0])  1.07 us
  transfers between devices with their start and end apart: 12, of which 0 were waited for; matrix products, arithmetic and copies ran while one was open for 0% of the time, Pallas kernels for 34%

profile of v2, /device:TPU:0, one launch (start us, length us, event | category | flops | bytes accessed | tf_op | source)
XLA Modules:
  0.0 29.8 jit_solution(17825713066444967851)
XLA Ops:
  0.7 2.4 %front.1 = (f32[192,128]{1,0:T(8,128)S(1)}, f32[192,128]{1,0:T(8,128)S(1)}, f32[192,128]{1,0:T(8,128)S(1)}, f32[32,256]{1,0:T(8,128)S(1)}, f32[32,256]{1,0:T(8,1...) custom-call(s32[1,512]{1,0:T(1,128)} %bitcast.11, f32[32,512]{1,0:T(8,128)} %bitcast.10, ...), custom_call_target="tpu_custom_call" | custom-call | tf_op jit(solution)/shard_map/front/pallas_call | solution.py:389
  3.0 3.1 %collective-permute-start.1 = (f32[192,128]{1,0:T(8,128)S(1)}, f32[192,128]{1,0:T(8,128)S(1)}, u32[]{:S(2)}, u32[]{:S(2)}) collective-permute-start(f32[192,128]{1,0:T(8,128)S(1)} %get-tuple-element.19), channel_id=1, source_target_pairs={{0,4},{1,2},{2,1},{3,7},{4,0},{5,6},{6,5},{7,3},{8,12},{9,10},{10,... | collective-permute-start | bytes 294920 | tf_op jit(solution)/shard_map/ppermute | solution.py:371
  6.1 0.0 collective-permute-start.2
  6.1 0.5 %collective-permute-start = (f32[192,128]{1,0:T(8,128)S(1)}, f32[192,128]{1,0:T(8,128)S(1)}, u32[]{:S(2)}, u32[]{:S(2)}) collective-permute-start(f32[192,128]{1,0:T(8,128)S(1)} %get-tuple-element.18), channel_id=1, source_target_pairs={{0,1},{1,0},{2,3},{3,2},{4,5},{5,4},{6,7},{7,6},{8,9},{9,8},{10,11... | collective-permute-start | bytes 294920 | tf_op jit(solution)/shard_map/ppermute | solution.py:375
  6.6 1.6 %collective-permute-start.6 = (f32[32,256]{1,0:T(8,128)S(1)}, f32[32,256]{1,0:T(8,128)S(1)}, u32[]{:S(2)}, u32[]{:S(2)}) collective-permute-start(f32[32,256]{1,0:T(8,128)S(1)} %get-tuple-element.25), channel_id=1, source_target_pairs={{0,4},{1,2},{2,1},{3,7},{4,0},{5,6},{6,5},{7,3},{8,12},{9,10},{10,... | collective-permute-start | bytes 98312 | tf_op jit(solution)/shard_map/ppermute | solution.py:371
  8.2 0.7 %collective-permute-start.7 = (f32[32,256]{1,0:T(8,128)S(1)}, f32[32,256]{1,0:T(8,128)S(1)}, u32[]{:S(2)}, u32[]{:S(2)}) collective-permute-start(f32[32,256]{1,0:T(8,128)S(1)} %get-tuple-element.25), channel_id=1, source_target_pairs={{0,1},{1,0},{2,5},{3,4},{4,3},{5,2},{6,9},{7,8},{8,7},{9,6},{10,13... | collective-permute-start | bytes 98312 | tf_op jit(solution)/shard_map/ppermute | solution.py:371
  8.9 0.0 collective-permute-done.1.near_ref
  8.9 0.0 collective-permute-start.8
  8.9 1.0 %load.1 = (bf16[512,192]{1,0:T(8,128)(2,1)S(1)}, bf16[256,512]{1,0:T(8,128)(2,1)S(1)}) custom-call(f32[192,128]{1,0:T(8,128)S(1)} %get-tuple-element.17.after_ref.own_ref, bf16[512,192]{1,0:T(8,128)(2,1)} %constant.18.clone.refs_0_, bf16[256,512]{1,0:T(8,128)(2,1)} %constant.19.clone.refs_1_), custom_call_target="tpu_custom_call" | custom-call | tf_op jit(solution)/shard_map/load/pallas_call | solution.py:389
  10.0 0.0 collective-permute-done.core_ref
  10.0 0.0 copy-start.1
  10.0 0.0 copy-start.2
  10.0 0.0 copy-start.3
  10.0 0.0 copy-start.4
  10.0 1.4 %edges.1 = (bf16[192,1536]{1,0:T(8,128)(2,1)S(1)}, f32[8,256]{1,0:T(8,128)S(1)}, f32[8,256]{1,0:T(8,128)S(1)}) custom-call(f32[1,12]{1,0:T(1,128)S(1)} %bitcast.8, f32[192,128]{1,0:T(8,128)S(1)} %get-tuple-element.17.after_ref.own_ref, f32[192,128]{1,0:T(8,128)S(1)} %collective-permute-done.core_ref, f32[192,128]{1,0:T(8,128)S(1)} %collective-permute-done.1.near_ref, ...), custom_call_target="tpu_custom_call" | custom-call | tf_op jit(solution)/shard_map/edges/pallas_call | solution.py:389
  11.4 2.8 %collective-permute-start.4 = (f32[8,256]{1,0:T(8,128)S(1)}, f32[8,256]{1,0:T(8,128)S(1)}, u32[]{:S(2)}, u32[]{:S(2)}) collective-permute-start(f32[8,256]{1,0:T(8,128)S(1)} %get-tuple-element.24), channel_id=1, source_target_pairs={{0,4},{1,2},{2,1},{3,7},{4,0},{5,6},{6,5},{7,3},{8,12},{9,10},{10,... | collective-permute-start | bytes 24584 | tf_op jit(solution)/shard_map/ppermute | solution.py:371
  14.2 0.5 %collective-permute-start.5 = (f32[8,256]{1,0:T(8,128)S(1)}, f32[8,256]{1,0:T(8,128)S(1)}, u32[]{:S(2)}, u32[]{:S(2)}) collective-permute-start(f32[8,256]{1,0:T(8,128)S(1)} %get-tuple-element.24), channel_id=1, source_target_pairs={{0,1},{1,0},{2,5},{3,4},{4,3},{5,2},{6,9},{7,8},{8,7},{9,6},{10,13... | collective-permute-start | bytes 24584 | tf_op jit(solution)/shard_map/ppermute | solution.py:371
  14.7 0.0 collective-permute-start.3
  14.8 1.9 %imaging.1.intensity_ref = bf16[256,256]{1,0:T(8,128)(2,1)S(1)} custom-call(f32[1,12]{1,0:T(1,128)S(1)} %bitcast.9, bf16[192,1536]{1,0:T(8,128)(2,1)S(1)} %get-tuple-element.22.product_ref, bf16[512,192]{1,0:T(8,128)(2,1)S(1)} %get-tuple-element.20.inverse_ref, bf16[256,512]{1,0:T(8,128)(2,1)S(1)} %get-tuple-element.21.spread_ref), custom_call_target="tpu_custom_call" | custom-call | tf_op jit(solution)/shard_map/imaging/pallas_call | solution.py:389
  16.7 0.0 copy-start.5
  16.7 0.0 collective-permute-done.7.coords_far_ref
  16.7 0.0 collective-permute-done.5.far_ref
  16.8 0.0 collective-permute-done.3.core_ref
  16.8 3.3 %resist.1 = (f32[256,1024]{1,0:T(8,128)}, bf16[256,1024]{1,0:T(8,128)(2,1)S(1)}, f32[8,256]{1,0:T(8,128)S(1)}) custom-call(bf16[256,256]{1,0:T(8,128)(2,1)S(1)} %imaging.1.intensity_ref, f32[8,256]{1,0:T(8,128)S(1)} %collective-permute-done.3.core_ref, f32[8,256]{1,0:T(8,128)S(1)} %collective-permute-done.4.near_ref, ...), custom_call_target="tpu_custom_call" | custom-call | tf_op jit(solution)/shard_map/resist/pallas_call | solution.py:389
  20.1 0.0 collective-permute-done.8.coords_ref
  20.1 2.4 %mean_core.1 = f32[8,256]{1,0:T(8,128)S(1)} custom-call(bf16[256,1024]{1,0:T(8,128)(2,1)S(1)} %get-tuple-element.28.table_ref, f32[32,256]{1,0:T(8,128)S(1)} %collective-permute-done.8.coords_ref), custom_call_target="tpu_custom_call" | custom-call | tf_op jit(solution)/shard_map/mean_core/pallas_call | solution.py:389
  22.5 0.6 %collective-permute-start.9 = (f32[8,256]{1,0:T(8,128)S(1)}, f32[8,256]{1,0:T(8,128)S(1)}, u32[]{:S(2)}, u32[]{:S(2)}) collective-permute-start(f32[8,256]{1,0:T(8,128)S(1)} %mean_core.1), channel_id=1, source_target_pairs={{0,1},{1,0},{2,3},{3,2},{4,5},{5,4},{6,7},{7,6},{8,9},{9,8},{10,11... | collective-permute-start | bytes 24584 | tf_op jit(solution)/shard_map/ppermute | solution.py:375
  23.1 2.5 %collective-permute-start.10 = (f32[8,256]{1,0:T(8,128)S(1)}, f32[8,256]{1,0:T(8,128)S(1)}, u32[]{:S(2)}, u32[]{:S(2)}) collective-permute-start(f32[8,256]{1,0:T(8,128)S(1)} %get-tuple-element.31), channel_id=1, source_target_pairs={{0,4},{1,2},{2,1},{3,7},{4,0},{5,6},{6,5},{7,3},{8,12},{9,10},{10,... | collective-permute-start | bytes 24584 | tf_op jit(solution)/shard_map/ppermute | solution.py:371
  25.6 0.2 collective-permute-start.11
  26.5 2.4 %mean_own.1.own_ref = f32[8,256]{1,0:T(8,128)S(1)} custom-call(bf16[256,1024]{1,0:T(8,128)(2,1)S(1)} %get-tuple-element.28.table_ref, f32[32,256]{1,0:T(8,128)S(1)} %get-tuple-element.29.coords_ref), custom_call_target="tpu_custom_call" | custom-call | tf_op jit(solution)/shard_map/mean_own/pallas_call | solution.py:389
  28.9 0.0 collective-permute-done.9.core_ref
  29.0 0.8 %bias.1 = f32[1,512]{1,0:T(1,128)} custom-call(f32[1]{0:T(128)S(6)} %copy.17.threshold_ref, bf16[3,256,512]{2,1,0:T(8,128)(2,1)S(1)} %get-tuple-element.27.chosen_ref, f32[8,256]{1,0:T(8,128)S(1)} %mean_own.1.own_ref, f32[8,256]{1,0:T(8,128)S(1)} %collective-permute-done.9.core_ref, f32[8,256]{1,0:T(8,128)S(1)} %collective-permute-done.10.near_ref, ...), custom_call_target="tpu_custom_call" | custom-call | tf_op jit(solution)/shard_map/bias/pallas_call | solution.py:389
  (14 shorter events, 0.0 us)
Async XLA Ops:
  0.6 9.3 %copy-start.6 = (f32[12]{0:T(128)S(1)}, f32[12]{0:T(128)}, u32[]{:S(2)}) copy-start(f32[12]{0:T(128)} %param.17) | copy-start | bytes 148
  0.6 9.3 %copy-start = (f32[2,96,12,128]{3,1,2,0:T(8,128)S(1)}, f32[2,96,12,128]{3,1,2,0:T(8,128)}, u32[]{:S(2)}) copy-start(f32[2,96,12,128]{3,1,2,0:T(8,128)} %param.16) | copy-start | bytes 3538948
  3.0 5.9 %collective-permute-start.1 = (f32[192,128]{1,0:T(8,128)S(1)}, f32[192,128]{1,0:T(8,128)S(1)}, u32[]{:S(2)}, u32[]{:S(2)}) collective-permute-start(f32[192,128]{1,0:T(8,128)S(1)} %get-tuple-element.19), channel_id=1, source_target_pairs={{0,4},{1,2},{2,1},{3,7},{4,0},{5,6},{6,5},{7,3},{8,12},{9,10},{10,... | collective-permute-start | bytes 294920 | tf_op jit(solution)/shard_map/ppermute | solution.py:371
  6.1 3.9 %collective-permute-start.2 = (f32[192,128]{1,0:T(8,128)S(1)}, f32[192,128]{1,0:T(8,128)S(1)}, u32[]{:S(2)}, u32[]{:S(2)}) collective-permute-start(f32[192,128]{1,0:T(8,128)S(1)} %get-tuple-element.19), channel_id=1, source_target_pairs={{0,1},{1,0},{2,5},{3,4},{4,3},{5,2},{6,9},{7,8},{8,7},{9,6},{10,13... | collective-permute-start | bytes 294920 | tf_op jit(solution)/shard_map/ppermute | solution.py:371
  6.1 3.8 %collective-permute-start = (f32[192,128]{1,0:T(8,128)S(1)}, f32[192,128]{1,0:T(8,128)S(1)}, u32[]{:S(2)}, u32[]{:S(2)}) collective-permute-start(f32[192,128]{1,0:T(8,128)S(1)} %get-tuple-element.18), channel_id=1, source_target_pairs={{0,1},{1,0},{2,3},{3,2},{4,5},{5,4},{6,7},{7,6},{8,9},{9,8},{10,11... | collective-permute-start | bytes 294920 | tf_op jit(solution)/shard_map/ppermute | solution.py:375
  6.6 8.1 %collective-permute-start.6 = (f32[32,256]{1,0:T(8,128)S(1)}, f32[32,256]{1,0:T(8,128)S(1)}, u32[]{:S(2)}, u32[]{:S(2)}) collective-permute-start(f32[32,256]{1,0:T(8,128)S(1)} %get-tuple-element.25), channel_id=1, source_target_pairs={{0,4},{1,2},{2,1},{3,7},{4,0},{5,6},{6,5},{7,3},{8,12},{9,10},{10,... | collective-permute-start | bytes 98312 | tf_op jit(solution)/shard_map/ppermute | solution.py:371
  8.2 8.5 %collective-permute-start.7 = (f32[32,256]{1,0:T(8,128)S(1)}, f32[32,256]{1,0:T(8,128)S(1)}, u32[]{:S(2)}, u32[]{:S(2)}) collective-permute-start(f32[32,256]{1,0:T(8,128)S(1)} %get-tuple-element.25), channel_id=1, source_target_pairs={{0,1},{1,0},{2,5},{3,4},{4,3},{5,2},{6,9},{7,8},{8,7},{9,6},{10,13... | collective-permute-start | bytes 98312 | tf_op jit(solution)/shard_map/ppermute | solution.py:371
  8.9 11.2 %collective-permute-start.8 = (f32[32,256]{1,0:T(8,128)S(1)}, f32[32,256]{1,0:T(8,128)S(1)}, u32[]{:S(2)}, u32[]{:S(2)}) collective-permute-start(f32[32,256]{1,0:T(8,128)S(1)} %get-tuple-element.30), channel_id=1, source_target_pairs={{0,1},{1,0},{2,3},{3,2},{4,5},{5,4},{6,7},{7,6},{8,9},{9,8},{10,11... | collective-permute-start | bytes 98312 | tf_op jit(solution)/shard_map/ppermute | solution.py:375
  10.0 6.8 %copy-start.1 = (bf16[256,1024]{1,0:T(8,128)(2,1)S(1)}, bf16[256,1024]{1,0:T(8,128)(2,1)}, u32[]{:S(2)}) copy-start(bf16[256,1024]{1,0:T(8,128)(2,1)} %constant.22.clone.high_ref) | copy-start | bytes 1572868
  10.0 6.8 %copy-start.2 = (bf16[256,1024]{1,0:T(8,128)(2,1)S(1)}, bf16[256,1024]{1,0:T(8,128)(2,1)}, u32[]{:S(2)}) copy-start(bf16[256,1024]{1,0:T(8,128)(2,1)} %constant.23.clone.low_ref) | copy-start | bytes 1572868
  10.0 6.8 %copy-start.3 = (bf16[256,256]{1,0:T(8,128)(2,1)S(1)}, bf16[256,256]{1,0:T(8,128)(2,1)}, u32[]{:S(2)}) copy-start(bf16[256,256]{1,0:T(8,128)(2,1)} %constant.20.clone.inner_ref) | copy-start | bytes 393220
  10.0 6.8 %copy-start.4 = (bf16[256,16]{1,0:T(8,128)(2,1)S(1)}, bf16[256,16]{1,0:T(8,128)(2,1)}, u32[]{:S(2)}) copy-start(bf16[256,16]{1,0:T(8,128)(2,1)} %constant.21.clone.outer_ref) | copy-start | bytes 24580
  11.4 5.3 %collective-permute-start.4 = (f32[8,256]{1,0:T(8,128)S(1)}, f32[8,256]{1,0:T(8,128)S(1)}, u32[]{:S(2)}, u32[]{:S(2)}) collective-permute-start(f32[8,256]{1,0:T(8,128)S(1)} %get-tuple-element.24), channel_id=1, source_target_pairs={{0,4},{1,2},{2,1},{3,7},{4,0},{5,6},{6,5},{7,3},{8,12},{9,10},{10,... | collective-permute-start | bytes 24584 | tf_op jit(solution)/shard_map/ppermute | solution.py:371
  14.2 2.5 %collective-permute-start.5 = (f32[8,256]{1,0:T(8,128)S(1)}, f32[8,256]{1,0:T(8,128)S(1)}, u32[]{:S(2)}, u32[]{:S(2)}) collective-permute-start(f32[8,256]{1,0:T(8,128)S(1)} %get-tuple-element.24), channel_id=1, source_target_pairs={{0,1},{1,0},{2,5},{3,4},{4,3},{5,2},{6,9},{7,8},{8,7},{9,6},{10,13... | collective-permute-start | bytes 24584 | tf_op jit(solution)/shard_map/ppermute | solution.py:371
  14.7 2.0 %collective-permute-start.3 = (f32[8,256]{1,0:T(8,128)S(1)}, f32[8,256]{1,0:T(8,128)S(1)}, u32[]{:S(2)}, u32[]{:S(2)}) collective-permute-start(f32[8,256]{1,0:T(8,128)S(1)} %get-tuple-element.23), channel_id=1, source_target_pairs={{0,1},{1,0},{2,3},{3,2},{4,5},{5,4},{6,7},{7,6},{8,9},{9,8},{10,11... | collective-permute-start | bytes 24584 | tf_op jit(solution)/shard_map/ppermute | solution.py:375
  16.7 12.2 %copy-start.5 = (s32[512]{0:T(512)S(1)}, s32[512]{0:T(512)}, u32[]{:S(2)}) copy-start(s32[512]{0:T(512)} %param.21) | copy-start | bytes 6148
  22.5 6.4 %collective-permute-start.9 = (f32[8,256]{1,0:T(8,128)S(1)}, f32[8,256]{1,0:T(8,128)S(1)}, u32[]{:S(2)}, u32[]{:S(2)}) collective-permute-start(f32[8,256]{1,0:T(8,128)S(1)} %mean_core.1), channel_id=1, source_target_pairs={{0,1},{1,0},{2,3},{3,2},{4,5},{5,4},{6,7},{7,6},{8,9},{9,8},{10,11... | collective-permute-start | bytes 24584 | tf_op jit(solution)/shard_map/ppermute | solution.py:375
  23.1 5.9 %collective-permute-start.10 = (f32[8,256]{1,0:T(8,128)S(1)}, f32[8,256]{1,0:T(8,128)S(1)}, u32[]{:S(2)}, u32[]{:S(2)}) collective-permute-start(f32[8,256]{1,0:T(8,128)S(1)} %get-tuple-element.31), channel_id=1, source_target_pairs={{0,4},{1,2},{2,1},{3,7},{4,0},{5,6},{6,5},{7,3},{8,12},{9,10},{10,... | collective-permute-start | bytes 24584 | tf_op jit(solution)/shard_map/ppermute | solution.py:371
  25.6 3.3 %collective-permute-start.11 = (f32[8,256]{1,0:T(8,128)S(1)}, f32[8,256]{1,0:T(8,128)S(1)}, u32[]{:S(2)}, u32[]{:S(2)}) collective-permute-start(f32[8,256]{1,0:T(8,128)S(1)} %get-tuple-element.31), channel_id=1, source_target_pairs={{0,1},{1,0},{2,5},{3,4},{4,3},{5,2},{6,9},{7,8},{8,7},{9,6},{10,13... | collective-permute-start | bytes 24584 | tf_op jit(solution)/shard_map/ppermute | solution.py:371

commit v3 on v2

--- a/solution.py
+++ b/solution.py
@@ -53,8 +53,8 @@
         centered(row_freqs), np.arange(window_rows), window_rows, 1.0 / math.sqrt(window_rows)
     )
     row_forward = rounded(np.concatenate([row_cos, -row_sin], axis=0))
-    row_blocks = np.stack(
-        [row_forward[:, i * tile_rows : (i + 1) * tile_rows] for i in range(3)]
+    row_blocks = np.concatenate(
+        [row_forward[:, i * tile_rows : (i + 1) * tile_rows] for i in range(3)], axis=0
     )
     back_cos, back_sin = twiddle(
         np.arange(tile_rows) + HALO, centered(row_freqs), window_rows, 1.0 / math.sqrt(row_freqs)
@@ -109,15 +109,6 @@
     return jnp.logical_and(me != 0, me != lax.axis_size("tx") - 1)
 
 
-def across():
-    rest = lax.rem(lax.axis_index("tx"), 4)
-    return jnp.logical_or(rest == 1, rest == 2)
-
-
-def from_chip(near_ref, far_ref):
-    return jnp.where(across(), near_ref[...], far_ref[...])
-
-
 def three_parts(values):
     first = values.astype(BF16)
     rest = values - first.astype(F32)
@@ -131,8 +122,8 @@
 
 
 def front_kernel(
-    eval_hbm, records_hbm, mask_hbm, forward_hbm, rows_hbm,
-    own_ref, core_ref, chip_ref, packed_core_ref, packed_chip_ref, packed_own_ref, chosen_ref,
+    eval_hbm, records_hbm, mask_hbm, forward_hbm, rows_hbm, inverse_hbm, spread_hbm,
+    inverse_ref, spread_ref, own_ref, core_ref, chip_ref, packed_core_ref, packed_chip_ref, packed_own_ref, chosen_ref,
     eval_ref, records_ref, mask_ref, forward_ref, rows_ref, sems,
 ):
     copies = [
@@ -144,6 +135,8 @@
                 (mask_hbm, mask_ref),
                 (forward_hbm, forward_ref),
                 (rows_hbm, rows_ref),
+                (inverse_hbm, inverse_ref),
+                (spread_hbm, spread_ref),
             )
         )
     ]
@@ -176,30 +169,23 @@
     packed(2 * odd, packed_chip_ref)
     packed(1, packed_own_ref)
 
-    for copy in copies[2:]:
+    for copy in copies[2:5]:
         copy.wait()
     col_spectra = jnp.dot(mask_ref[...], forward_ref[...], preferred_element_type=F32).astype(BF16)
+    product = jnp.dot(rows_ref[...], col_spectra, preferred_element_type=F32)
     freqs, cols = own_ref.shape[0] // 2, own_ref.shape[1]
 
-    def partial(block, out_ref):
-        product = jnp.dot(rows_ref[block], col_spectra, preferred_element_type=F32)
-        out_ref[:freqs, :] = product[:freqs, :cols] - product[freqs:, cols:]
-        out_ref[freqs:, :] = product[:freqs, cols:] + product[freqs:, :cols]
-
-    partial(2 - 2 * odd, chip_ref)
-    partial(2 * odd, core_ref)
-    partial(1, own_ref)
-
-
-def load_kernel(after_ref, *refs):
-    count = (len(refs) - 1) // 2
-    sems = refs[-1]
-    copies = [
-        pltpu.make_async_copy(refs[i], refs[count + i], sems.at[i]) for i in range(count)
-    ]
-    for copy in copies:
-        copy.start()
-    for copy in copies:
+    def partial(block):
+        part = product[2 * freqs * block : 2 * freqs * (block + 1)]
+        real = part[:freqs, :cols] - part[freqs:, cols:]
+        imag = part[:freqs, cols:] + part[freqs:, :cols]
+        return jnp.concatenate([real, imag], axis=0)
+
+    upper_side, own, lower_side = partial(0), partial(1), partial(2)
+    chip_ref[...] = jnp.where(odd == 1, upper_side, lower_side)
+    core_ref[...] = jnp.where(odd == 1, lower_side, upper_side)
+    own_ref[...] = own
+    for copy in copies[5:]:
         copy.wait()
 
 
@@ -216,14 +202,14 @@
 
 
 def edge_kernel(
-    weights_ref, own_ref, core_ref, near_ref, far_ref, kern_ref, inverse_ref, spread_ref,
+    weights_ref, own_ref, core_ref, chip_ref, kern_ref, inverse_ref, spread_ref,
     product_ref, edge_core_ref, edge_chip_ref,
 ):
     freqs, cols = own_ref.shape[0] // 2, own_ref.shape[1]
     rows = inverse_ref.shape[0] // 2
     kernels = kern_ref.shape[1]
     odd = parity()
-    chip = jnp.where(has_chip_side(), from_chip(near_ref, far_ref), 0.0)
+    chip = jnp.where(has_chip_side(), chip_ref[...], 0.0)
     spectrum = own_ref[...] + core_ref[...] + chip
     spec_real, spec_imag = spectrum[:freqs], spectrum[freqs:]
     for k in range(kernels):
@@ -240,7 +226,22 @@
         axis=0,
     )
     half = jnp.dot(lines, product_ref[...], preferred_element_type=F32).astype(BF16)
-    total = summed_intensity(half, 2 * reach, kernels, cols, spread_ref[...], weights_ref)
+    pairs = jnp.concatenate(
+        [
+            jnp.concatenate(
+                [half[: 2 * reach, k * cols : (k + 1) * cols], half[2 * reach :, k * cols : (k + 1) * cols]],
+                axis=1,
+            )
+            for k in range(kernels)
+        ],
+        axis=0,
+    )
+    field = jnp.dot(pairs, spread_ref[...], preferred_element_type=F32)
+    total = jnp.zeros((2 * reach, 2 * cols), F32)
+    for k in range(kernels):
+        part = field[2 * reach * k : 2 * reach * (k + 1)]
+        real, imag = part[:, : 2 * cols], part[:, 2 * cols :]
+        total = total + weights_ref[0, k] * (real * real + imag * imag)
     values = total.astype(BF16).astype(F32)
     top, bottom = values[:reach], values[reach:]
     edge_core_ref[...] = jnp.where(odd == 1, top, bottom)
@@ -300,12 +301,13 @@
 
 
 def resist_kernel(
-    intensity_ref, core_ref, near_ref, far_ref, inner_ref, outer_ref, high_ref, low_ref,
-    coords_near_ref, coords_far_ref,
-    resist_ref, table_ref, mean_chip_ref,
+    intensity_ref, core_ref, chip_ref, inner_ref, outer_ref, high_ref, low_ref,
+    coords_ref,
+    resist_hbm, table_ref, mean_chip_ref,
+    resist_ref, sem,
 ):
     odd = parity()
-    chip_edge = jnp.where(has_chip_side(), from_chip(near_ref, far_ref), 0.0)
+    chip_edge = jnp.where(has_chip_side(), chip_ref[...], 0.0)
     core_edge = core_ref[...]
     above = jnp.where(odd == 1, core_edge, chip_edge)
     below = jnp.where(odd == 1, chip_edge, core_edge)
@@ -320,21 +322,24 @@
         + jnp.dot(high, low_ref[...], preferred_element_type=F32)
     )
     resist_ref[...] = resist
+    copy = pltpu.make_async_copy(resist_ref, resist_hbm, sem)
+    copy.start()
     table_ref[...] = resist.astype(BF16)
-    mean_chip_ref[...] = site_means(table_ref[...], from_chip(coords_near_ref, coords_far_ref))
+    mean_chip_ref[...] = site_means(table_ref[...], coords_ref[...])
+    copy.wait()
 
 
 def mean_kernel(table_ref, coords_ref, mean_ref):
     mean_ref[...] = site_means(table_ref[...], coords_ref[...])
 
 
-def bias_kernel(threshold_ref, chosen_ref, own_ref, core_ref, near_ref, far_ref, steps_ref, out_ref):
+def bias_kernel(threshold_ref, chosen_ref, own_ref, core_ref, chip_ref, steps_ref, out_ref):
     frags = steps_ref.shape[1]
     odd = parity()
     lanes = lax.broadcasted_iota(jnp.int32, own_ref.shape, 0)
     total = jnp.zeros((8, frags), F32)
     for side, mean in (
-        (1, own_ref[...]), (2 - 2 * odd, core_ref[...]), (2 * odd, from_chip(near_ref, far_ref))
+        (1, own_ref[...]), (2 - 2 * odd, core_ref[...]), (2 * odd, chip_ref[...])
     ):
         first, second, third = (part.astype(F32) for part in three_parts(mean))
         parts = jnp.where(
@@ -347,35 +352,32 @@
     )
 
 
-def swaps(count):
-    def whole(pairs):
-        partner = {}
-        for a, b in pairs:
-            partner[a], partner[b] = b, a
-        return [(i, partner[i]) for i in range(count)]
-
-    quads = count // 4
-    core = [(i, i + 1) for i in range(0, count, 2)]
-    near = [(i + 1, i + 2) for i in range(0, count, 4)]
-    for quad in range(0, quads - 1, 2):
-        near += [(4 * quad + i, 4 * quad + 4 + i) for i in (0, 3)]
-    if quads % 2:
-        near.append((count - 4, count - 1))
-    far = [(0, 1), (count - 2, count - 1)] + [(i + 3, i + 4) for i in range(0, count - 4, 4)]
-    far += [(i + 2, i + 5) for i in range(0, count - 4, 4)]
-    return whole(core), whole(near), whole(far)
-
-
-def exchange_chip(to_chip):
-    _, near, far = swaps(lax.axis_size("tx"))
-    return lax.ppermute(to_chip, "tx", near), lax.ppermute(to_chip, "tx", far)
-
-
-def exchange_core(to_core):
-    return lax.ppermute(to_core, "tx", swaps(lax.axis_size("tx"))[0])
-
-
-def call(kernel, outs, args, smem=(), hbm=(), scratch=(), name=None):
+def chip_pairs(groups, count):
+    pairs = []
+    for group in range(groups):
+        first = group * count
+        for i in range(1, count - 1, 2):
+            pairs += [(first + i, first + i + 1), (first + i + 1, first + i)]
+    if groups % 2:
+        for group in range(groups):
+            pairs += [(group * count, (group + 1) * count - 1), ((group + 1) * count - 1, group * count)]
+    else:
+        for group in range(groups):
+            for end in (0, count - 1):
+                pairs.append((group * count + end, (group ^ 1) * count + end))
+    return pairs
+
+
+def swap_chips(to_chip):
+    pairs = chip_pairs(lax.axis_size("groups"), lax.axis_size("tx"))
+    return lax.ppermute(to_chip, ("groups", "tx"), pairs)
+
+
+def swap_cores(to_core):
+    return lax.ppermute(to_core, "tx", [(i, i ^ 1) for i in range(lax.axis_size("tx"))])
+
+
+def call(kernel, outs, args, smem=(), hbm=(), hbm_outs=(), scratch=(), name=None):
     specs = [
         pl.BlockSpec(
             memory_space=pltpu.SMEM if i in smem else pltpu.HBM if i in hbm else pltpu.VMEM
@@ -390,7 +392,10 @@
         kernel,
         out_shape=[jax.ShapeDtypeStruct(s, d) for s, d in outs],
         in_specs=specs,
-        out_specs=[pl.BlockSpec(memory_space=pltpu.VMEM) for _ in outs],
+        out_specs=[
+            pl.BlockSpec(memory_space=pltpu.HBM if i in hbm_outs else pltpu.VMEM)
+            for i in range(len(outs))
+        ],
         scratch_shapes=list(scratch),
         compiler_params=pltpu.CompilerParams(vmem_limit_bytes=VMEM_BYTES),
         name=name,
@@ -415,48 +420,43 @@
     means = ((8, capacity), F32)
     weights = kernel_weights.reshape(1, kernels)
 
-    own, to_core, to_chip, packed_core, packed_chip, packed_own, chosen = call(
+    inverse, spread, own, to_core, to_chip, packed_core, packed_chip, packed_own, chosen = call(
         front_kernel,
-        [spectrum] * 3 + [packed] * 3 + [((3, capacity, frags), BF16)],
+        [(row_inverse.shape, BF16), (col_inverse.shape, BF16)]
+        + [spectrum] * 3
+        + [packed] * 3
+        + [((3, capacity, frags), BF16)],
         (
             eval_tile.reshape(1, frags), site_coords.reshape(records, frags),
-            mask, col_forward, row_blocks,
+            mask, col_forward, row_blocks, row_inverse, col_inverse,
         ),
-        hbm=range(5),
+        hbm=range(7),
         scratch=[
             pltpu.VMEM((1, frags), jnp.int32),
             pltpu.VMEM((records, frags), F32),
             pltpu.VMEM(mask.shape, BF16),
             pltpu.VMEM(col_forward.shape, BF16),
             pltpu.VMEM(row_blocks.shape, BF16),
-            pltpu.SemaphoreType.DMA((5,)),
+            pltpu.SemaphoreType.DMA((7,)),
         ],
         name="front",
     )
-    got_near, got_far = exchange_chip(to_chip)
-    got_core = exchange_core(to_core)
-    coords_near, coords_far = exchange_chip(packed_chip)
-    coords_core = exchange_core(packed_core)
-    inverse, spread = call(
-        load_kernel,
-        [(row_inverse.shape, BF16), (col_inverse.shape, BF16)],
-        (own, row_inverse, col_inverse),
-        hbm=(1, 2),
-        scratch=[pltpu.SemaphoreType.DMA((2,))],
-        name="load",
-    )
+    got_chip = swap_chips(to_chip)
+    got_core = swap_cores(to_core)
+    coords_chip = swap_chips(packed_chip)
+    coords_core = swap_cores(packed_core)
     product, edge_core, edge_chip = call(
         edge_kernel,
         [((2 * row_freqs, flat), BF16), edge, edge],
         (
-            weights, own, got_core, got_near, got_far,
+            weights, own, got_core, got_chip,
             jnp.transpose(kernel_spectra, (0, 2, 1, 3)), inverse, spread,
         ),
         smem=(0,),
         name="edges",
     )
-    edge_near, edge_far = exchange_chip(edge_chip)
-    edge_core = exchange_core(edge_core)
+    edge_chip = swap_chips(edge_chip)
+    edge_core = swap_cores(edge_core)
     (intensity,) = call(
         imaging_kernel,
         [((tile_rows, samples), BF16)],
@@ -468,23 +468,19 @@
     resist, table, mean_chip = call(
         resist_kernel,
         [((tile_rows, tile_cols), F32), ((tile_rows, tile_cols), BF16), means],
-        (
-            intensity, edge_core, edge_near, edge_far, inner, outer, high, low,
-            coords_near, coords_far,
-        ),
+        (intensity, edge_core, edge_chip, inner, outer, high, low, coords_chip),
+        hbm_outs=(0,),
+        scratch=[pltpu.VMEM((tile_rows, tile_cols), F32), pltpu.SemaphoreType.DMA],
         name="resist",
     )
-    back_near, back_far = exchange_chip(mean_chip)
+    back_chip = swap_chips(mean_chip)
     (mean_core,) = call(mean_kernel, [means], (table, coords_core), name="mean_core")
-    back_core = exchange_core(mean_core)
+    back_core = swap_cores(mean_core)
     (mean_own,) = call(mean_kernel, [means], (table, packed_own), name="mean_own")
     (new_bias,) = call(
         bias_kernel,
         [((1, frags), F32)],
-        (
-            threshold, chosen, mean_own, back_core, back_near, back_far,
-            bias_steps.reshape(1, frags),
-        ),
+        (threshold, chosen, mean_own, back_core, back_chip, bias_steps.reshape(1, frags)),
         smem=(0,),
         name="bias",
     )

time: 29.9 us -> 26.4 us (0.88)
  starting transfers between devices: 12.5 us -> 7.79 us
  waiting for transfers between devices: 0.03 us -> 2.45 us
  Pallas kernels: 15.6 us -> 14.3 us
    ppermute x12 -> x8, starting transfers between devices: 12.5 us -> 7.79 us  [the longest x4 6.28 us: swap_chips(): return lax.ppermute(to_chip, ('groups', 'tx'), pairs)]
    ppermute x12 -> x8, waiting for transfers between devices: 0.03 us -> 2.45 us  [the longest x4 2.44 us: swap_chips(): return lax.ppermute(to_chip, ('groups', 'tx'), pairs)]
    pallas_call x8 -> x7, Pallas kernels: 15.6 us -> 14.3 us  [call(): pl.pallas_call(kernel, out_shape=[jax.ShapeDtypeStruct(s, d) for s, d in...]
  transfers between devices with their start and end apart: 12 -> 8, of which waited for: 0 -> 1; matrix products, arithmetic and copies ran while one was open for 0% -> 0% of each run, Pallas kernels for 34% -> 33%
where the time goes in v3:
time: 26.4 us; the launch traced here: 26 us
  Pallas kernels  14.3 us (54%)
  starting transfers between devices  7.79 us (30%)
  waiting for transfers between devices  2.45 us (9%)
  between operations  1.46 us (6%)
    pallas_call x7, Pallas kernels, call(): pl.pallas_call(kernel, out_shape=[jax.ShapeDtypeStruct(s, d) for s, d in...  14.3 us
    ppermute x4, starting transfers between devices, swap_chips(): return lax.ppermute(to_chip, ('groups', 'tx'), pairs)  6.28 us
    ppermute x4, waiting for transfers between devices, swap_chips(): return lax.ppermute(to_chip, ('groups', 'tx'), pairs)  2.44 us
    ppermute x4, starting transfers between devices, swap_cores(): lax.ppermute(to_core, 'tx', [(i, i ^ 1) for i in range(lax.axis_size('tx'...  1.51 us
  transfers between devices with their start and end apart: 8, of which 1 were waited for; matrix products, arithmetic and copies ran while one was open for 0% of the time, Pallas kernels for 33%

profile of v3, /device:TPU:0, one launch (start us, length us, event | category | flops | bytes accessed | tf_op | source)
XLA Modules:
  0.0 26.0 jit_solution(3449206251717644911)
XLA Ops:
  0.6 0.0 copy-start.6
  0.6 0.0 copy-start
  0.7 2.4 %front.1 = (bf16[512,192]{1,0:T(8,128)(2,1)S(1)}, bf16[256,512]{1,0:T(8,128)(2,1)S(1)}, f32[192,128]{1,0:T(8,128)S(1)}, f32[192,128]{1,0:T(8,128)S(1)}, f32[192,...) custom-call(s32[1,512]{1,0:T(1,128)} %bitcast.11, ...), custom_call_target="tpu_custom_call" | custom-call | tf_op jit(solution)/shard_map/front/pallas_call | solution.py:391
  3.0 0.5 %collective-permute-start = (f32[192,128]{1,0:T(8,128)S(1)}, f32[192,128]{1,0:T(8,128)S(1)}, u32[]{:S(2)}, u32[]{:S(2)}) collective-permute-start(f32[192,128]{1,0:T(8,128)S(1)} %get-tuple-element.18), channel_id=1, source_target_pairs={{0,1},{1,0},{2,3},{3,2},{4,5},{5,4},{6,7},{7,6},{8,9},{9,8},{10,11... | collective-permute-start | bytes 294920 | tf_op jit(solution)/shard_map/ppermute | solution.py:377
  3.5 2.6 %collective-permute-start.1 = (f32[192,128]{1,0:T(8,128)S(1)}, f32[192,128]{1,0:T(8,128)S(1)}, u32[]{:S(2)}, u32[]{:S(2)}) collective-permute-start(f32[192,128]{1,0:T(8,128)S(1)} %get-tuple-element.19), channel_id=1, source_target_pairs={{1,2},{2,1},{3,4},{4,3},{5,6},{6,5},{7,8},{8,7},{9,10},{10,9},{11,... | collective-permute-start | bytes 294920 | tf_op jit(solution)/shard_map/ppermute | solution.py:373
  6.1 0.1 collective-permute-start.4
  6.2 0.1 collective-permute-start.5
  6.3 0.0 collective-permute-done.core_ref
  6.3 2.4 %collective-permute-done.1.chip_ref = f32[192,128]{1,0:T(8,128)S(1)} collective-permute-done((f32[192,128]{1,0:T(8,128)S(1)}, f32[192,128]{1,0:T(8,128)S(1)}, u32[]{:S(2)}, u32[]{:S(2)}) %collective-permute-start.1) | collective-permute-done | bytes 98336 | tf_op jit(solution)/shard_map/ppermute | solution.py:373
  8.8 0.0 copy-start.3
  8.8 0.0 copy-start.4
  8.8 1.1 %edges.1 = (bf16[192,1536]{1,0:T(8,128)(2,1)S(1)}, f32[8,256]{1,0:T(8,128)S(1)}, f32[8,256]{1,0:T(8,128)S(1)}) custom-call(f32[1,12]{1,0:T(1,128)S(1)} %bitcast.8, f32[192,128]{1,0:T(8,128)S(1)} %get-tuple-element.17.own_ref, f32[192,128]{1,0:T(8,128)S(1)} %collective-permute-done.core_ref, f32[192,128]{1,0:T(8,128)S(1)} %collective-permute-done.1.chip_ref, ...), custom_call_target="tpu_custom_call" | custom-call | tf_op jit(solution)/shard_map/edges/pallas_call | solution.py:391
  9.9 0.1 collective-permute-start.2
  10.0 2.1 %collective-permute-start.3 = (f32[8,256]{1,0:T(8,128)S(1)}, f32[8,256]{1,0:T(8,128)S(1)}, u32[]{:S(2)}, u32[]{:S(2)}) collective-permute-start(f32[8,256]{1,0:T(8,128)S(1)} %get-tuple-element.24), channel_id=1, source_target_pairs={{1,2},{2,1},{3,4},{4,3},{5,6},{6,5},{7,8},{8,7},{9,10},{10,9},{11,... | collective-permute-start | bytes 24584 | tf_op jit(solution)/shard_map/ppermute | solution.py:373
  12.1 1.9 %imaging.1.intensity_ref = bf16[256,256]{1,0:T(8,128)(2,1)S(1)} custom-call(f32[1,12]{1,0:T(1,128)S(1)} %bitcast.9, bf16[192,1536]{1,0:T(8,128)(2,1)S(1)} %get-tuple-element.22.product_ref, bf16[512,192]{1,0:T(8,128)(2,1)S(1)} %get-tuple-element.20.inverse_ref, bf16[256,512]{1,0:T(8,128)(2,1)S(1)} %get-tuple-element.21.spread_ref), custom_call_target="tpu_custom_call" | custom-call | tf_op jit(solution)/shard_map/imaging/pallas_call | solution.py:391
  14.0 0.0 copy-start.5
  14.0 0.0 collective-permute-done.4.coords_ref
  14.0 0.0 collective-permute-done.2.core_ref
  14.1 0.0 collective-permute-done.3.chip_ref
  14.1 0.0 copy-done.1
  14.1 0.0 copy-done.2
  14.1 0.0 copy-done.3
  14.1 0.0 copy-done.4
  14.1 3.3 %resist.1 = (f32[256,1024]{1,0:T(8,128)}, bf16[256,1024]{1,0:T(8,128)(2,1)S(1)}, f32[8,256]{1,0:T(8,128)S(1)}) custom-call(bf16[256,256]{1,0:T(8,128)(2,1)S(1)} %imaging.1.intensity_ref, f32[8,256]{1,0:T(8,128)S(1)} %collective-permute-done.2.core_ref, f32[8,256]{1,0:T(8,128)S(1)} %collective-permute-done.3.chip_ref, bf16[256,256]{1,0:T(8,128)(2,1)S(1)} %copy-done.3, ...), custom_call_target="tpu_custom_call" | custom-call | tf_op jit(solution)/shard_map/resist/pallas_call | solution.py:391
  17.4 0.0 collective-permute-done.5.coords_ref
  17.4 2.4 %mean_core.1 = f32[8,256]{1,0:T(8,128)S(1)} custom-call(bf16[256,1024]{1,0:T(8,128)(2,1)S(1)} %get-tuple-element.28.table_ref, f32[32,256]{1,0:T(8,128)S(1)} %collective-permute-done.5.coords_ref), custom_call_target="tpu_custom_call" | custom-call | tf_op jit(solution)/shard_map/mean_core/pallas_call | solution.py:391
  19.8 0.8 %collective-permute-start.6 = (f32[8,256]{1,0:T(8,128)S(1)}, f32[8,256]{1,0:T(8,128)S(1)}, u32[]{:S(2)}, u32[]{:S(2)}) collective-permute-start(f32[8,256]{1,0:T(8,128)S(1)} %mean_core.1), channel_id=1, source_target_pairs={{0,1},{1,0},{2,3},{3,2},{4,5},{5,4},{6,7},{7,6},{8,9},{9,8},{10,11... | collective-permute-start | bytes 24584 | tf_op jit(solution)/shard_map/ppermute | solution.py:377
  20.6 1.5 %collective-permute-start.7 = (f32[8,256]{1,0:T(8,128)S(1)}, f32[8,256]{1,0:T(8,128)S(1)}, u32[]{:S(2)}, u32[]{:S(2)}) collective-permute-start(f32[8,256]{1,0:T(8,128)S(1)} %get-tuple-element.31), channel_id=1, source_target_pairs={{1,2},{2,1},{3,4},{4,3},{5,6},{6,5},{7,8},{8,7},{9,10},{10,9},{11,... | collective-permute-start | bytes 24584 | tf_op jit(solution)/shard_map/ppermute | solution.py:373
  22.8 2.4 %mean_own.1.own_ref = f32[8,256]{1,0:T(8,128)S(1)} custom-call(bf16[256,1024]{1,0:T(8,128)(2,1)S(1)} %get-tuple-element.28.table_ref, f32[32,256]{1,0:T(8,128)S(1)} %get-tuple-element.29.coords_ref), custom_call_target="tpu_custom_call" | custom-call | tf_op jit(solution)/shard_map/mean_own/pallas_call | solution.py:391
  25.2 0.0 collective-permute-done.6.core_ref
  25.2 0.0 collective-permute-done.7.chip_ref
  25.2 0.8 %bias.1 = f32[1,512]{1,0:T(1,128)} custom-call(f32[1]{0:T(128)S(6)} %copy.17.threshold_ref, bf16[3,256,512]{2,1,0:T(8,128)(2,1)S(1)} %get-tuple-element.27.chosen_ref, f32[8,256]{1,0:T(8,128)S(1)} %mean_own.1.own_ref, f32[8,256]{1,0:T(8,128)S(1)} %collective-permute-done.6.core_ref, f32[8,256]{1,0:T(8,128)S(1)} %collective-permute-done.7.chip_ref, ...), custom_call_target="tpu_custom_call" | custom-call | tf_op jit(solution)/shard_map/bias/pallas_call | solution.py:391
  (5 shorter events, 0.0 us)
Async XLA Ops:
  0.6 8.1 %copy-start.6 = (f32[12]{0:T(128)S(1)}, f32[12]{0:T(128)}, u32[]{:S(2)}) copy-start(f32[12]{0:T(128)} %param.17) | copy-start | bytes 148
  0.6 8.1 %copy-start = (f32[2,96,12,128]{3,1,2,0:T(8,128)S(1)}, f32[2,96,12,128]{3,1,2,0:T(8,128)}, u32[]{:S(2)}) copy-start(f32[2,96,12,128]{3,1,2,0:T(8,128)} %param.16) | copy-start | bytes 3538948
  3.0 3.3 %collective-permute-start = (f32[192,128]{1,0:T(8,128)S(1)}, f32[192,128]{1,0:T(8,128)S(1)}, u32[]{:S(2)}, u32[]{:S(2)}) collective-permute-start(f32[192,128]{1,0:T(8,128)S(1)} %get-tuple-element.18), channel_id=1, source_target_pairs={{0,1},{1,0},{2,3},{3,2},{4,5},{5,4},{6,7},{7,6},{8,9},{9,8},{10,11... | collective-permute-start | bytes 294920 | tf_op jit(solution)/shard_map/ppermute | solution.py:377
  3.5 5.2 %collective-permute-start.1 = (f32[192,128]{1,0:T(8,128)S(1)}, f32[192,128]{1,0:T(8,128)S(1)}, u32[]{:S(2)}, u32[]{:S(2)}) collective-permute-start(f32[192,128]{1,0:T(8,128)S(1)} %get-tuple-element.19), channel_id=1, source_target_pairs={{1,2},{2,1},{3,4},{4,3},{5,6},{6,5},{7,8},{8,7},{9,10},{10,9},{11,... | collective-permute-start | bytes 294920 | tf_op jit(solution)/shard_map/ppermute | solution.py:373
  6.1 7.9 %collective-permute-start.4 = (f32[32,256]{1,0:T(8,128)S(1)}, f32[32,256]{1,0:T(8,128)S(1)}, u32[]{:S(2)}, u32[]{:S(2)}) collective-permute-start(f32[32,256]{1,0:T(8,128)S(1)} %get-tuple-element.25), channel_id=1, source_target_pairs={{1,2},{2,1},{3,4},{4,3},{5,6},{6,5},{7,8},{8,7},{9,10},{10,9},{11,... | collective-permute-start | bytes 98312 | tf_op jit(solution)/shard_map/ppermute | solution.py:373
  6.2 11.2 %collective-permute-start.5 = (f32[32,256]{1,0:T(8,128)S(1)}, f32[32,256]{1,0:T(8,128)S(1)}, u32[]{:S(2)}, u32[]{:S(2)}) collective-permute-start(f32[32,256]{1,0:T(8,128)S(1)} %get-tuple-element.30), channel_id=1, source_target_pairs={{0,1},{1,0},{2,3},{3,2},{4,5},{5,4},{6,7},{7,6},{8,9},{9,8},{10,11... | collective-permute-start | bytes 98312 | tf_op jit(solution)/shard_map/ppermute | solution.py:377
  8.7 5.3 %copy-start.1 = (bf16[256,1024]{1,0:T(8,128)(2,1)S(1)}, bf16[256,1024]{1,0:T(8,128)(2,1)}, u32[]{:S(2)}) copy-start(bf16[256,1024]{1,0:T(8,128)(2,1)} %constant.22.clone.high_ref) | copy-start | bytes 1572868
  8.7 5.3 %copy-start.2 = (bf16[256,1024]{1,0:T(8,128)(2,1)S(1)}, bf16[256,1024]{1,0:T(8,128)(2,1)}, u32[]{:S(2)}) copy-start(bf16[256,1024]{1,0:T(8,128)(2,1)} %constant.23.clone.low_ref) | copy-start | bytes 1572868
  8.8 5.3 %copy-start.3 = (bf16[256,256]{1,0:T(8,128)(2,1)S(1)}, bf16[256,256]{1,0:T(8,128)(2,1)}, u32[]{:S(2)}) copy-start(bf16[256,256]{1,0:T(8,128)(2,1)} %constant.20.clone.inner_ref) | copy-start | bytes 393220
  8.8 5.3 %copy-start.4 = (bf16[256,16]{1,0:T(8,128)(2,1)S(1)}, bf16[256,16]{1,0:T(8,128)(2,1)}, u32[]{:S(2)}) copy-start(bf16[256,16]{1,0:T(8,128)(2,1)} %constant.21.clone.outer_ref) | copy-start | bytes 24580
  9.9 4.2 %collective-permute-start.2 = (f32[8,256]{1,0:T(8,128)S(1)}, f32[8,256]{1,0:T(8,128)S(1)}, u32[]{:S(2)}, u32[]{:S(2)}) collective-permute-start(f32[8,256]{1,0:T(8,128)S(1)} %get-tuple-element.23), channel_id=1, source_target_pairs={{0,1},{1,0},{2,3},{3,2},{4,5},{5,4},{6,7},{7,6},{8,9},{9,8},{10,11... | collective-permute-start | bytes 24584 | tf_op jit(solution)/shard_map/ppermute | solution.py:377
  10.0 4.1 %collective-permute-start.3 = (f32[8,256]{1,0:T(8,128)S(1)}, f32[8,256]{1,0:T(8,128)S(1)}, u32[]{:S(2)}, u32[]{:S(2)}) collective-permute-start(f32[8,256]{1,0:T(8,128)S(1)} %get-tuple-element.24), channel_id=1, source_target_pairs={{1,2},{2,1},{3,4},{4,3},{5,6},{6,5},{7,8},{8,7},{9,10},{10,9},{11,... | collective-permute-start | bytes 24584 | tf_op jit(solution)/shard_map/ppermute | solution.py:373
  14.0 11.2 %copy-start.5 = (s32[512]{0:T(512)S(1)}, s32[512]{0:T(512)}, u32[]{:S(2)}) copy-start(s32[512]{0:T(512)} %param.21) | copy-start | bytes 6148
  19.8 5.4 %collective-permute-start.6 = (f32[8,256]{1,0:T(8,128)S(1)}, f32[8,256]{1,0:T(8,128)S(1)}, u32[]{:S(2)}, u32[]{:S(2)}) collective-permute-start(f32[8,256]{1,0:T(8,128)S(1)} %mean_core.1), channel_id=1, source_target_pairs={{0,1},{1,0},{2,3},{3,2},{4,5},{5,4},{6,7},{7,6},{8,9},{9,8},{10,11... | collective-permute-start | bytes 24584 | tf_op jit(solution)/shard_map/ppermute | solution.py:377
  20.6 4.6 %collective-permute-start.7 = (f32[8,256]{1,0:T(8,128)S(1)}, f32[8,256]{1,0:T(8,128)S(1)}, u32[]{:S(2)}, u32[]{:S(2)}) collective-permute-start(f32[8,256]{1,0:T(8,128)S(1)} %get-tuple-element.31), channel_id=1, source_target_pairs={{1,2},{2,1},{3,4},{4,3},{5,6},{6,5},{7,8},{8,7},{9,10},{10,9},{11,... | collective-permute-start | bytes 24584 | tf_op jit(solution)/shard_map/ppermute | solution.py:373

commit v4 on v3

--- a/solution.py
+++ b/solution.py
@@ -20,6 +20,7 @@
 F32 = jnp.float32
 BF16 = jnp.bfloat16
 BLOCK = 64
+TOGETHER = 12
 VMEM_BYTES = 48 * 1024 * 1024
 
 
@@ -97,7 +98,8 @@
     row_blur = rounded(blur_weight(row_diff, reach))
     inner = row_blur[:, reach : reach + tile_rows]
     outer = np.concatenate([row_blur[:, :reach], row_blur[:, reach + tile_rows :]], axis=1)
-    return halves(spread_blur), np.ascontiguousarray(inner), np.ascontiguousarray(outer)
+    high, low = halves(spread_blur)
+    return np.concatenate([high, high, low], axis=0), np.ascontiguousarray(inner), np.ascontiguousarray(outer)
 
 
 def parity():
@@ -121,27 +123,42 @@
     return lax.dot_general(left, right, (((1,), (1,)), ((), ())), preferred_element_type=F32)
 
 
+def started(sems, first, *moves):
+    copies = []
+    for source, target, pieces in moves:
+        rows = source.shape[0] // pieces
+        for i in range(pieces):
+            part = pl.ds(i * rows, rows)
+            copies.append(
+                pltpu.make_async_copy(
+                    source.at[part], target.at[part], sems.at[first + len(copies)]
+                )
+            )
+            copies[-1].start()
+    return copies
+
+
+def load_kernel(
+    after_ref, threshold_ref, kern_hbm, inverse_hbm, spread_hbm,
+    level_ref, kern_ref, inverse_ref, spread_ref, sems,
+):
+    copies = started(
+        sems, 0, (kern_hbm, kern_ref, 2), (inverse_hbm, inverse_ref, 1), (spread_hbm, spread_ref, 1)
+    )
+    level_ref[...] = jnp.full(level_ref.shape, threshold_ref[0], F32)
+    for copy in copies:
+        copy.wait()
+
+
 def front_kernel(
-    eval_hbm, records_hbm, mask_hbm, forward_hbm, rows_hbm, inverse_hbm, spread_hbm,
-    inverse_ref, spread_ref, own_ref, core_ref, chip_ref, packed_core_ref, packed_chip_ref, packed_own_ref, chosen_ref,
+    eval_hbm, records_hbm, mask_hbm, forward_hbm, rows_hbm,
+    own_ref, core_ref, chip_ref, packed_core_ref, packed_chip_ref, packed_own_ref, chosen_ref,
     eval_ref, records_ref, mask_ref, forward_ref, rows_ref, sems,
 ):
-    copies = [
-        pltpu.make_async_copy(source, target, sems.at[i])
-        for i, (source, target) in enumerate(
-            (
-                (eval_hbm, eval_ref),
-                (records_hbm, records_ref),
-                (mask_hbm, mask_ref),
-                (forward_hbm, forward_ref),
-                (rows_hbm, rows_ref),
-                (inverse_hbm, inverse_ref),
-                (spread_hbm, spread_ref),
-            )
-        )
-    ]
-    for copy in copies:
-        copy.start()
+    small = started(sems, 0, (eval_hbm, eval_ref, 1), (records_hbm, records_ref, 1))
+    large = started(
+        sems, 2, (mask_hbm, mask_ref, 2), (forward_hbm, forward_ref, 2), (rows_hbm, rows_ref, 1)
+    )
     me = lax.axis_index("tx")
     odd = parity()
     frags = eval_ref.shape[1]
@@ -151,25 +168,26 @@
     after = lax.broadcasted_iota(jnp.int32, (frags, frags), 1)
     upper = (before <= after).astype(F32).astype(BF16)
     slots = lax.broadcasted_iota(jnp.int32, (capacity, frags), 0).astype(F32).astype(BF16)
-    copies[0].wait()
-    copies[1].wait()
+    for copy in small:
+        copy.wait()
     member = lax.broadcasted_iota(jnp.int32, (8, frags), 0) == eval_ref[...] - me + 1
     counts = jnp.dot(member.astype(F32).astype(BF16), upper, preferred_element_type=F32)
     code = jnp.where(member, counts - 1.0, -1.0)
     for side in range(3):
         row = jnp.broadcast_to(code[side : side + 1].astype(BF16), (capacity, frags))
-        chosen_ref[side] = jnp.where(slots == row, jnp.ones_like(slots), jnp.zeros_like(slots))
+        chosen_ref[pl.ds(side * capacity, capacity)] = jnp.where(slots == row, jnp.ones_like(slots), jnp.zeros_like(slots))
     pieces = jnp.concatenate(three_parts(records_ref[...]), axis=0)
 
     def packed(side, out_ref):
-        got = transposed_dot(pieces, chosen_ref[side])
+        chosen = chosen_ref[pl.ds(pl.multiple_of(side * capacity, capacity), capacity)]
+        got = transposed_dot(pieces, chosen)
         out_ref[...] = got[:count] + got[count : 2 * count] + got[2 * count :]
 
     packed(2 - 2 * odd, packed_core_ref)
     packed(2 * odd, packed_chip_ref)
     packed(1, packed_own_ref)
 
-    for copy in copies[2:5]:
+    for copy in large:
         copy.wait()
     col_spectra = jnp.dot(mask_ref[...], forward_ref[...], preferred_element_type=F32).astype(BF16)
     product = jnp.dot(rows_ref[...], col_spectra, preferred_element_type=F32)
@@ -185,20 +203,6 @@
     chip_ref[...] = jnp.where(odd == 1, upper_side, lower_side)
     core_ref[...] = jnp.where(odd == 1, lower_side, upper_side)
     own_ref[...] = own
-    for copy in copies[5:]:
-        copy.wait()
-
-
-def summed_intensity(half, rows, kernels, cols, spread, weights_ref):
-    total = None
-    for k in range(kernels):
-        lanes = slice(k * cols, (k + 1) * cols)
-        pair = jnp.concatenate([half[:rows, lanes], half[rows:, lanes]], axis=1)
-        field = jnp.dot(pair, spread, preferred_element_type=F32)
-        real, imag = field[:, : 2 * cols], field[:, 2 * cols :]
-        term = weights_ref[0, k] * (real * real + imag * imag)
-        total = term if total is None else total + term
-    return total
 
 
 def edge_kernel(
@@ -241,25 +245,42 @@
     for k in range(kernels):
         part = field[2 * reach * k : 2 * reach * (k + 1)]
         real, imag = part[:, : 2 * cols], part[:, 2 * cols :]
-        total = total + weights_ref[0, k] * (real * real + imag * imag)
+        total = total + weights_ref[:, k : k + 1] * (real * real + imag * imag)
     values = total.astype(BF16).astype(F32)
     top, bottom = values[:reach], values[reach:]
     edge_core_ref[...] = jnp.where(odd == 1, top, bottom)
     edge_chip_ref[...] = jnp.where(odd == 1, bottom, top)
 
 
-def imaging_kernel(weights_ref, product_ref, inverse_ref, spread_ref, intensity_ref, half_ref):
+def imaging_kernel(weights_ref, product_ref, inverse_ref, spread_ref, intensity_ref):
     rows, samples = intensity_ref.shape
     cols = samples // 2
     kernels = product_ref.shape[1] // cols
-    half_ref[...] = jnp.dot(
-        inverse_ref[...], product_ref[...], preferred_element_type=F32
-    ).astype(BF16)
-    total = summed_intensity(half_ref, rows, kernels, cols, spread_ref[...], weights_ref)
+    total = jnp.zeros((rows, samples), F32)
+    for first in range(0, kernels, TOGETHER):
+        lanes = slice(first * cols, (first + TOGETHER) * cols)
+        half = jnp.dot(
+            inverse_ref[...], product_ref[:, lanes], preferred_element_type=F32
+        ).astype(BF16)
+        pairs = [
+            jnp.concatenate(
+                [half[:rows, i * cols : (i + 1) * cols], half[rows:, i * cols : (i + 1) * cols]],
+                axis=1,
+            )
+            for i in range(TOGETHER)
+        ]
+        fields = jnp.dot(
+            jnp.concatenate(pairs, axis=0), spread_ref[...], preferred_element_type=F32
+        )
+        for i in range(TOGETHER):
+            field = fields[i * rows : (i + 1) * rows]
+            real, imag = field[:, :samples], field[:, samples:]
+            k = first + i
+            total = total + weights_ref[:, k : k + 1] * (real * real + imag * imag)
     intensity_ref[...] = total.astype(BF16)
 
 
-def site_means(table, coords):
+def site_means(table, coords, middle):
     tile_rows, tile_cols = table.shape
     slots = coords.shape[1]
     width = 256
@@ -297,13 +318,14 @@
         for g in range(groups + 1):
             weight = jnp.maximum(1.0 - jnp.abs(within - (eight + 8.0 * g)), 0.0)
             total = total + held[g] * weight
-    return jnp.broadcast_to(jnp.sum(total, axis=0, keepdims=True) * (1.0 / SITES), (8, slots))
+    mean = middle + jnp.sum(total, axis=0, keepdims=True) * (1.0 / SITES)
+    return jnp.broadcast_to(mean, (8, slots))
 
 
 def resist_kernel(
-    intensity_ref, core_ref, chip_ref, inner_ref, outer_ref, high_ref, low_ref,
+    intensity_ref, core_ref, chip_ref, inner_ref, outer_ref, operator_ref,
     coords_ref,
-    resist_hbm, table_ref, mean_chip_ref,
+    resist_hbm, table_ref, middle_ref, mean_chip_ref,
     resist_ref, sem,
 ):
     odd = parity()
@@ -314,41 +336,40 @@
     edges = jnp.concatenate([above, below], axis=0).astype(BF16)
     blurred = jnp.dot(inner_ref[...], intensity_ref[...], preferred_element_type=F32)
     blurred += jnp.dot(outer_ref[...], edges, preferred_element_type=F32)
+    middle = jnp.sum(jnp.sum(blurred, axis=0, keepdims=True), axis=1, keepdims=True)
+    middle = middle * (1.0 / (blurred.shape[0] * blurred.shape[1]))
     high = blurred.astype(BF16)
     low = (blurred - high.astype(F32)).astype(BF16)
-    resist = (
-        jnp.dot(high, high_ref[...], preferred_element_type=F32)
-        + jnp.dot(low, high_ref[...], preferred_element_type=F32)
-        + jnp.dot(high, low_ref[...], preferred_element_type=F32)
+    resist = jnp.dot(
+        jnp.concatenate([high, low, high], axis=1), operator_ref[...], preferred_element_type=F32
     )
     resist_ref[...] = resist
     copy = pltpu.make_async_copy(resist_ref, resist_hbm, sem)
     copy.start()
-    table_ref[...] = resist.astype(BF16)
-    mean_chip_ref[...] = site_means(table_ref[...], coords_ref[...])
+    table_ref[...] = (resist - middle).astype(BF16)
+    middle_ref[...] = jnp.broadcast_to(middle, middle_ref.shape)
+    mean_chip_ref[...] = site_means(table_ref[...], coords_ref[...], middle_ref[:1, :1])
     copy.wait()
 
 
-def mean_kernel(table_ref, coords_ref, mean_ref):
-    mean_ref[...] = site_means(table_ref[...], coords_ref[...])
-
-
-def bias_kernel(threshold_ref, chosen_ref, own_ref, core_ref, chip_ref, steps_ref, out_ref):
-    frags = steps_ref.shape[1]
-    odd = parity()
-    lanes = lax.broadcasted_iota(jnp.int32, own_ref.shape, 0)
-    total = jnp.zeros((8, frags), F32)
-    for side, mean in (
-        (1, own_ref[...]), (2 - 2 * odd, core_ref[...]), (2 * odd, chip_ref[...])
-    ):
-        first, second, third = (part.astype(F32) for part in three_parts(mean))
-        parts = jnp.where(
-            lanes == 0, first, jnp.where(lanes == 1, second, jnp.where(lanes == 2, third, 0.0))
-        ).astype(BF16)
-        total = total + jnp.dot(parts, chosen_ref[side], preferred_element_type=F32)
-    site_mean = jnp.sum(total, axis=0, keepdims=True)
+def mean_kernel(table_ref, middle_ref, coords_ref, mean_ref):
+    mean_ref[...] = site_means(table_ref[...], coords_ref[...], middle_ref[:1, :1])
+
+
+def bias_kernel(level_ref, chosen_ref, own_ref, core_ref, chip_ref, steps_ref, out_ref):
+    odd = parity() == 1
+    core, chip = core_ref[...], chip_ref[...]
+    means = jnp.concatenate(
+        [jnp.where(odd, core, chip), own_ref[...], jnp.where(odd, chip, core)], axis=1
+    )
+    lines = lax.broadcasted_iota(jnp.int32, means.shape, 0)
+    first, second, third = (part.astype(F32) for part in three_parts(means))
+    parts = jnp.where(lines == 0, first, jnp.where(lines == 1, second, third))
+    parts = jnp.where(lines < 3, parts, 0.0).astype(BF16)
+    found = jnp.dot(parts, chosen_ref[...], preferred_element_type=F32)
+    site_mean = jnp.sum(found, axis=0, keepdims=True)
     out_ref[...] = bias_step * steps_ref[...].astype(F32) - bias_gain * (
-        site_mean - threshold_ref[0]
+        site_mean - level_ref[:1, :1]
     )
 
 
@@ -413,24 +434,23 @@
     col_forward, row_blocks, row_inverse, col_inverse = imaging_tables(
         tile_rows, tile_cols, row_freqs, col_freqs
     )
-    (high, low), inner, outer = blur_tables(tile_rows, tile_cols, col_freqs, BLUR_REACH)
+    operator, inner, outer = blur_tables(tile_rows, tile_cols, col_freqs, BLUR_REACH)
     spectrum = ((2 * row_freqs, col_freqs), F32)
     packed = ((records, capacity), F32)
     edge = ((BLUR_REACH, samples), F32)
     means = ((8, capacity), F32)
     weights = kernel_weights.reshape(1, kernels)
 
-    inverse, spread, own, to_core, to_chip, packed_core, packed_chip, packed_own, chosen = call(
+    own, to_core, to_chip, packed_core, packed_chip, packed_own, chosen = call(
         front_kernel,
-        [(row_inverse.shape, BF16), (col_inverse.shape, BF16)]
-        + [spectrum] * 3
+        [spectrum] * 3
         + [packed] * 3
-        + [((3, capacity, frags), BF16)],
+        + [((3 * capacity, frags), BF16)],
         (
             eval_tile.reshape(1, frags), site_coords.reshape(records, frags),
-            mask, col_forward, row_blocks, row_inverse, col_inverse,
+            mask, col_forward, row_blocks,
         ),
-        hbm=range(7),
+        hbm=range(5),
         scratch=[
             pltpu.VMEM((1, frags), jnp.int32),
             pltpu.VMEM((records, frags), F32),
@@ -445,14 +465,22 @@
     got_core = swap_cores(to_core)
     coords_chip = swap_chips(packed_chip)
     coords_core = swap_cores(packed_core)
+    kern = jnp.transpose(kernel_spectra, (0, 2, 1, 3))
+    level, kern, inverse, spread = call(
+        load_kernel,
+        [((8, 128), F32), (kern.shape, F32), (row_inverse.shape, BF16), (col_inverse.shape, BF16)],
+        (own, threshold, kern, row_inverse, col_inverse),
+        smem=(1,),
+        hbm=(2, 3, 4),
+        scratch=[pltpu.SemaphoreType.DMA((4,))],
+        name="load",
+    )
     product, edge_core, edge_chip = call(
         edge_kernel,
         [((2 * row_freqs, flat), BF16), edge, edge],
         (
-            weights, own, got_core, got_chip,
-            jnp.transpose(kernel_spectra, (0, 2, 1, 3)), inverse, spread,
+            weights, own, got_core, got_chip, kern, inverse, spread,
         ),
-        smem=(0,),
         name="edges",
     )
     edge_chip = swap_chips(edge_chip)
@@ -461,27 +489,24 @@
         imaging_kernel,
         [((tile_rows, samples), BF16)],
         (weights, product, inverse, spread),
-        smem=(0,),
-        scratch=[pltpu.VMEM((2 * tile_rows, flat), BF16)],
         name="imaging",
     )
-    resist, table, mean_chip = call(
+    resist, table, middle, mean_chip = call(
         resist_kernel,
-        [((tile_rows, tile_cols), F32), ((tile_rows, tile_cols), BF16), means],
-        (intensity, edge_core, edge_chip, inner, outer, high, low, coords_chip),
+        [((tile_rows, tile_cols), F32), ((tile_rows, tile_cols), BF16), ((8, 128), F32), means],
+        (intensity, edge_core, edge_chip, inner, outer, operator, coords_chip),
         hbm_outs=(0,),
         scratch=[pltpu.VMEM((tile_rows, tile_cols), F32), pltpu.SemaphoreType.DMA],
         name="resist",
     )
     back_chip = swap_chips(mean_chip)
-    (mean_core,) = call(mean_kernel, [means], (table, coords_core), name="mean_core")
+    (mean_core,) = call(mean_kernel, [means], (table, middle, coords_core), name="mean_core")
     back_core = swap_cores(mean_core)
-    (mean_own,) = call(mean_kernel, [means], (table, packed_own), name="mean_own")
+    (mean_own,) = call(mean_kernel, [means], (table, middle, packed_own), name="mean_own")
     (new_bias,) = call(
         bias_kernel,
         [((1, frags), F32)],
-        (threshold, chosen, mean_own, back_core, back_chip, bias_steps.reshape(1, frags)),
-        smem=(0,),
+        (level, chosen, mean_own, back_core, back_chip, bias_steps.reshape(1, frags)),
         name="bias",
     )
     return resist, new_bias.reshape(frags)

time: 26.4 us -> 24.5 us (0.928)
  waiting for transfers between devices: 2.45 us -> 0.55 us
    ppermute x4, waiting for transfers between devices: 2.44 us -> 0.54 us  [swap_chips(): return lax.ppermute(to_chip, ('groups', 'tx'), pairs)]
    ppermute x4, starting transfers between devices: 6.28 us -> 6.79 us  [swap_chips(): return lax.ppermute(to_chip, ('groups', 'tx'), pairs)]
    ppermute x4, starting transfers between devices: 1.51 us -> 1.01 us  [swap_cores(): lax.ppermute(to_core, 'tx', [(i, i ^ 1) for i in range(lax.axis_size('tx'...]
    pallas_call x7 -> x8, Pallas kernels: 14.3 us -> 14.3 us  [call(): pl.pallas_call(kernel, out_shape=[jax.ShapeDtypeStruct(s, d) for s, d in...]
  transfers between devices with their start and end apart: 8 -> 8, of which waited for: 1 -> 2; matrix products, arithmetic and copies ran while one was open for 0% -> 0% of each run, Pallas kernels for 33% -> 47%
where the time goes in v4:
time: 24.5 us; the launch traced here: 24.1 us
  Pallas kernels  14.3 us (58%)
  starting transfers between devices  7.79 us (32%)
  between operations  1.41 us (6%)
  waiting for transfers between devices  0.55 us (2%)
    pallas_call x8, Pallas kernels, call(): pl.pallas_call(kernel, out_shape=[jax.ShapeDtypeStruct(s, d) for s, d in...  14.3 us
    ppermute x4, starting transfers between devices, swap_chips(): return lax.ppermute(to_chip, ('groups', 'tx'), pairs)  6.79 us
    ppermute x4, starting transfers between devices, swap_cores(): lax.ppermute(to_core, 'tx', [(i, i ^ 1) for i in range(lax.axis_size('tx'...  1.01 us
    ppermute x4, waiting for transfers between devices, swap_chips(): return lax.ppermute(to_chip, ('groups', 'tx'), pairs)  0.54 us
  transfers between devices with their start and end apart: 8, of which 2 were waited for; matrix products, arithmetic and copies ran while one was open for 0% of the time, Pallas kernels for 47%

profile of v4, /device:TPU:0, one launch (start us, length us, event | category | flops | bytes accessed | tf_op | source)
XLA Modules:
  0.0 24.1 jit_solution(15270736962015114533)
XLA Ops:
  0.6 2.3 %front.1 = (f32[192,128]{1,0:T(8,128)S(1)}, f32[192,128]{1,0:T(8,128)S(1)}, f32[192,128]{1,0:T(8,128)S(1)}, f32[32,256]{1,0:T(8,128)S(1)}, f32[32,256]{1,0:T(8,1...) custom-call(s32[1,512]{1,0:T(1,128)} %bitcast.11, f32[32,512]{1,0:T(8,128)} %bitcast.10, ...), custom_call_target="tpu_custom_call" | custom-call | tf_op jit(solution)/shard_map/front/pallas_call | solution.py:412
  2.9 0.0 copy-start.4
  2.9 0.5 %collective-permute-start = (f32[192,128]{1,0:T(8,128)S(1)}, f32[192,128]{1,0:T(8,128)S(1)}, u32[]{:S(2)}, u32[]{:S(2)}) collective-permute-start(f32[192,128]{1,0:T(8,128)S(1)} %get-tuple-element.21), channel_id=1, source_target_pairs={{0,1},{1,0},{2,3},{3,2},{4,5},{5,4},{6,7},{7,6},{8,9},{9,8},{10,11... | collective-permute-start | bytes 294920 | tf_op jit(solution)/shard_map/ppermute | solution.py:398
  3.4 2.6 %collective-permute-start.1 = (f32[192,128]{1,0:T(8,128)S(1)}, f32[192,128]{1,0:T(8,128)S(1)}, u32[]{:S(2)}, u32[]{:S(2)}) collective-permute-start(f32[192,128]{1,0:T(8,128)S(1)} %get-tuple-element.22), channel_id=1, source_target_pairs={{1,2},{2,1},{3,4},{4,3},{5,6},{6,5},{7,8},{8,7},{9,10},{10,9},{11,... | collective-permute-start | bytes 294920 | tf_op jit(solution)/shard_map/ppermute | solution.py:394
  6.0 0.1 collective-permute-start.4
  6.1 0.1 collective-permute-start.5
  6.9 1.4 %load.1 = (f32[8,128]{1,0:T(8,128)S(1)}, f32[2,12,96,128]{3,2,1,0:T(8,128)S(1)}, bf16[512,192]{1,0:T(8,128)(2,1)S(1)}, bf16[256,512]{1,0:T(8,128)(2,1)S(1)}) custom-call(f32[192,128]{1,0:T(8,128)S(1)} %get-tuple-element.20.after_ref.own_ref, f32[1]{0:T(128)S(6)} %copy.16.threshold_ref, f32[2,12,96,128]{3,2,1,0:T(8,128)} %bitcast.9, ...), custom_call_target="tpu_custom_call" | custom-call | tf_op jit(solution)/shard_map/load/pallas_call | solution.py:412
  8.3 0.0 collective-permute-done.core_ref
  8.3 0.3 %collective-permute-done.1.chip_ref = f32[192,128]{1,0:T(8,128)S(1)} collective-permute-done((f32[192,128]{1,0:T(8,128)S(1)}, f32[192,128]{1,0:T(8,128)S(1)}, u32[]{:S(2)}, u32[]{:S(2)}) %collective-permute-start.1) | collective-permute-done | bytes 98336 | tf_op jit(solution)/shard_map/ppermute | solution.py:394
  8.6 0.0 copy-done.4
  8.6 0.0 copy-start
  8.6 0.5 %edges.1 = (bf16[192,1536]{1,0:T(8,128)(2,1)S(1)}, f32[8,256]{1,0:T(8,128)S(1)}, f32[8,256]{1,0:T(8,128)S(1)}) custom-call(f32[1,12]{1,0:T(1,128)S(1)} %bitcast.7, f32[192,128]{1,0:T(8,128)S(1)} %get-tuple-element.20.after_ref.own_ref, f32[192,128]{1,0:T(8,128)S(1)} %collective-permute-done.core_ref, f32[192,128]{1,0:T(8,128)S(1)} %collective-permute-done.1.chip_ref, ...), custom_call_target="tpu_custom_call" | custom-call | tf_op jit(solution)/shard_map/edges/pallas_call | solution.py:412
  9.2 0.2 collective-permute-start.2
  9.4 2.0 %collective-permute-start.3 = (f32[8,256]{1,0:T(8,128)S(1)}, f32[8,256]{1,0:T(8,128)S(1)}, u32[]{:S(2)}, u32[]{:S(2)}) collective-permute-start(f32[8,256]{1,0:T(8,128)S(1)} %get-tuple-element.28), channel_id=1, source_target_pairs={{1,2},{2,1},{3,4},{4,3},{5,6},{6,5},{7,8},{8,7},{9,10},{10,9},{11,... | collective-permute-start | bytes 24584 | tf_op jit(solution)/shard_map/ppermute | solution.py:394
  11.4 1.4 %imaging.1.intensity_ref = bf16[256,256]{1,0:T(8,128)(2,1)S(1)} custom-call(f32[1,12]{1,0:T(1,128)S(1)} %bitcast.8, bf16[192,1536]{1,0:T(8,128)(2,1)S(1)} %get-tuple-element.26.product_ref, bf16[512,192]{1,0:T(8,128)(2,1)S(1)} %get-tuple-element.24.inverse_ref, bf16[256,512]{1,0:T(8,128)(2,1)S(1)} %get-tuple-element.25.spread_ref), custom_call_target="tpu_custom_call" | custom-call | tf_op jit(solution)/shard_map/imaging/pallas_call | solution.py:412
  12.8 0.0 copy-start.3
  12.8 0.0 collective-permute-done.4.coords_ref
  12.8 0.0 collective-permute-done.2.core_ref
  12.8 0.2 collective-permute-done.3.chip_ref
  13.0 0.0 copy-done
  13.0 0.0 copy-done.1
  13.0 0.0 copy-done.2
  13.1 3.1 %resist.1 = (f32[256,1024]{1,0:T(8,128)}, bf16[256,1024]{1,0:T(8,128)(2,1)S(1)}, f32[8,128]{1,0:T(8,128)S(1)}, f32[8,256]{1,0:T(8,128)S(1)}) custom-call(bf16[256,256]{1,0:T(8,128)(2,1)S(1)} %imaging.1.intensity_ref, f32[8,256]{1,0:T(8,128)S(1)} %collective-permute-done.2.core_ref, f32[8,256]{1,0:T(8,128)S(1)} %collective-permute-done.3.chip_ref, ...), custom_call_target="tpu_custom_call" | custom-call | tf_op jit(solution)/shard_map/resist/pallas_call | solution.py:412
  16.1 2.1 %collective-permute-start.7 = (f32[8,256]{1,0:T(8,128)S(1)}, f32[8,256]{1,0:T(8,128)S(1)}, u32[]{:S(2)}, u32[]{:S(2)}) collective-permute-start(f32[8,256]{1,0:T(8,128)S(1)} %get-tuple-element.37), channel_id=1, source_target_pairs={{1,2},{2,1},{3,4},{4,3},{5,6},{6,5},{7,8},{8,7},{9,10},{10,9},{11,... | collective-permute-start | bytes 24584 | tf_op jit(solution)/shard_map/ppermute | solution.py:394
  18.2 0.0 collective-permute-done.5.coords_ref
  18.2 2.4 %mean_core.1 = f32[8,256]{1,0:T(8,128)S(1)} custom-call(bf16[256,1024]{1,0:T(8,128)(2,1)S(1)} %get-tuple-element.33.table_ref, f32[8,128]{1,0:T(8,128)S(1)} %get-tuple-element.34.middle_ref, f32[32,256]{1,0:T(8,128)S(1)} %collective-permute-done.5.coords_ref), custom_call_target="tpu_custom_call" | custom-call | tf_op jit(solution)/shard_map/mean_core/pallas_call | solution.py:412
  20.7 0.2 collective-permute-start.6
  20.8 2.4 %mean_own.1.own_ref = f32[8,256]{1,0:T(8,128)S(1)} custom-call(bf16[256,1024]{1,0:T(8,128)(2,1)S(1)} %get-tuple-element.33.table_ref, f32[8,128]{1,0:T(8,128)S(1)} %get-tuple-element.34.middle_ref, f32[32,256]{1,0:T(8,128)S(1)} %get-tuple-element.35.coords_ref), custom_call_target="tpu_custom_call" | custom-call | tf_op jit(solution)/shard_map/mean_own/pallas_call | solution.py:412
  23.3 0.0 collective-permute-done.7.chip_ref
  23.3 0.0 collective-permute-done.6.core_ref
  23.3 0.0 copy-done.3
  23.3 0.8 %bias.1 = f32[1,512]{1,0:T(1,128)} custom-call(f32[8,128]{1,0:T(8,128)S(1)} %get-tuple-element.31.level_ref, bf16[768,512]{1,0:T(8,128)(2,1)S(1)} %get-tuple-element.32.chosen_ref, f32[8,256]{1,0:T(8,128)S(1)} %mean_own.1.own_ref, f32[8,256]{1,0:T(8,128)S(1)} %collective-permute-done.6.core_ref, f32[8,256]{1,0:T(8,128)S(1)} %collective-permute-done.7.chip_ref, ...), custom_call_target="tpu_custom_call" | custom-call | tf_op jit(solution)/shard_map/bias/pallas_call | solution.py:412
  (2 shorter events, 0.0 us)
Async XLA Ops:
  2.9 5.7 %copy-start.4 = (f32[12]{0:T(128)S(1)}, f32[12]{0:T(128)}, u32[]{:S(2)}) copy-start(f32[12]{0:T(128)} %param.16) | copy-start | bytes 148
  2.9 5.4 %collective-permute-start = (f32[192,128]{1,0:T(8,128)S(1)}, f32[192,128]{1,0:T(8,128)S(1)}, u32[]{:S(2)}, u32[]{:S(2)}) collective-permute-start(f32[192,128]{1,0:T(8,128)S(1)} %get-tuple-element.21), channel_id=1, source_target_pairs={{0,1},{1,0},{2,3},{3,2},{4,5},{5,4},{6,7},{7,6},{8,9},{9,8},{10,11... | collective-permute-start | bytes 294920 | tf_op jit(solution)/shard_map/ppermute | solution.py:398
  3.4 5.2 %collective-permute-start.1 = (f32[192,128]{1,0:T(8,128)S(1)}, f32[192,128]{1,0:T(8,128)S(1)}, u32[]{:S(2)}, u32[]{:S(2)}) collective-permute-start(f32[192,128]{1,0:T(8,128)S(1)} %get-tuple-element.22), channel_id=1, source_target_pairs={{1,2},{2,1},{3,4},{4,3},{5,6},{6,5},{7,8},{8,7},{9,10},{10,9},{11,... | collective-permute-start | bytes 294920 | tf_op jit(solution)/shard_map/ppermute | solution.py:394
  6.0 6.8 %collective-permute-start.4 = (f32[32,256]{1,0:T(8,128)S(1)}, f32[32,256]{1,0:T(8,128)S(1)}, u32[]{:S(2)}, u32[]{:S(2)}) collective-permute-start(f32[32,256]{1,0:T(8,128)S(1)} %get-tuple-element.29), channel_id=1, source_target_pairs={{1,2},{2,1},{3,4},{4,3},{5,6},{6,5},{7,8},{8,7},{9,10},{10,9},{11,... | collective-permute-start | bytes 98312 | tf_op jit(solution)/shard_map/ppermute | solution.py:394
  6.1 12.1 %collective-permute-start.5 = (f32[32,256]{1,0:T(8,128)S(1)}, f32[32,256]{1,0:T(8,128)S(1)}, u32[]{:S(2)}, u32[]{:S(2)}) collective-permute-start(f32[32,256]{1,0:T(8,128)S(1)} %get-tuple-element.36), channel_id=1, source_target_pairs={{0,1},{1,0},{2,3},{3,2},{4,5},{5,4},{6,7},{7,6},{8,9},{9,8},{10,11... | collective-permute-start | bytes 98312 | tf_op jit(solution)/shard_map/ppermute | solution.py:398
  8.6 4.4 %copy-start = (bf16[768,1024]{1,0:T(8,128)(2,1)S(1)}, bf16[768,1024]{1,0:T(8,128)(2,1)}, u32[]{:S(2)}) copy-start(bf16[768,1024]{1,0:T(8,128)(2,1)} %constant.20.clone.operator_ref) | copy-start | bytes 4718596
  8.6 4.4 %copy-start.1 = (bf16[256,256]{1,0:T(8,128)(2,1)S(1)}, bf16[256,256]{1,0:T(8,128)(2,1)}, u32[]{:S(2)}) copy-start(bf16[256,256]{1,0:T(8,128)(2,1)} %constant.18.clone.inner_ref) | copy-start | bytes 393220
  8.6 4.4 %copy-start.2 = (bf16[256,16]{1,0:T(8,128)(2,1)S(1)}, bf16[256,16]{1,0:T(8,128)(2,1)}, u32[]{:S(2)}) copy-start(bf16[256,16]{1,0:T(8,128)(2,1)} %constant.19.clone.outer_ref) | copy-start | bytes 24580
  9.2 3.7 %collective-permute-start.2 = (f32[8,256]{1,0:T(8,128)S(1)}, f32[8,256]{1,0:T(8,128)S(1)}, u32[]{:S(2)}, u32[]{:S(2)}) collective-permute-start(f32[8,256]{1,0:T(8,128)S(1)} %get-tuple-element.27), channel_id=1, source_target_pairs={{0,1},{1,0},{2,3},{3,2},{4,5},{5,4},{6,7},{7,6},{8,9},{9,8},{10,11... | collective-permute-start | bytes 24584 | tf_op jit(solution)/shard_map/ppermute | solution.py:398
  9.4 3.7 %collective-permute-start.3 = (f32[8,256]{1,0:T(8,128)S(1)}, f32[8,256]{1,0:T(8,128)S(1)}, u32[]{:S(2)}, u32[]{:S(2)}) collective-permute-start(f32[8,256]{1,0:T(8,128)S(1)} %get-tuple-element.28), channel_id=1, source_target_pairs={{1,2},{2,1},{3,4},{4,3},{5,6},{6,5},{7,8},{8,7},{9,10},{10,9},{11,... | collective-permute-start | bytes 24584 | tf_op jit(solution)/shard_map/ppermute | solution.py:394
  12.8 10.5 %copy-start.3 = (s32[512]{0:T(512)S(1)}, s32[512]{0:T(512)}, u32[]{:S(2)}) copy-start(s32[512]{0:T(512)} %param.20) | copy-start | bytes 6148
  16.1 7.2 %collective-permute-start.7 = (f32[8,256]{1,0:T(8,128)S(1)}, f32[8,256]{1,0:T(8,128)S(1)}, u32[]{:S(2)}, u32[]{:S(2)}) collective-permute-start(f32[8,256]{1,0:T(8,128)S(1)} %get-tuple-element.37), channel_id=1, source_target_pairs={{1,2},{2,1},{3,4},{4,3},{5,6},{6,5},{7,8},{8,7},{9,10},{10,9},{11,... | collective-permute-start | bytes 24584 | tf_op jit(solution)/shard_map/ppermute | solution.py:394
  20.7 2.6 %collective-permute-start.6 = (f32[8,256]{1,0:T(8,128)S(1)}, f32[8,256]{1,0:T(8,128)S(1)}, u32[]{:S(2)}, u32[]{:S(2)}) collective-permute-start(f32[8,256]{1,0:T(8,128)S(1)} %mean_core.1), channel_id=1, source_target_pairs={{0,1},{1,0},{2,3},{3,2},{4,5},{5,4},{6,7},{7,6},{8,9},{9,8},{10,11... | collective-permute-start | bytes 24584 | tf_op jit(solution)/shard_map/ppermute | solution.py:398

commit v5 on v4

--- a/solution.py
+++ b/solution.py
@@ -1,3 +1,4 @@
+import functools
 import math
 
 import jax
@@ -19,9 +20,9 @@
 
 F32 = jnp.float32
 BF16 = jnp.bfloat16
-BLOCK = 64
-TOGETHER = 12
-VMEM_BYTES = 48 * 1024 * 1024
+SINE = (1.57079628989, -0.645963358138, 0.0796884742403, -0.0046722194159, 0.000150816735945)
+COSINE = (0.99999999978, -1.23370053428, 0.253669322509, -0.0208626876045, 0.000917723911039, -2.38245358719e-05)
+VMEM_BYTES = 32 * 1024 * 1024
 
 
 def rounded(table):
@@ -99,7 +100,25 @@
     inner = row_blur[:, reach : reach + tile_rows]
     outer = np.concatenate([row_blur[:, :reach], row_blur[:, reach + tile_rows :]], axis=1)
     high, low = halves(spread_blur)
-    return np.concatenate([high, high, low], axis=0), np.ascontiguousarray(inner), np.ascontiguousarray(outer)
+    operator = np.concatenate([high, high, low], axis=0)
+
+    freqs = np.arange(col_freqs)
+    gauss = blur_weight(np.arange(-reach, reach + 1), reach)
+    gauss = rounded(gauss).astype(np.float64)
+    theta = 2.0 * math.pi * freqs / tile_cols
+    gain = np.cos(theta[:, None] * np.arange(-reach, reach + 1)[None, :]) @ gauss
+    gain = gain * np.where(freqs == 0, 1.0, 2.0) / samples * np.cos(theta / 2.0)
+    cosines, sines = twiddle(freqs, np.arange(samples), samples, 1.0)
+    ring = np.zeros((tile_cols, tile_cols))
+    for shift in range(-reach, reach + 1):
+        ring[line, (line + shift) % tile_cols] = gauss[shift + reach]
+    edge = np.concatenate([line[:reach], line[tile_cols - reach :]])
+    cut = (spread @ (col_blur.astype(np.float64) - ring)[:, edge]).T
+    waves = np.concatenate([gain[:, None] * cosines, -gain[:, None] * sines, cut], axis=0)
+    high, low = halves(waves)
+    waves = np.concatenate([high, high, low], axis=1)
+    slope = np.broadcast_to(np.tan(theta / 2.0)[:, None], (col_freqs, 128)).astype(np.float32)
+    return operator, waves, np.ascontiguousarray(slope), np.ascontiguousarray(inner), np.ascontiguousarray(outer)
 
 
 def parity():
@@ -139,13 +158,14 @@
 
 
 def load_kernel(
-    after_ref, threshold_ref, kern_hbm, inverse_hbm, spread_hbm,
-    level_ref, kern_ref, inverse_ref, spread_ref, sems,
+    cols, coords_ref, threshold_ref, kern_hbm, inverse_hbm, spread_hbm,
+    level_ref, kern_ref, inverse_ref, spread_ref, tents_ref, spin_ref, ends_ref, sems,
 ):
     copies = started(
         sems, 0, (kern_hbm, kern_ref, 2), (inverse_hbm, inverse_ref, 1), (spread_hbm, spread_ref, 1)
     )
     level_ref[...] = jnp.full(level_ref.shape, threshold_ref[0], F32)
+    site_tables(coords_ref[...], tents_ref, spin_ref, ends_ref, cols)
     for copy in copies:
         copy.wait()
 
@@ -203,6 +223,14 @@
     chip_ref[...] = jnp.where(odd == 1, upper_side, lower_side)
     core_ref[...] = jnp.where(odd == 1, lower_side, upper_side)
     own_ref[...] = own
+
+
+def stacked_pairs(half, rows, kernels, cols):
+    pairs = []
+    for k in range(kernels):
+        lanes = slice(k * cols, (k + 1) * cols)
+        pairs.append(jnp.concatenate([half[:rows, lanes], half[rows:, lanes]], axis=1))
+    return jnp.concatenate(pairs, axis=0)
 
 
 def edge_kernel(
@@ -230,16 +258,7 @@
         axis=0,
     )
     half = jnp.dot(lines, product_ref[...], preferred_element_type=F32).astype(BF16)
-    pairs = jnp.concatenate(
-        [
-            jnp.concatenate(
-                [half[: 2 * reach, k * cols : (k + 1) * cols], half[2 * reach :, k * cols : (k + 1) * cols]],
-                axis=1,
-            )
-            for k in range(kernels)
-        ],
-        axis=0,
-    )
+    pairs = stacked_pairs(half, 2 * reach, kernels, cols)
     field = jnp.dot(pairs, spread_ref[...], preferred_element_type=F32)
     total = jnp.zeros((2 * reach, 2 * cols), F32)
     for k in range(kernels):
@@ -252,81 +271,110 @@
     edge_chip_ref[...] = jnp.where(odd == 1, bottom, top)
 
 
-def imaging_kernel(weights_ref, product_ref, inverse_ref, spread_ref, intensity_ref):
+def imaging_kernel(
+    tile_cols, weights_ref, product_ref, inverse_ref, spread_ref, chip_coords_ref, core_coords_ref,
+    intensity_ref, chip_tents_ref, chip_spin_ref, chip_ends_ref,
+    core_tents_ref, core_spin_ref, core_ends_ref,
+):
     rows, samples = intensity_ref.shape
     cols = samples // 2
     kernels = product_ref.shape[1] // cols
+    half = jnp.dot(inverse_ref[...], product_ref[...], preferred_element_type=F32).astype(BF16)
+    fields = jnp.dot(
+        stacked_pairs(half, rows, kernels, cols), spread_ref[...], preferred_element_type=F32
+    )
     total = jnp.zeros((rows, samples), F32)
-    for first in range(0, kernels, TOGETHER):
-        lanes = slice(first * cols, (first + TOGETHER) * cols)
-        half = jnp.dot(
-            inverse_ref[...], product_ref[:, lanes], preferred_element_type=F32
-        ).astype(BF16)
-        pairs = [
-            jnp.concatenate(
-                [half[:rows, i * cols : (i + 1) * cols], half[rows:, i * cols : (i + 1) * cols]],
-                axis=1,
-            )
-            for i in range(TOGETHER)
-        ]
-        fields = jnp.dot(
-            jnp.concatenate(pairs, axis=0), spread_ref[...], preferred_element_type=F32
-        )
-        for i in range(TOGETHER):
-            field = fields[i * rows : (i + 1) * rows]
-            real, imag = field[:, :samples], field[:, samples:]
-            k = first + i
-            total = total + weights_ref[:, k : k + 1] * (real * real + imag * imag)
+    for k in range(kernels):
+        field = fields[k * rows : (k + 1) * rows]
+        real, imag = field[:, :samples], field[:, samples:]
+        total = total + weights_ref[:, k : k + 1] * (real * real + imag * imag)
     intensity_ref[...] = total.astype(BF16)
-
-
-def site_means(table, coords, middle):
-    tile_rows, tile_cols = table.shape
-    slots = coords.shape[1]
-    width = 256
-    low_line = lax.broadcasted_iota(jnp.int32, (width, slots), 0).astype(F32).astype(BF16)
-    none = jnp.zeros((width, slots), BF16)
+    site_tables(chip_coords_ref[...], chip_tents_ref, chip_spin_ref, chip_ends_ref, tile_cols)
+    site_tables(core_coords_ref[...], core_tents_ref, core_spin_ref, core_ends_ref, tile_cols)
+
+
+def turned(index, period):
+    turns = index * (1.0 / period)
+    part = 2.0 * (turns - jnp.round(turns))
+    square = part * part
+    sine = SINE[-1]
+    for term in SINE[-2::-1]:
+        sine = sine * square + term
+    sine = sine * part
+    cosine = COSINE[-1]
+    for term in COSINE[-2::-1]:
+        cosine = cosine * square + term
+    return 1.0 - 2.0 * sine * sine, 2.0 * sine * cosine
+
+
+def site_tables(coords, tents_ref, spin_ref, ends_ref, tile_cols):
+    tile_rows, slots = tents_ref.shape[1:]
+    groups = spin_ref.shape[1] // 2
     eight = lax.broadcasted_iota(jnp.int32, (8, slots), 0).astype(F32)
-    groups = BLOCK // 8
-    blocks = tile_rows // BLOCK
-    total = jnp.zeros((8, slots), F32)
+    group = lax.broadcasted_iota(jnp.int32, (groups, slots), 0).astype(F32)
+    line = lax.broadcasted_iota(jnp.int32, (tile_rows, slots), 0).astype(F32).astype(BF16)
+    none = jnp.zeros((tile_rows, slots), BF16)
+    edge = lax.broadcasted_iota(jnp.int32, (2 * BLUR_REACH, slots), 0).astype(F32)
+    edge = jnp.where(edge < BLUR_REACH, edge, edge + (tile_cols - 2.0 * BLUR_REACH))
+
+    def wide(row, dtype=F32):
+        return jnp.broadcast_to(row.astype(dtype), (tile_rows, slots))
+
     for site in range(SITES):
-        col_pos = coords[SITES + site : SITES + site + 1] * (tile_cols - 1)
-        low = jnp.minimum(jnp.floor(col_pos), tile_cols - 2.0)
-        part = col_pos - low
-        low_weight = jnp.broadcast_to((1.0 - part).astype(BF16), (width, slots))
-        high_weight = jnp.broadcast_to(part.astype(BF16), (width, slots))
-        tents = []
-        for start in range(0, tile_cols, width):
-            hits = []
-            for index in (low - start, low + (1.0 - start)):
-                inside = jnp.logical_and(index >= 0.0, index < width)
-                index = jnp.where(inside, index, -1.0).astype(BF16)
-                hits.append(low_line == jnp.broadcast_to(index, (width, slots)))
-            tents.append(jnp.where(hits[0], low_weight, jnp.where(hits[1], high_weight, none)))
-        picked = jnp.dot(table, jnp.concatenate(tents, axis=0), preferred_element_type=F32)
-        row_pos = coords[site : site + 1] * (tile_rows - 1)
-        block = jnp.minimum(jnp.floor(row_pos * (1.0 / BLOCK)), blocks - 1.0)
-        within = jnp.broadcast_to(row_pos - block * BLOCK, (8, slots))
-        block = jnp.broadcast_to(block, (8, slots))
-        held = [jnp.zeros((8, slots), F32) for _ in range(groups + 1)]
-        for b in range(blocks):
-            hit = block == float(b)
-            for g in range(groups + 1 if b < blocks - 1 else groups):
-                first = b * BLOCK + 8 * g
-                held[g] = jnp.where(hit, picked[first : first + 8], held[g])
-        for g in range(groups + 1):
-            weight = jnp.maximum(1.0 - jnp.abs(within - (eight + 8.0 * g)), 0.0)
-            total = total + held[g] * weight
+        position = coords[site : site + 1] * (tile_rows - 1)
+        low = jnp.minimum(jnp.floor(position), tile_rows - 2.0)
+        part = position - low
+        high_tent = jnp.where(line == wide(low + 1.0, BF16), wide(part, BF16), none)
+        tents_ref[site] = jnp.where(line == wide(low, BF16), wide(1.0 - part, BF16), high_tent)
+        position = coords[SITES + site : SITES + site + 1] * (tile_cols - 1)
+        low = jnp.minimum(jnp.floor(position), tile_cols - 2.0)
+        tilt = 2.0 * (position - low) - 1.0
+        center = 2.0 * low + 1.0
+        spin_ref[site, :groups], spin_ref[site, groups:] = turned(center * (8.0 * group), 2 * tile_cols)
+        cosine, sine = turned(center * eight, 2 * tile_cols)
+        ends_ref[site, :8] = cosine
+        ends_ref[site, 8:16] = sine
+        ends_ref[site, 16:24] = tilt * sine
+        ends_ref[site, 24:32] = tilt * cosine
+        ends_ref[site, 32:] = jnp.maximum(1.0 - jnp.abs(position - edge), 0.0)
+
+
+def site_means(table_ref, slope_ref, tents_ref, spin_ref, ends_ref, middle):
+    slots = tents_ref.shape[2]
+    groups = spin_ref.shape[1] // 2
+    freqs = 8 * groups
+    none = jnp.zeros((8, slots), F32)
+    slopes = [
+        jnp.concatenate([slope_ref[8 * g : 8 * g + 8]] * (slots // slope_ref.shape[1]), axis=1)
+        for g in range(groups)
+    ]
+    total = none
+    for site in range(SITES):
+        picked = jnp.dot(table_ref[...], tents_ref[site], preferred_element_type=F32)
+        real = imag = tilted_real = tilted_imag = none
+        for g in range(groups):
+            part_real = picked[8 * g : 8 * g + 8]
+            part_imag = picked[freqs + 8 * g : freqs + 8 * g + 8]
+            cosine = jnp.broadcast_to(spin_ref[site, g : g + 1], (8, slots))
+            sine = jnp.broadcast_to(spin_ref[site, groups + g : groups + g + 1], (8, slots))
+            turn_real = part_real * cosine - part_imag * sine
+            turn_imag = part_real * sine + part_imag * cosine
+            real += turn_real
+            imag += turn_imag
+            tilted_real += slopes[g] * turn_real
+            tilted_imag += slopes[g] * turn_imag
+        total += real * ends_ref[site, :8] - imag * ends_ref[site, 8:16]
+        total -= tilted_real * ends_ref[site, 16:24] + tilted_imag * ends_ref[site, 24:32]
+        edge = picked[2 * freqs :] * ends_ref[site, 32:]
+        total += edge[:8] + edge[8:]
     mean = middle + jnp.sum(total, axis=0, keepdims=True) * (1.0 / SITES)
     return jnp.broadcast_to(mean, (8, slots))
 
 
 def resist_kernel(
-    intensity_ref, core_ref, chip_ref, inner_ref, outer_ref, operator_ref,
-    coords_ref,
-    resist_hbm, table_ref, middle_ref, mean_chip_ref,
-    resist_ref, sem,
+    intensity_ref, core_ref, chip_ref, inner_ref, outer_ref, waves_ref, slope_ref,
+    tents_ref, spin_ref, ends_ref,
+    parts_ref, table_ref, middle_ref, mean_ref,
 ):
     odd = parity()
     chip_edge = jnp.where(has_chip_side(), chip_ref[...], 0.0)
@@ -340,20 +388,34 @@
     middle = middle * (1.0 / (blurred.shape[0] * blurred.shape[1]))
     high = blurred.astype(BF16)
     low = (blurred - high.astype(F32)).astype(BF16)
-    resist = jnp.dot(
-        jnp.concatenate([high, low, high], axis=1), operator_ref[...], preferred_element_type=F32
-    )
-    resist_ref[...] = resist
+    parts = jnp.concatenate([high, low, high], axis=1)
+    parts_ref[...] = parts
+    table = transposed_dot(waves_ref[...], parts)
+    first = lax.broadcasted_iota(jnp.int32, table.shape, 0) == 0
+    table_ref[...] = jnp.where(first, table - middle, table).astype(BF16)
+    middle_ref[...] = jnp.broadcast_to(middle, middle_ref.shape)
+    mean_ref[...] = site_means(
+        table_ref, slope_ref, tents_ref, spin_ref, ends_ref, middle_ref[:1, :1]
+    )
+
+
+def core_kernel(table_ref, slope_ref, tents_ref, spin_ref, ends_ref, middle_ref, mean_ref):
+    mean_ref[...] = site_means(
+        table_ref, slope_ref, tents_ref, spin_ref, ends_ref, middle_ref[:1, :1]
+    )
+
+
+def own_kernel(
+    parts_ref, operator_ref, table_ref, slope_ref, tents_ref, spin_ref, ends_ref, middle_ref,
+    resist_hbm, mean_ref, resist_ref, sem,
+):
+    resist_ref[...] = jnp.dot(parts_ref[...], operator_ref[...], preferred_element_type=F32)
     copy = pltpu.make_async_copy(resist_ref, resist_hbm, sem)
     copy.start()
-    table_ref[...] = (resist - middle).astype(BF16)
-    middle_ref[...] = jnp.broadcast_to(middle, middle_ref.shape)
-    mean_chip_ref[...] = site_means(table_ref[...], coords_ref[...], middle_ref[:1, :1])
+    mean_ref[...] = site_means(
+        table_ref, slope_ref, tents_ref, spin_ref, ends_ref, middle_ref[:1, :1]
+    )
     copy.wait()
-
-
-def mean_kernel(table_ref, middle_ref, coords_ref, mean_ref):
-    mean_ref[...] = site_means(table_ref[...], coords_ref[...], middle_ref[:1, :1])
 
 
 def bias_kernel(level_ref, chosen_ref, own_ref, core_ref, chip_ref, steps_ref, out_ref):
@@ -434,11 +496,16 @@
     col_forward, row_blocks, row_inverse, col_inverse = imaging_tables(
         tile_rows, tile_cols, row_freqs, col_freqs
     )
-    operator, inner, outer = blur_tables(tile_rows, tile_cols, col_freqs, BLUR_REACH)
+    operator, waves, slope, inner, outer = blur_tables(tile_rows, tile_cols, col_freqs, BLUR_REACH)
     spectrum = ((2 * row_freqs, col_freqs), F32)
     packed = ((records, capacity), F32)
     edge = ((BLUR_REACH, samples), F32)
     means = ((8, capacity), F32)
+    site_shapes = [
+        ((SITES, tile_rows, capacity), BF16),
+        ((SITES, col_freqs // 4, capacity), F32),
+        ((SITES, 32 + 2 * BLUR_REACH, capacity), F32),
+    ]
     weights = kernel_weights.reshape(1, kernels)
 
     own, to_core, to_chip, packed_core, packed_chip, packed_own, chosen = call(
@@ -466,10 +533,11 @@
     coords_chip = swap_chips(packed_chip)
     coords_core = swap_cores(packed_core)
     kern = jnp.transpose(kernel_spectra, (0, 2, 1, 3))
-    level, kern, inverse, spread = call(
-        load_kernel,
-        [((8, 128), F32), (kern.shape, F32), (row_inverse.shape, BF16), (col_inverse.shape, BF16)],
-        (own, threshold, kern, row_inverse, col_inverse),
+    level, kern, inverse, spread, *own_sites = call(
+        functools.partial(load_kernel, tile_cols),
+        [((8, 128), F32), (kern.shape, F32), (row_inverse.shape, BF16), (col_inverse.shape, BF16)]
+        + site_shapes,
+        (packed_own, threshold, kern, row_inverse, col_inverse),
         smem=(1,),
         hbm=(2, 3, 4),
         scratch=[pltpu.SemaphoreType.DMA((4,))],
@@ -485,24 +553,30 @@
     )
     edge_chip = swap_chips(edge_chip)
     edge_core = swap_cores(edge_core)
-    (intensity,) = call(
-        imaging_kernel,
-        [((tile_rows, samples), BF16)],
-        (weights, product, inverse, spread),
+    intensity, *other_sites = call(
+        functools.partial(imaging_kernel, tile_cols),
+        [((tile_rows, samples), BF16)] + site_shapes * 2,
+        (weights, product, inverse, spread, coords_chip, coords_core),
         name="imaging",
     )
-    resist, table, middle, mean_chip = call(
+    chip_sites, core_sites = other_sites[:3], other_sites[3:]
+    parts, table, middle, mean_chip = call(
         resist_kernel,
-        [((tile_rows, tile_cols), F32), ((tile_rows, tile_cols), BF16), ((8, 128), F32), means],
-        (intensity, edge_core, edge_chip, inner, outer, operator, coords_chip),
+        [((tile_rows, 3 * samples), BF16), ((waves.shape[0], tile_rows), BF16), ((8, 128), F32), means],
+        (intensity, edge_core, edge_chip, inner, outer, waves, slope, *chip_sites),
+        name="resist",
+    )
+    back_chip = swap_chips(mean_chip)
+    (mean_core,) = call(core_kernel, [means], (table, slope, *core_sites, middle), name="mean_core")
+    back_core = swap_cores(mean_core)
+    resist, mean_own = call(
+        own_kernel,
+        [((tile_rows, tile_cols), F32), means],
+        (parts, operator, table, slope, *own_sites, middle),
         hbm_outs=(0,),
         scratch=[pltpu.VMEM((tile_rows, tile_cols), F32), pltpu.SemaphoreType.DMA],
-        name="resist",
-    )
-    back_chip = swap_chips(mean_chip)
-    (mean_core,) = call(mean_kernel, [means], (table, middle, coords_core), name="mean_core")
-    back_core = swap_cores(mean_core)
-    (mean_own,) = call(mean_kernel, [means], (table, middle, packed_own), name="mean_own")
+        name="mean_own",
+    )
     (new_bias,) = call(
         bias_kernel,
         [((1, frags), F32)],

time: 24.5 us -> 22.9 us (0.935)
  the two profiles are of different devices: /device:TPU:0 before, /device:TPU:13 now
where the time goes in v5:
time: 22.9 us; the launch traced here: 22.7 us
  Pallas kernels  13.9 us (61%)
  starting transfers between devices  6.81 us (30%)
  between operations  1.47 us (6%)
  waiting for transfers between devices  0.54 us (2%)
    pallas_call x8, Pallas kernels, call(): pl.pallas_call(kernel, out_shape=[jax.ShapeDtypeStruct(s, d) for s, d in...  13.9 us
    ppermute x4, starting transfers between devices, swap_chips(): return lax.ppermute(to_chip, ('groups', 'tx'), pairs)  3.62 us
    ppermute x4, starting transfers between devices, swap_cores(): lax.ppermute(to_core, 'tx', [(i, i ^ 1) for i in range(lax.axis_size('tx'...  3.19 us
    ppermute x4, waiting for transfers between devices, swap_chips(): return lax.ppermute(to_chip, ('groups', 'tx'), pairs)  0.53 us
  transfers between devices with their start and end apart: 8, of which 1 were waited for; matrix products, arithmetic and copies ran while one was open for 0% of the time, Pallas kernels for 38%

profile of v5, /device:TPU:13, one launch (start us, length us, event | category | flops | bytes accessed | tf_op | source)
XLA Modules:
  0.0 22.7 jit_solution(13327925970748890205)
XLA Ops:
  0.6 0.0 copy-start.6
  0.6 2.3 %front.1 = (f32[192,128]{1,0:T(8,128)S(1)}, f32[192,128]{1,0:T(8,128)S(1)}, f32[192,128]{1,0:T(8,128)S(1)}, f32[32,256]{1,0:T(8,128)S(1)}, f32[32,256]{1,0:T(8,1...) custom-call(s32[1,512]{1,0:T(1,128)} %bitcast.11, f32[32,512]{1,0:T(8,128)} %bitcast.10, ...), custom_call_target="tpu_custom_call" | custom-call | tf_op jit(solution)/shard_map/front/pallas_call | solution.py:474
  2.9 0.7 %collective-permute-start = (f32[192,128]{1,0:T(8,128)S(1)}, f32[192,128]{1,0:T(8,128)S(1)}, u32[]{:S(2)}, u32[]{:S(2)}) collective-permute-start(f32[192,128]{1,0:T(8,128)S(1)} %get-tuple-element.33), channel_id=1, source_target_pairs={{0,1},{1,0},{2,3},{3,2},{4,5},{5,4},{6,7},{7,6},{8,9},{9,8},{10,11... | collective-permute-start | bytes 294920 | tf_op jit(solution)/shard_map/ppermute | solution.py:460
  3.7 1.2 %collective-permute-start.1 = (f32[192,128]{1,0:T(8,128)S(1)}, f32[192,128]{1,0:T(8,128)S(1)}, u32[]{:S(2)}, u32[]{:S(2)}) collective-permute-start(f32[192,128]{1,0:T(8,128)S(1)} %get-tuple-element.34), channel_id=1, source_target_pairs={{1,2},{2,1},{3,4},{4,3},{5,6},{6,5},{7,8},{8,7},{9,10},{10,9},{11,... | collective-permute-start | bytes 294920 | tf_op jit(solution)/shard_map/ppermute | solution.py:456
  4.8 0.6 %collective-permute-start.2 = (f32[32,256]{1,0:T(8,128)S(1)}, f32[32,256]{1,0:T(8,128)S(1)}, u32[]{:S(2)}, u32[]{:S(2)}) collective-permute-start(f32[32,256]{1,0:T(8,128)S(1)} %get-tuple-element.40), channel_id=1, source_target_pairs={{1,2},{2,1},{3,4},{4,3},{5,6},{6,5},{7,8},{8,7},{9,10},{10,9},{11,... | collective-permute-start | bytes 98312 | tf_op jit(solution)/shard_map/ppermute | solution.py:456
  5.4 1.0 %collective-permute-start.3 = (f32[32,256]{1,0:T(8,128)S(1)}, f32[32,256]{1,0:T(8,128)S(1)}, u32[]{:S(2)}, u32[]{:S(2)}) collective-permute-start(f32[32,256]{1,0:T(8,128)S(1)} %get-tuple-element.41), channel_id=1, source_target_pairs={{0,1},{1,0},{2,3},{3,2},{4,5},{5,4},{6,7},{7,6},{8,9},{9,8},{10,11... | collective-permute-start | bytes 98312 | tf_op jit(solution)/shard_map/ppermute | solution.py:460
  7.0 0.0 copy-start.1
  7.1 0.0 copy-start.2
  7.1 0.0 copy-start.3
  7.1 0.0 copy-start.4
  7.1 1.5 %load.1 = (f32[8,128]{1,0:T(8,128)S(1)}, f32[2,12,96,128]{3,2,1,0:T(8,128)S(1)}, bf16[512,192]{1,0:T(8,128)(2,1)S(1)}, bf16[256,512]{1,0:T(8,128)(2,1)S(1)}, bf1...) custom-call(f32[32,256]{1,0:T(8,128)S(1)} %get-tuple-element.35.coords_ref, ...), custom_call_target="tpu_custom_call" | custom-call | tf_op jit(solution)/shard_map/load/pallas_call | solution.py:474
  8.6 0.0 collective-permute-done.core_ref
  8.6 0.5 %collective-permute-done.1.chip_ref = f32[192,128]{1,0:T(8,128)S(1)} collective-permute-done((f32[192,128]{1,0:T(8,128)S(1)}, f32[192,128]{1,0:T(8,128)S(1)}, u32[]{:S(2)}, u32[]{:S(2)}) %collective-permute-start.1) | collective-permute-done | bytes 98336 | tf_op jit(solution)/shard_map/ppermute | solution.py:456
  9.1 0.0 copy-done.6
  9.1 0.5 %edges.1 = (bf16[192,1536]{1,0:T(8,128)(2,1)S(1)}, f32[8,256]{1,0:T(8,128)S(1)}, f32[8,256]{1,0:T(8,128)S(1)}) custom-call(f32[1,12]{1,0:T(1,128)S(1)} %bitcast.7, f32[192,128]{1,0:T(8,128)S(1)} %get-tuple-element.32.own_ref, f32[192,128]{1,0:T(8,128)S(1)} %collective-permute-done.core_ref, f32[192,128]{1,0:T(8,128)S(1)} %collective-permute-done.1.chip_ref, ...), custom_call_target="tpu_custom_call" | custom-call | tf_op jit(solution)/shard_map/edges/pallas_call | solution.py:474
  9.6 0.1 collective-permute-start.4
  9.7 1.1 %collective-permute-start.5 = (f32[8,256]{1,0:T(8,128)S(1)}, f32[8,256]{1,0:T(8,128)S(1)}, u32[]{:S(2)}, u32[]{:S(2)}) collective-permute-start(f32[8,256]{1,0:T(8,128)S(1)} %get-tuple-element.44), channel_id=1, source_target_pairs={{1,2},{2,1},{3,4},{4,3},{5,6},{6,5},{7,8},{8,7},{9,10},{10,9},{11,... | collective-permute-start | bytes 24584 | tf_op jit(solution)/shard_map/ppermute | solution.py:456
  10.8 0.0 collective-permute-done.2.chip_coords_ref
  10.8 0.0 collective-permute-done.3.core_coords_ref
  10.8 3.1 %imaging.1 = (bf16[256,256]{1,0:T(8,128)(2,1)S(1)}, bf16[16,256,256]{2,1,0:T(8,128)(2,1)S(1)}, f32[16,32,256]{2,1,0:T(8,128)S(1)}, f32[16,48,256]{2,1,0:T(8,128)...) custom-call(f32[1,12]{1,0:T(1,128)S(1)} %bitcast.8, ...), custom_call_target="tpu_custom_call" | custom-call | tf_op jit(solution)/shard_map/imaging/pallas_call | solution.py:474
  13.9 0.0 collective-permute-done.4.core_ref
  13.9 0.0 collective-permute-done.5.chip_ref
  13.9 0.0 copy-done.1
  14.0 2.2 %resist.1 = (bf16[256,768]{1,0:T(8,128)(2,1)S(1)}, bf16[272,256]{1,0:T(8,128)(2,1)S(1)}, f32[8,128]{1,0:T(8,128)S(1)}, f32[8,256]{1,0:T(8,128)S(1)}) custom-call(bf16[256,256]{1,0:T(8,128)(2,1)S(1)} %get-tuple-element.42.intensity_ref, f32[8,256]{1,0:T(8,128)S(1)} %collective-permute-done.4.core_ref, f32[8,256]{1,0:T(8,128)S(1)} %collective-permute-done.5.chip_ref, ...), custom_call_target="tpu_custom_call" | custom-call | tf_op jit(solution)/shard_map/resist/pallas_call | solution.py:474
  16.1 0.0 copy-start
  16.1 0.8 %collective-permute-start.7 = (f32[8,256]{1,0:T(8,128)S(1)}, f32[8,256]{1,0:T(8,128)S(1)}, u32[]{:S(2)}, u32[]{:S(2)}) collective-permute-start(f32[8,256]{1,0:T(8,128)S(1)} %get-tuple-element.61), channel_id=1, source_target_pairs={{1,2},{2,1},{3,4},{4,3},{5,6},{6,5},{7,8},{8,7},{9,10},{10,9},{11,... | collective-permute-start | bytes 24584 | tf_op jit(solution)/shard_map/ppermute | solution.py:456
  16.9 1.5 %mean_core.1 = f32[8,256]{1,0:T(8,128)S(1)} custom-call(bf16[272,256]{1,0:T(8,128)(2,1)S(1)} %get-tuple-element.49.table_ref, f32[128,128]{1,0:T(8,128)S(1)} %copy-done.1, bf16[16,256,256]{2,1,0:T(8,128)(2,1)S(1)} %get-tuple-element.58.tents_ref, f32[16,32,256]{2,1,0:T(8,128)S(1)} %get-tuple-element.59.spin_ref, ...), custom_call_target="tpu_custom_call" | custom-call | tf_op jit(solution)/shard_map/mean_core/pallas_call | solution.py:474
  18.4 1.4 %collective-permute-start.6 = (f32[8,256]{1,0:T(8,128)S(1)}, f32[8,256]{1,0:T(8,128)S(1)}, u32[]{:S(2)}, u32[]{:S(2)}) collective-permute-start(f32[8,256]{1,0:T(8,128)S(1)} %mean_core.1), channel_id=1, source_target_pairs={{0,1},{1,0},{2,3},{3,2},{4,5},{5,4},{6,7},{7,6},{8,9},{9,8},{10,11... | collective-permute-start | bytes 24584 | tf_op jit(solution)/shard_map/ppermute | solution.py:460
  19.8 2.0 %mean_own.1 = (f32[256,1024]{1,0:T(8,128)}, f32[8,256]{1,0:T(8,128)S(1)}) custom-call(bf16[256,768]{1,0:T(8,128)(2,1)S(1)} %get-tuple-element.48.parts_ref, bf16[768,1024]{1,0:T(8,128)(2,1)S(1)} %copy-done, bf16[272,256]{1,0:T(8,128)(2,1)S(1)} %get-tuple-element.49.table_ref, f32[128,128]{1,0:T(8,128)S(1)} %copy-done.1, ...), custom_call_target="tpu_custom_call" | custom-call | tf_op jit(solution)/shard_map/mean_own/pallas_call | solution.py:474
  21.9 0.0 collective-permute-done.7.chip_ref
  21.9 0.0 collective-permute-done.6.core_ref
  21.9 0.8 %bias.1 = f32[1,512]{1,0:T(1,128)} custom-call(f32[8,128]{1,0:T(8,128)S(1)} %get-tuple-element.55.level_ref, bf16[768,512]{1,0:T(8,128)(2,1)S(1)} %get-tuple-element.56.chosen_ref, f32[8,256]{1,0:T(8,128)S(1)} %get-tuple-element.57.own_ref, f32[8,256]{1,0:T(8,128)S(1)} %collective-permute-done.6.core_ref, f32[8,256]{1,0:T(8,128)S(1)} %collective-permute-done.7.chip_ref, ...), custom_call_target="tpu_custom_call" | custom-call | tf_op jit(solution)/shard_map/bias/pallas_call | solution.py:474
  (6 shorter events, 0.0 us)
Async XLA Ops:
  0.6 8.5 %copy-start.6 = (f32[12]{0:T(128)S(1)}, f32[12]{0:T(128)}, u32[]{:S(2)}) copy-start(f32[12]{0:T(128)} %param.18) | copy-start | bytes 148
  2.9 5.7 %collective-permute-start = (f32[192,128]{1,0:T(8,128)S(1)}, f32[192,128]{1,0:T(8,128)S(1)}, u32[]{:S(2)}, u32[]{:S(2)}) collective-permute-start(f32[192,128]{1,0:T(8,128)S(1)} %get-tuple-element.33), channel_id=1, source_target_pairs={{0,1},{1,0},{2,3},{3,2},{4,5},{5,4},{6,7},{7,6},{8,9},{9,8},{10,11... | collective-permute-start | bytes 294920 | tf_op jit(solution)/shard_map/ppermute | solution.py:460
  3.7 5.4 %collective-permute-start.1 = (f32[192,128]{1,0:T(8,128)S(1)}, f32[192,128]{1,0:T(8,128)S(1)}, u32[]{:S(2)}, u32[]{:S(2)}) collective-permute-start(f32[192,128]{1,0:T(8,128)S(1)} %get-tuple-element.34), channel_id=1, source_target_pairs={{1,2},{2,1},{3,4},{4,3},{5,6},{6,5},{7,8},{8,7},{9,10},{10,9},{11,... | collective-permute-start | bytes 294920 | tf_op jit(solution)/shard_map/ppermute | solution.py:456
  4.8 6.0 %collective-permute-start.2 = (f32[32,256]{1,0:T(8,128)S(1)}, f32[32,256]{1,0:T(8,128)S(1)}, u32[]{:S(2)}, u32[]{:S(2)}) collective-permute-start(f32[32,256]{1,0:T(8,128)S(1)} %get-tuple-element.40), channel_id=1, source_target_pairs={{1,2},{2,1},{3,4},{4,3},{5,6},{6,5},{7,8},{8,7},{9,10},{10,9},{11,... | collective-permute-start | bytes 98312 | tf_op jit(solution)/shard_map/ppermute | solution.py:456
  5.4 5.4 %collective-permute-start.3 = (f32[32,256]{1,0:T(8,128)S(1)}, f32[32,256]{1,0:T(8,128)S(1)}, u32[]{:S(2)}, u32[]{:S(2)}) collective-permute-start(f32[32,256]{1,0:T(8,128)S(1)} %get-tuple-element.41), channel_id=1, source_target_pairs={{0,1},{1,0},{2,3},{3,2},{4,5},{5,4},{6,7},{7,6},{8,9},{9,8},{10,11... | collective-permute-start | bytes 98312 | tf_op jit(solution)/shard_map/ppermute | solution.py:460
  7.0 6.9 %copy-start.1 = (f32[128,128]{1,0:T(8,128)S(1)}, f32[128,128]{1,0:T(8,128)}, u32[]{:S(2)}) copy-start(f32[128,128]{1,0:T(8,128)} %constant.25.clone.slope_ref) | copy-start | bytes 196612
  7.1 6.9 %copy-start.2 = (bf16[272,768]{1,0:T(8,128)(2,1)S(1)}, bf16[272,768]{1,0:T(8,128)(2,1)}, u32[]{:S(2)}) copy-start(bf16[272,768]{1,0:T(8,128)(2,1)} %constant.24.clone.waves_ref) | copy-start | bytes 1253380
  7.1 6.9 %copy-start.3 = (bf16[256,256]{1,0:T(8,128)(2,1)S(1)}, bf16[256,256]{1,0:T(8,128)(2,1)}, u32[]{:S(2)}) copy-start(bf16[256,256]{1,0:T(8,128)(2,1)} %constant.22.clone.inner_ref) | copy-start | bytes 393220
  7.1 6.9 %copy-start.4 = (bf16[256,16]{1,0:T(8,128)(2,1)S(1)}, bf16[256,16]{1,0:T(8,128)(2,1)}, u32[]{:S(2)}) copy-start(bf16[256,16]{1,0:T(8,128)(2,1)} %constant.23.clone.outer_ref) | copy-start | bytes 24580
  9.6 4.3 %collective-permute-start.4 = (f32[8,256]{1,0:T(8,128)S(1)}, f32[8,256]{1,0:T(8,128)S(1)}, u32[]{:S(2)}, u32[]{:S(2)}) collective-permute-start(f32[8,256]{1,0:T(8,128)S(1)} %get-tuple-element.43), channel_id=1, source_target_pairs={{0,1},{1,0},{2,3},{3,2},{4,5},{5,4},{6,7},{7,6},{8,9},{9,8},{10,11... | collective-permute-start | bytes 24584 | tf_op jit(solution)/shard_map/ppermute | solution.py:460
  9.7 4.2 %collective-permute-start.5 = (f32[8,256]{1,0:T(8,128)S(1)}, f32[8,256]{1,0:T(8,128)S(1)}, u32[]{:S(2)}, u32[]{:S(2)}) collective-permute-start(f32[8,256]{1,0:T(8,128)S(1)} %get-tuple-element.44), channel_id=1, source_target_pairs={{1,2},{2,1},{3,4},{4,3},{5,6},{6,5},{7,8},{8,7},{9,10},{10,9},{11,... | collective-permute-start | bytes 24584 | tf_op jit(solution)/shard_map/ppermute | solution.py:456
  16.1 3.7 %copy-start = (bf16[768,1024]{1,0:T(8,128)(2,1)S(1)}, bf16[768,1024]{1,0:T(8,128)(2,1)}, u32[]{:S(2)}) copy-start(bf16[768,1024]{1,0:T(8,128)(2,1)} %constant.26.clone.operator_ref) | copy-start | bytes 4718596
  16.1 5.8 %collective-permute-start.7 = (f32[8,256]{1,0:T(8,128)S(1)}, f32[8,256]{1,0:T(8,128)S(1)}, u32[]{:S(2)}, u32[]{:S(2)}) collective-permute-start(f32[8,256]{1,0:T(8,128)S(1)} %get-tuple-element.61), channel_id=1, source_target_pairs={{1,2},{2,1},{3,4},{4,3},{5,6},{6,5},{7,8},{8,7},{9,10},{10,9},{11,... | collective-permute-start | bytes 24584 | tf_op jit(solution)/shard_map/ppermute | solution.py:456
  18.4 3.5 %collective-permute-start.6 = (f32[8,256]{1,0:T(8,128)S(1)}, f32[8,256]{1,0:T(8,128)S(1)}, u32[]{:S(2)}, u32[]{:S(2)}) collective-permute-start(f32[8,256]{1,0:T(8,128)S(1)} %mean_core.1), channel_id=1, source_target_pairs={{0,1},{1,0},{2,3},{3,2},{4,5},{5,4},{6,7},{7,6},{8,9},{9,8},{10,11... | collective-permute-start | bytes 24584 | tf_op jit(solution)/shard_map/ppermute | solution.py:460
  19.8 2.1 %copy-start.5 = (s32[512]{0:T(512)S(1)}, s32[512]{0:T(512)}, u32[]{:S(2)}) copy-start(s32[512]{0:T(512)} %param.22) | copy-start | bytes 6148

commit v6 on v5

--- a/solution.py
+++ b/solution.py
@@ -55,9 +55,9 @@
         centered(row_freqs), np.arange(window_rows), window_rows, 1.0 / math.sqrt(window_rows)
     )
     row_forward = rounded(np.concatenate([row_cos, -row_sin], axis=0))
-    row_blocks = np.concatenate(
-        [row_forward[:, i * tile_rows : (i + 1) * tile_rows] for i in range(3)], axis=0
-    )
+    row_blocks = [row_forward[:, i * tile_rows : (i + 1) * tile_rows] for i in range(3)]
+    side_rows = np.concatenate([row_blocks[0], row_blocks[2]], axis=0)
+    own_rows = np.ascontiguousarray(row_blocks[1])
     back_cos, back_sin = twiddle(
         np.arange(tile_rows) + HALO, centered(row_freqs), window_rows, 1.0 / math.sqrt(row_freqs)
     )
@@ -70,7 +70,7 @@
         centered(col_freqs), np.arange(samples) * step, tile_cols, 1.0 / math.sqrt(col_freqs)
     )
     col_inverse = rounded(np.block([[out_cos, out_sin], [-out_sin, out_cos]]))
-    return col_forward, row_blocks, row_inverse, col_inverse
+    return col_forward, side_rows, own_rows, row_inverse, col_inverse
 
 
 def blur_weight(offset, reach):
@@ -107,18 +107,27 @@
     gauss = rounded(gauss).astype(np.float64)
     theta = 2.0 * math.pi * freqs / tile_cols
     gain = np.cos(theta[:, None] * np.arange(-reach, reach + 1)[None, :]) @ gauss
-    gain = gain * np.where(freqs == 0, 1.0, 2.0) / samples * np.cos(theta / 2.0)
+    gain = gain * np.where(freqs == 0, 1.0, 2.0) / samples
     cosines, sines = twiddle(freqs, np.arange(samples), samples, 1.0)
+    real = (gain[:, None] * cosines).reshape(-1, 8, samples)
+    imag = (-gain[:, None] * sines).reshape(-1, 8, samples)
+    mid = col_freqs // 16
+    above, below = slice(mid + 1, None), slice(mid - 1, 0, -1)
+    paired = [
+        real[above] + real[below], imag[above] - imag[below],
+        imag[above] + imag[below], real[above] - real[below],
+        real[mid : mid + 1], imag[mid : mid + 1], real[:1], imag[:1],
+    ]
+    paired = np.concatenate(paired, axis=0).reshape(-1, samples)
     ring = np.zeros((tile_cols, tile_cols))
     for shift in range(-reach, reach + 1):
         ring[line, (line + shift) % tile_cols] = gauss[shift + reach]
     edge = np.concatenate([line[:reach], line[tile_cols - reach :]])
     cut = (spread @ (col_blur.astype(np.float64) - ring)[:, edge]).T
-    waves = np.concatenate([gain[:, None] * cosines, -gain[:, None] * sines, cut], axis=0)
+    waves = np.concatenate([paired, cut], axis=0)
     high, low = halves(waves)
     waves = np.concatenate([high, high, low], axis=1)
-    slope = np.broadcast_to(np.tan(theta / 2.0)[:, None], (col_freqs, 128)).astype(np.float32)
-    return operator, waves, np.ascontiguousarray(slope), np.ascontiguousarray(inner), np.ascontiguousarray(outer)
+    return operator, waves, np.ascontiguousarray(inner), np.ascontiguousarray(outer)
 
 
 def parity():
@@ -142,43 +151,57 @@
     return lax.dot_general(left, right, (((1,), (1,)), ((), ())), preferred_element_type=F32)
 
 
-def started(sems, first, *moves):
-    copies = []
-    for source, target, pieces in moves:
-        rows = source.shape[0] // pieces
-        for i in range(pieces):
-            part = pl.ds(i * rows, rows)
-            copies.append(
-                pltpu.make_async_copy(
-                    source.at[part], target.at[part], sems.at[first + len(copies)]
-                )
-            )
-            copies[-1].start()
+def started(sems, *moves):
+    copies = [
+        pltpu.make_async_copy(source, target, sems.at[i])
+        for i, (source, target) in enumerate(moves)
+    ]
+    for copy in copies:
+        copy.start()
     return copies
 
 
-def load_kernel(
-    cols, coords_ref, threshold_ref, kern_hbm, inverse_hbm, spread_hbm,
-    level_ref, kern_ref, inverse_ref, spread_ref, tents_ref, spin_ref, ends_ref, sems,
+def part_spectrum(product, freqs, cols):
+    real = product[:freqs, :cols] - product[freqs:, cols:]
+    imag = product[:freqs, cols:] + product[freqs:, :cols]
+    return jnp.concatenate([real, imag], axis=0)
+
+
+def front_kernel(
+    mask_hbm, forward_hbm, rows_hbm, eval_hbm, records_hbm,
+    spectra_ref, core_ref, chip_ref, eval_ref, records_ref,
+    mask_ref, forward_ref, rows_ref, sems,
 ):
+    depth = mask_ref.shape[1] // 2
+    parts = [pl.ds(i * depth, depth) for i in range(2)]
     copies = started(
-        sems, 0, (kern_hbm, kern_ref, 2), (inverse_hbm, inverse_ref, 1), (spread_hbm, spread_ref, 1)
-    )
-    level_ref[...] = jnp.full(level_ref.shape, threshold_ref[0], F32)
-    site_tables(coords_ref[...], tents_ref, spin_ref, ends_ref, cols)
-    for copy in copies:
-        copy.wait()
-
-
-def front_kernel(
-    eval_hbm, records_hbm, mask_hbm, forward_hbm, rows_hbm,
-    own_ref, core_ref, chip_ref, packed_core_ref, packed_chip_ref, packed_own_ref, chosen_ref,
-    eval_ref, records_ref, mask_ref, forward_ref, rows_ref, sems,
+        sems,
+        (mask_hbm, mask_ref),
+        (forward_hbm, forward_ref),
+        (rows_hbm, rows_ref),
+        (eval_hbm, eval_ref),
+        (records_hbm, records_ref),
+    )
+    copies[0].wait()
+    copies[1].wait()
+    spectra = jnp.dot(mask_ref[...], forward_ref[...], preferred_element_type=F32).astype(BF16)
+    spectra_ref[...] = spectra
+    copies[2].wait()
+    product = jnp.dot(rows_ref[...], spectra, preferred_element_type=F32)
+    freqs, cols = core_ref.shape[0] // 2, core_ref.shape[1]
+    upper_side = part_spectrum(product[: 2 * freqs], freqs, cols)
+    lower_side = part_spectrum(product[2 * freqs :], freqs, cols)
+    odd = parity()
+    chip_ref[...] = jnp.where(odd == 1, upper_side, lower_side)
+    core_ref[...] = jnp.where(odd == 1, lower_side, upper_side)
+    copies[3].wait()
+    copies[4].wait()
+
+
+def pack_kernel(
+    after_ref, eval_ref, records_ref, packed_core_ref, packed_chip_ref, packed_own_ref, places_ref,
+    chosen_ref,
 ):
-    small = started(sems, 0, (eval_hbm, eval_ref, 1), (records_hbm, records_ref, 1))
-    large = started(
-        sems, 2, (mask_hbm, mask_ref, 2), (forward_hbm, forward_ref, 2), (rows_hbm, rows_ref, 1)
-    )
     me = lax.axis_index("tx")
     odd = parity()
     frags = eval_ref.shape[1]
@@ -188,14 +211,17 @@
     after = lax.broadcasted_iota(jnp.int32, (frags, frags), 1)
     upper = (before <= after).astype(F32).astype(BF16)
     slots = lax.broadcasted_iota(jnp.int32, (capacity, frags), 0).astype(F32).astype(BF16)
-    for copy in small:
-        copy.wait()
     member = lax.broadcasted_iota(jnp.int32, (8, frags), 0) == eval_ref[...] - me + 1
     counts = jnp.dot(member.astype(F32).astype(BF16), upper, preferred_element_type=F32)
     code = jnp.where(member, counts - 1.0, -1.0)
+    side = lax.broadcasted_iota(jnp.int32, (8, frags), 0) * capacity
+    place = jnp.where(member, side + counts.astype(jnp.int32) - 1, 0)
+    places_ref[...] = jnp.sum(place, axis=0, keepdims=True)
     for side in range(3):
         row = jnp.broadcast_to(code[side : side + 1].astype(BF16), (capacity, frags))
-        chosen_ref[pl.ds(side * capacity, capacity)] = jnp.where(slots == row, jnp.ones_like(slots), jnp.zeros_like(slots))
+        chosen_ref[pl.ds(side * capacity, capacity)] = jnp.where(
+            slots == row, jnp.ones_like(slots), jnp.zeros_like(slots)
+        )
     pieces = jnp.concatenate(three_parts(records_ref[...]), axis=0)
 
     def packed(side, out_ref):
@@ -207,22 +233,22 @@
     packed(2 * odd, packed_chip_ref)
     packed(1, packed_own_ref)
 
-    for copy in large:
-        copy.wait()
-    col_spectra = jnp.dot(mask_ref[...], forward_ref[...], preferred_element_type=F32).astype(BF16)
-    product = jnp.dot(rows_ref[...], col_spectra, preferred_element_type=F32)
-    freqs, cols = own_ref.shape[0] // 2, own_ref.shape[1]
-
-    def partial(block):
-        part = product[2 * freqs * block : 2 * freqs * (block + 1)]
-        real = part[:freqs, :cols] - part[freqs:, cols:]
-        imag = part[:freqs, cols:] + part[freqs:, :cols]
-        return jnp.concatenate([real, imag], axis=0)
-
-    upper_side, own, lower_side = partial(0), partial(1), partial(2)
-    chip_ref[...] = jnp.where(odd == 1, upper_side, lower_side)
-    core_ref[...] = jnp.where(odd == 1, lower_side, upper_side)
-    own_ref[...] = own
+
+def load_kernel(
+    cols, spectra_ref, coords_ref, threshold_ref, rows_hbm, inverse_hbm, spread_hbm,
+    level_ref, own_ref, inverse_ref, spread_ref, tents_ref, spin_ref, ends_ref,
+    rows_ref, sems,
+):
+    copies = started(
+        sems, (rows_hbm, rows_ref), (inverse_hbm, inverse_ref), (spread_hbm, spread_ref)
+    )
+    level_ref[...] = jnp.full(level_ref.shape, threshold_ref[0], F32)
+    site_tables(coords_ref[...], tents_ref, spin_ref, ends_ref, cols)
+    copies[0].wait()
+    product = jnp.dot(rows_ref[...], spectra_ref[...], preferred_element_type=F32)
+    own_ref[...] = part_spectrum(product, own_ref.shape[0] // 2, own_ref.shape[1])
+    copies[1].wait()
+    copies[2].wait()
 
 
 def stacked_pairs(half, rows, kernels, cols):
@@ -271,11 +297,15 @@
     edge_chip_ref[...] = jnp.where(odd == 1, bottom, top)
 
 
-def imaging_kernel(
-    tile_cols, weights_ref, product_ref, inverse_ref, spread_ref, chip_coords_ref, core_coords_ref,
-    intensity_ref, chip_tents_ref, chip_spin_ref, chip_ends_ref,
-    core_tents_ref, core_spin_ref, core_ends_ref,
+def prepare_kernel(
+    tile_cols, chip_coords_ref, core_coords_ref,
+    chip_tents_ref, chip_spin_ref, chip_ends_ref, core_tents_ref, core_spin_ref, core_ends_ref,
 ):
+    site_tables(chip_coords_ref[...], chip_tents_ref, chip_spin_ref, chip_ends_ref, tile_cols)
+    site_tables(core_coords_ref[...], core_tents_ref, core_spin_ref, core_ends_ref, tile_cols)
+
+
+def imaging_kernel(weights_ref, product_ref, inverse_ref, spread_ref, intensity_ref):
     rows, samples = intensity_ref.shape
     cols = samples // 2
     kernels = product_ref.shape[1] // cols
@@ -289,13 +319,11 @@
         real, imag = field[:, :samples], field[:, samples:]
         total = total + weights_ref[:, k : k + 1] * (real * real + imag * imag)
     intensity_ref[...] = total.astype(BF16)
-    site_tables(chip_coords_ref[...], chip_tents_ref, chip_spin_ref, chip_ends_ref, tile_cols)
-    site_tables(core_coords_ref[...], core_tents_ref, core_spin_ref, core_ends_ref, tile_cols)
 
 
 def turned(index, period):
     turns = index * (1.0 / period)
-    part = 2.0 * (turns - jnp.round(turns))
+    part = 2.0 * (turns - jnp.floor(turns + 0.5))
     square = part * part
     sine = SINE[-1]
     for term in SINE[-2::-1]:
@@ -309,9 +337,10 @@
 
 def site_tables(coords, tents_ref, spin_ref, ends_ref, tile_cols):
     tile_rows, slots = tents_ref.shape[1:]
-    groups = spin_ref.shape[1] // 2
     eight = lax.broadcasted_iota(jnp.int32, (8, slots), 0).astype(F32)
-    group = lax.broadcasted_iota(jnp.int32, (groups, slots), 0).astype(F32)
+    count = spin_ref.shape[1] // 4
+    steps = jnp.concatenate([8.0 * eight + 8.0, eight + 8.0 * count], axis=0)
+    one_cosine, one_sine = turned(steps, tile_cols)
     line = lax.broadcasted_iota(jnp.int32, (tile_rows, slots), 0).astype(F32).astype(BF16)
     none = jnp.zeros((tile_rows, slots), BF16)
     edge = lax.broadcasted_iota(jnp.int32, (2 * BLUR_REACH, slots), 0).astype(F32)
@@ -328,51 +357,53 @@
         tents_ref[site] = jnp.where(line == wide(low, BF16), wide(1.0 - part, BF16), high_tent)
         position = coords[SITES + site : SITES + site + 1] * (tile_cols - 1)
         low = jnp.minimum(jnp.floor(position), tile_cols - 2.0)
-        tilt = 2.0 * (position - low) - 1.0
-        center = 2.0 * low + 1.0
-        spin_ref[site, :groups], spin_ref[site, groups:] = turned(center * (8.0 * group), 2 * tile_cols)
-        cosine, sine = turned(center * eight, 2 * tile_cols)
-        ends_ref[site, :8] = cosine
-        ends_ref[site, 8:16] = sine
-        ends_ref[site, 16:24] = tilt * sine
-        ends_ref[site, 24:32] = tilt * cosine
+        part = position - low
+        cosine, sine = turned(low * steps, tile_cols)
+        next_cosine = cosine * one_cosine - sine * one_sine
+        next_sine = sine * one_cosine + cosine * one_sine
+        spin_ref[site, :8] = cosine[:8]
+        spin_ref[site, 8:16] = sine[:8]
+        spin_ref[site, 16:24] = next_cosine[:8]
+        spin_ref[site, 24:] = next_sine[:8]
+        ends_ref[site, :8] = (1.0 - part) * cosine[8:]
+        ends_ref[site, 8:16] = (1.0 - part) * sine[8:]
+        ends_ref[site, 16:24] = part * next_cosine[8:]
+        ends_ref[site, 24:32] = part * next_sine[8:]
         ends_ref[site, 32:] = jnp.maximum(1.0 - jnp.abs(position - edge), 0.0)
 
 
-def site_means(table_ref, slope_ref, tents_ref, spin_ref, ends_ref, middle):
+def site_means(table_ref, tents_ref, spin_ref, ends_ref, middle):
     slots = tents_ref.shape[2]
-    groups = spin_ref.shape[1] // 2
-    freqs = 8 * groups
+    count = spin_ref.shape[1] // 4
+    pairs = count - 1
     none = jnp.zeros((8, slots), F32)
-    slopes = [
-        jnp.concatenate([slope_ref[8 * g : 8 * g + 8]] * (slots // slope_ref.shape[1]), axis=1)
-        for g in range(groups)
-    ]
     total = none
     for site in range(SITES):
         picked = jnp.dot(table_ref[...], tents_ref[site], preferred_element_type=F32)
-        real = imag = tilted_real = tilted_imag = none
-        for g in range(groups):
-            part_real = picked[8 * g : 8 * g + 8]
-            part_imag = picked[freqs + 8 * g : freqs + 8 * g + 8]
-            cosine = jnp.broadcast_to(spin_ref[site, g : g + 1], (8, slots))
-            sine = jnp.broadcast_to(spin_ref[site, groups + g : groups + g + 1], (8, slots))
-            turn_real = part_real * cosine - part_imag * sine
-            turn_imag = part_real * sine + part_imag * cosine
-            real += turn_real
-            imag += turn_imag
-            tilted_real += slopes[g] * turn_real
-            tilted_imag += slopes[g] * turn_imag
-        total += real * ends_ref[site, :8] - imag * ends_ref[site, 8:16]
-        total -= tilted_real * ends_ref[site, 16:24] + tilted_imag * ends_ref[site, 24:32]
-        edge = picked[2 * freqs :] * ends_ref[site, 32:]
-        total += edge[:8] + edge[8:]
+        rows = [picked[8 * i : 8 * i + 8] for i in range(4 * pairs + 6)]
+
+        def spin(i):
+            return jnp.broadcast_to(spin_ref[site, i : i + 1], (8, slots))
+
+        for side in range(2):
+            first = 2 * count * side
+            cosine, sine = spin(first + pairs), spin(first + count + pairs)
+            low_real, low_imag = rows[4 * pairs + 2], rows[4 * pairs + 3]
+            real = rows[4 * pairs] + low_real * cosine + low_imag * sine
+            imag = rows[4 * pairs + 1] + low_imag * cosine - low_real * sine
+            for k in range(pairs):
+                cosine, sine = spin(first + k), spin(first + count + k)
+                real += rows[k] * cosine - rows[pairs + k] * sine
+                imag += rows[2 * pairs + k] * cosine + rows[3 * pairs + k] * sine
+            total += real * ends_ref[site, 16 * side : 16 * side + 8]
+            total -= imag * ends_ref[site, 16 * side + 8 : 16 * side + 16]
+        total += rows[4 * pairs + 4] * ends_ref[site, 32:40] + rows[4 * pairs + 5] * ends_ref[site, 40:]
     mean = middle + jnp.sum(total, axis=0, keepdims=True) * (1.0 / SITES)
     return jnp.broadcast_to(mean, (8, slots))
 
 
 def resist_kernel(
-    intensity_ref, core_ref, chip_ref, inner_ref, outer_ref, waves_ref, slope_ref,
+    intensity_ref, core_ref, chip_ref, inner_ref, outer_ref, waves_ref,
     tents_ref, spin_ref, ends_ref,
     parts_ref, table_ref, middle_ref, mean_ref,
 ):
@@ -391,45 +422,48 @@
     parts = jnp.concatenate([high, low, high], axis=1)
     parts_ref[...] = parts
     table = transposed_dot(waves_ref[...], parts)
-    first = lax.broadcasted_iota(jnp.int32, table.shape, 0) == 0
+    lowest = table.shape[0] - 2 * BLUR_REACH - 16
+    first = lax.broadcasted_iota(jnp.int32, table.shape, 0) == lowest
     table_ref[...] = jnp.where(first, table - middle, table).astype(BF16)
     middle_ref[...] = jnp.broadcast_to(middle, middle_ref.shape)
     mean_ref[...] = site_means(
-        table_ref, slope_ref, tents_ref, spin_ref, ends_ref, middle_ref[:1, :1]
-    )
-
-
-def core_kernel(table_ref, slope_ref, tents_ref, spin_ref, ends_ref, middle_ref, mean_ref):
+        table_ref, tents_ref, spin_ref, ends_ref, middle_ref[:1, :1]
+    )
+
+
+def core_kernel(table_ref, tents_ref, spin_ref, ends_ref, middle_ref, mean_ref):
     mean_ref[...] = site_means(
-        table_ref, slope_ref, tents_ref, spin_ref, ends_ref, middle_ref[:1, :1]
+        table_ref, tents_ref, spin_ref, ends_ref, middle_ref[:1, :1]
     )
 
 
 def own_kernel(
-    parts_ref, operator_ref, table_ref, slope_ref, tents_ref, spin_ref, ends_ref, middle_ref,
+    parts_ref, operator_ref, table_ref, tents_ref, spin_ref, ends_ref, middle_ref,
     resist_hbm, mean_ref, resist_ref, sem,
 ):
     resist_ref[...] = jnp.dot(parts_ref[...], operator_ref[...], preferred_element_type=F32)
     copy = pltpu.make_async_copy(resist_ref, resist_hbm, sem)
     copy.start()
     mean_ref[...] = site_means(
-        table_ref, slope_ref, tents_ref, spin_ref, ends_ref, middle_ref[:1, :1]
+        table_ref, tents_ref, spin_ref, ends_ref, middle_ref[:1, :1]
     )
     copy.wait()
 
 
-def bias_kernel(level_ref, chosen_ref, own_ref, core_ref, chip_ref, steps_ref, out_ref):
+def bias_kernel(level_ref, places_ref, own_ref, core_ref, chip_ref, steps_ref, out_ref):
     odd = parity() == 1
     core, chip = core_ref[...], chip_ref[...]
-    means = jnp.concatenate(
-        [jnp.where(odd, core, chip), own_ref[...], jnp.where(odd, chip, core)], axis=1
-    )
-    lines = lax.broadcasted_iota(jnp.int32, means.shape, 0)
-    first, second, third = (part.astype(F32) for part in three_parts(means))
-    parts = jnp.where(lines == 0, first, jnp.where(lines == 1, second, third))
-    parts = jnp.where(lines < 3, parts, 0.0).astype(BF16)
-    found = jnp.dot(parts, chosen_ref[...], preferred_element_type=F32)
-    site_mean = jnp.sum(found, axis=0, keepdims=True)
+    means = (jnp.where(odd, core, chip), own_ref[...], jnp.where(odd, chip, core))
+    means = [part[:, i : i + 128] for part in means for i in range(0, part.shape[1], 128)]
+    found = []
+    for start in range(0, out_ref.shape[1], 128):
+        place = jnp.broadcast_to(places_ref[:, start : start + 128], (8, 128))
+        tile, lane = place // 128, place % 128
+        site_mean = jnp.zeros((8, 128), F32)
+        for i, part in enumerate(means):
+            site_mean = jnp.where(tile == i, jnp.take_along_axis(part, lane, axis=1), site_mean)
+        found.append(site_mean[:1])
+    site_mean = jnp.concatenate(found, axis=1)
     out_ref[...] = bias_step * steps_ref[...].astype(F32) - bias_gain * (
         site_mean - level_ref[:1, :1]
     )
@@ -493,10 +527,10 @@
     samples = 2 * col_freqs
     flat = kernels * col_freqs
     records = 2 * SITES
-    col_forward, row_blocks, row_inverse, col_inverse = imaging_tables(
+    col_forward, side_rows, own_rows, row_inverse, col_inverse = imaging_tables(
         tile_rows, tile_cols, row_freqs, col_freqs
     )
-    operator, waves, slope, inner, outer = blur_tables(tile_rows, tile_cols, col_freqs, BLUR_REACH)
+    operator, waves, inner, outer = blur_tables(tile_rows, tile_cols, col_freqs, BLUR_REACH)
     spectrum = ((2 * row_freqs, col_freqs), F32)
     packed = ((records, capacity), F32)
     edge = ((BLUR_REACH, samples), F32)
@@ -508,41 +542,45 @@
     ]
     weights = kernel_weights.reshape(1, kernels)
 
-    own, to_core, to_chip, packed_core, packed_chip, packed_own, chosen = call(
+    spectra, to_core, to_chip, targets, coords = call(
         front_kernel,
-        [spectrum] * 3
-        + [packed] * 3
-        + [((3 * capacity, frags), BF16)],
+        [((tile_rows, 2 * col_freqs), BF16), spectrum, spectrum]
+        + [((1, frags), jnp.int32), ((records, frags), F32)],
         (
+            mask, col_forward, side_rows,
             eval_tile.reshape(1, frags), site_coords.reshape(records, frags),
-            mask, col_forward, row_blocks,
         ),
         hbm=range(5),
         scratch=[
-            pltpu.VMEM((1, frags), jnp.int32),
-            pltpu.VMEM((records, frags), F32),
             pltpu.VMEM(mask.shape, BF16),
             pltpu.VMEM(col_forward.shape, BF16),
-            pltpu.VMEM(row_blocks.shape, BF16),
-            pltpu.SemaphoreType.DMA((7,)),
+            pltpu.VMEM(side_rows.shape, BF16),
+            pltpu.SemaphoreType.DMA((5,)),
         ],
         name="front",
     )
     got_chip = swap_chips(to_chip)
     got_core = swap_cores(to_core)
+    packed_core, packed_chip, packed_own, places = call(
+        pack_kernel,
+        [packed] * 3 + [((1, frags), jnp.int32)],
+        (spectra, targets, coords),
+        scratch=[pltpu.VMEM((3 * capacity, frags), BF16)],
+        name="pack",
+    )
     coords_chip = swap_chips(packed_chip)
     coords_core = swap_cores(packed_core)
+    level, own, inverse, spread, *own_sites = call(
+        functools.partial(load_kernel, tile_cols),
+        [((8, 128), F32), spectrum, (row_inverse.shape, BF16), (col_inverse.shape, BF16)]
+        + site_shapes,
+        (spectra, packed_own, threshold, own_rows, row_inverse, col_inverse),
+        smem=(2,),
+        hbm=(3, 4, 5),
+        scratch=[pltpu.VMEM(own_rows.shape, BF16), pltpu.SemaphoreType.DMA((3,))],
+        name="load",
+    )
     kern = jnp.transpose(kernel_spectra, (0, 2, 1, 3))
-    level, kern, inverse, spread, *own_sites = call(
-        functools.partial(load_kernel, tile_cols),
-        [((8, 128), F32), (kern.shape, F32), (row_inverse.shape, BF16), (col_inverse.shape, BF16)]
-        + site_shapes,
-        (packed_own, threshold, kern, row_inverse, col_inverse),
-        smem=(1,),
-        hbm=(2, 3, 4),
-        scratch=[pltpu.SemaphoreType.DMA((4,))],
-        name="load",
-    )
     product, edge_core, edge_chip = call(
         edge_kernel,
         [((2 * row_freqs, flat), BF16), edge, edge],
@@ -553,26 +591,32 @@
     )
     edge_chip = swap_chips(edge_chip)
     edge_core = swap_cores(edge_core)
-    intensity, *other_sites = call(
-        functools.partial(imaging_kernel, tile_cols),
-        [((tile_rows, samples), BF16)] + site_shapes * 2,
-        (weights, product, inverse, spread, coords_chip, coords_core),
+    (intensity,) = call(
+        imaging_kernel,
+        [((tile_rows, samples), BF16)],
+        (weights, product, inverse, spread),
         name="imaging",
+    )
+    other_sites = call(
+        functools.partial(prepare_kernel, tile_cols),
+        site_shapes * 2,
+        (coords_chip, coords_core),
+        name="prepare",
     )
     chip_sites, core_sites = other_sites[:3], other_sites[3:]
     parts, table, middle, mean_chip = call(
         resist_kernel,
         [((tile_rows, 3 * samples), BF16), ((waves.shape[0], tile_rows), BF16), ((8, 128), F32), means],
-        (intensity, edge_core, edge_chip, inner, outer, waves, slope, *chip_sites),
+        (intensity, edge_core, edge_chip, inner, outer, waves, *chip_sites),
         name="resist",
     )
     back_chip = swap_chips(mean_chip)
-    (mean_core,) = call(core_kernel, [means], (table, slope, *core_sites, middle), name="mean_core")
+    (mean_core,) = call(core_kernel, [means], (table, *core_sites, middle), name="mean_core")
     back_core = swap_cores(mean_core)
     resist, mean_own = call(
         own_kernel,
         [((tile_rows, tile_cols), F32), means],
-        (parts, operator, table, slope, *own_sites, middle),
+        (parts, operator, table, *own_sites, middle),
         hbm_outs=(0,),
         scratch=[pltpu.VMEM((tile_rows, tile_cols), F32), pltpu.SemaphoreType.DMA],
         name="mean_own",
@@ -580,7 +624,7 @@
     (new_bias,) = call(
         bias_kernel,
         [((1, frags), F32)],
-        (level, chosen, mean_own, back_core, back_chip, bias_steps.reshape(1, frags)),
+        (level, places, mean_own, back_core, back_chip, bias_steps.reshape(1, frags)),
         name="bias",
     )
     return resist, new_bias.reshape(frags)

time: 22.9 us -> 21.7 us (0.948)
  the two profiles are of different devices: /device:TPU:13 before, /device:TPU:0 now
where the time goes in v6:
time: 21.7 us; the launch traced here: 21.3 us
  Pallas kernels  13.1 us (60%)
  starting transfers between devices  6.67 us (31%)
  between operations  1.48 us (7%)
    pallas_call x10, Pallas kernels, call(): pl.pallas_call(kernel, out_shape=[jax.ShapeDtypeStruct(s, d) for s, d in...  13.1 us
    ppermute x4, starting transfers between devices, swap_chips(): return lax.ppermute(to_chip, ('groups', 'tx'), pairs)  5.32 us
    ppermute x4, starting transfers between devices, swap_cores(): lax.ppermute(to_core, 'tx', [(i, i ^ 1) for i in range(lax.axis_size('tx'...  1.35 us
  transfers between devices with their start and end apart: 8, of which 0 were waited for; matrix products, arithmetic and copies ran while one was open for 0% of the time, Pallas kernels for 40%

profile of v6, /device:TPU:0, one launch (start us, length us, event | category | flops | bytes accessed | tf_op | source)
XLA Modules:
  0.0 21.3 jit_solution(4258837869308073882)
XLA Ops:
  0.7 2.0 %front.1 = (bf16[256,256]{1,0:T(8,128)(2,1)S(1)}, f32[192,128]{1,0:T(8,128)S(1)}, f32[192,128]{1,0:T(8,128)S(1)}, s32[1,512]{1,0:T(1,128)S(1)}, f32[32,512]{1,0:T(8,128)S(1)}) custom-call(bf16[256,1024]{1,0:T(8,128)(2,1)} %mask_hbm.1, bf16[1024,256]{1,0:T(8,128)(2,1)} %constant.18.clone.forward_hbm, bf16[384,256]{1,0:T(8,128)(2,1)} %constant.19.clone.rows_hbm, ...), custom_call_target="tpu_custom_call" | custom-call | tf_op jit(solution)/shard_map/front/pallas_call | solution.py:508
  2.6 0.5 %collective-permute-start = (f32[192,128]{1,0:T(8,128)S(1)}, f32[192,128]{1,0:T(8,128)S(1)}, u32[]{:S(2)}, u32[]{:S(2)}) collective-permute-start(f32[192,128]{1,0:T(8,128)S(1)} %get-tuple-element.38), channel_id=1, source_target_pairs={{0,1},{1,0},{2,3},{3,2},{4,5},{5,4},{6,7},{7,6},{8,9},{9,8},{10,11... | collective-permute-start | bytes 294920 | tf_op jit(solution)/shard_map/ppermute | solution.py:494
  3.1 2.6 %collective-permute-start.1 = (f32[192,128]{1,0:T(8,128)S(1)}, f32[192,128]{1,0:T(8,128)S(1)}, u32[]{:S(2)}, u32[]{:S(2)}) collective-permute-start(f32[192,128]{1,0:T(8,128)S(1)} %get-tuple-element.39), channel_id=1, source_target_pairs={{1,2},{2,1},{3,4},{4,3},{5,6},{6,5},{7,8},{8,7},{9,10},{10,9},{11,... | collective-permute-start | bytes 294920 | tf_op jit(solution)/shard_map/ppermute | solution.py:490
  5.7 0.6 %pack.1 = (f32[32,256]{1,0:T(8,128)S(1)}, f32[32,256]{1,0:T(8,128)S(1)}, f32[32,256]{1,0:T(8,128)S(1)}, s32[1,512]{1,0:T(1,128)S(1)}) custom-call(bf16[256,256]{1,0:T(8,128)(2,1)S(1)} %get-tuple-element.33.after_ref.spectra_ref, s32[1,512]{1,0:T(1,128)S(1)} %get-tuple-element.34.eval_ref, f32[32,512]{1,0:T(8,128)S(1)} %get-tuple-element.35.records_ref), custom_call_target="tpu_custom_call" | custom-call | tf_op jit(solution)/shard_map/pack/pallas_call | solution.py:508
  6.3 0.0 copy-start.2
  6.3 0.0 copy-start.3
  6.4 0.0 copy-start.4
  6.4 0.1 collective-permute-start.4
  6.5 0.1 collective-permute-start.5
  7.3 1.1 %load.1 = (f32[8,128]{1,0:T(8,128)S(1)}, f32[192,128]{1,0:T(8,128)S(1)}, bf16[512,192]{1,0:T(8,128)(2,1)S(1)}, bf16[256,512]{1,0:T(8,128)(2,1)S(1)}, bf16[16,256...) custom-call(bf16[256,256]{1,0:T(8,128)(2,1)S(1)} %get-tuple-element.33.after_ref.spectra_ref, ...), custom_call_target="tpu_custom_call" | custom-call | tf_op jit(solution)/shard_map/load/pallas_call | solution.py:508
  8.4 0.0 collective-permute-done.core_ref
  8.4 0.0 collective-permute-done.1.chip_ref
  8.4 0.5 %edges.1 = (bf16[192,1536]{1,0:T(8,128)(2,1)S(1)}, f32[8,256]{1,0:T(8,128)S(1)}, f32[8,256]{1,0:T(8,128)S(1)}) custom-call(f32[1,12]{1,0:T(1,128)S(1)} %bitcast.7, f32[192,128]{1,0:T(8,128)S(1)} %get-tuple-element.37.own_ref, f32[192,128]{1,0:T(8,128)S(1)} %collective-permute-done.core_ref, f32[192,128]{1,0:T(8,128)S(1)} %collective-permute-done.1.chip_ref, ...), custom_call_target="tpu_custom_call" | custom-call | tf_op jit(solution)/shard_map/edges/pallas_call | solution.py:508
  9.0 0.5 %collective-permute-start.2 = (f32[8,256]{1,0:T(8,128)S(1)}, f32[8,256]{1,0:T(8,128)S(1)}, u32[]{:S(2)}, u32[]{:S(2)}) collective-permute-start(f32[8,256]{1,0:T(8,128)S(1)} %get-tuple-element.43), channel_id=1, source_target_pairs={{0,1},{1,0},{2,3},{3,2},{4,5},{5,4},{6,7},{7,6},{8,9},{9,8},{10,11... | collective-permute-start | bytes 24584 | tf_op jit(solution)/shard_map/ppermute | solution.py:494
  9.4 1.9 %collective-permute-start.3 = (f32[8,256]{1,0:T(8,128)S(1)}, f32[8,256]{1,0:T(8,128)S(1)}, u32[]{:S(2)}, u32[]{:S(2)}) collective-permute-start(f32[8,256]{1,0:T(8,128)S(1)} %get-tuple-element.44), channel_id=1, source_target_pairs={{1,2},{2,1},{3,4},{4,3},{5,6},{6,5},{7,8},{8,7},{9,10},{10,9},{11,... | collective-permute-start | bytes 24584 | tf_op jit(solution)/shard_map/ppermute | solution.py:490
  11.4 0.0 collective-permute-done.4.chip_coords_ref
  11.4 0.0 collective-permute-done.5.core_coords_ref
  11.4 1.6 %prepare.1 = (bf16[16,256,256]{2,1,0:T(8,128)(2,1)S(1)}, f32[16,32,256]{2,1,0:T(8,128)S(1)}, f32[16,48,256]{2,1,0:T(8,128)S(1)}, bf16[16,256,256]{2,1,0:T(8,128)...) custom-call(f32[32,256]{1,0:T(8,128)S(1)} %collective-permute-done.4.chip_coords_ref, ...), custom_call_target="tpu_custom_call" | custom-call | tf_op jit(solution)/shard_map/prepare/pallas_call | solution.py:508
  13.0 1.4 %imaging.1.intensity_ref = bf16[256,256]{1,0:T(8,128)(2,1)S(1)} custom-call(f32[1,12]{1,0:T(1,128)S(1)} %bitcast.8, bf16[192,1536]{1,0:T(8,128)(2,1)S(1)} %get-tuple-element.42.product_ref, bf16[512,192]{1,0:T(8,128)(2,1)S(1)} %get-tuple-element.40.inverse_ref, bf16[256,512]{1,0:T(8,128)(2,1)S(1)} %get-tuple-element.41.spread_ref), custom_call_target="tpu_custom_call" | custom-call | tf_op jit(solution)/shard_map/imaging/pallas_call | solution.py:508
  14.4 0.0 collective-permute-done.2.core_ref
  14.4 0.0 collective-permute-done.3.chip_ref
  14.4 0.0 copy-done.2
  14.4 0.0 copy-done.3
  14.4 1.9 %resist.1 = (bf16[256,768]{1,0:T(8,128)(2,1)S(1)}, bf16[272,256]{1,0:T(8,128)(2,1)S(1)}, f32[8,128]{1,0:T(8,128)S(1)}, f32[8,256]{1,0:T(8,128)S(1)}) custom-call(bf16[256,256]{1,0:T(8,128)(2,1)S(1)} %imaging.1.intensity_ref, f32[8,256]{1,0:T(8,128)S(1)} %collective-permute-done.2.core_ref, f32[8,256]{1,0:T(8,128)S(1)} %collective-permute-done.3.chip_ref, ...), custom_call_target="tpu_custom_call" | custom-call | tf_op jit(solution)/shard_map/resist/pallas_call | solution.py:508
  16.3 0.0 copy-start
  16.3 0.7 %collective-permute-start.7 = (f32[8,256]{1,0:T(8,128)S(1)}, f32[8,256]{1,0:T(8,128)S(1)}, u32[]{:S(2)}, u32[]{:S(2)}) collective-permute-start(f32[8,256]{1,0:T(8,128)S(1)} %get-tuple-element.63), channel_id=1, source_target_pairs={{1,2},{2,1},{3,4},{4,3},{5,6},{6,5},{7,8},{8,7},{9,10},{10,9},{11,... | collective-permute-start | bytes 24584 | tf_op jit(solution)/shard_map/ppermute | solution.py:490
  17.0 1.5 %mean_core.1 = f32[8,256]{1,0:T(8,128)S(1)} custom-call(bf16[272,256]{1,0:T(8,128)(2,1)S(1)} %get-tuple-element.51.table_ref, bf16[16,256,256]{2,1,0:T(8,128)(2,1)S(1)} %get-tuple-element.60.tents_ref, f32[16,32,256]{2,1,0:T(8,128)S(1)} %get-tuple-element.61.spin_ref, f32[16,48,256]{2,1,0:T(8,128)S(1)} %get-tuple-element.62.ends_ref, ...), custom_call_target="tpu_custom_call" | custom-call | tf_op jit(solution)/shard_map/mean_core/pallas_call | solution.py:508
  18.5 0.2 collective-permute-start.6
  18.7 1.8 %mean_own.1 = (f32[256,1024]{1,0:T(8,128)}, f32[8,256]{1,0:T(8,128)S(1)}) custom-call(bf16[256,768]{1,0:T(8,128)(2,1)S(1)} %get-tuple-element.50.parts_ref, bf16[768,1024]{1,0:T(8,128)(2,1)S(1)} %copy-done, bf16[272,256]{1,0:T(8,128)(2,1)S(1)} %get-tuple-element.51.table_ref, bf16[16,256,256]{2,1,0:T(8,128)(2,1)S(1)} %get-tuple-element.52.tents_ref, ...), custom_call_target="tpu_custom_call" | custom-call | tf_op jit(solution)/shard_map/mean_own/pallas_call | solution.py:508
  20.6 0.0 collective-permute-done.7.chip_ref
  20.6 0.0 collective-permute-done.6.core_ref
  20.6 0.7 %bias.1 = f32[1,512]{1,0:T(1,128)} custom-call(f32[8,128]{1,0:T(8,128)S(1)} %get-tuple-element.57.level_ref, s32[1,512]{1,0:T(1,128)S(1)} %get-tuple-element.58.places_ref, f32[8,256]{1,0:T(8,128)S(1)} %get-tuple-element.59.own_ref, f32[8,256]{1,0:T(8,128)S(1)} %collective-permute-done.6.core_ref, f32[8,256]{1,0:T(8,128)S(1)} %collective-permute-done.7.chip_ref, ...), custom_call_target="tpu_custom_call" | custom-call | tf_op jit(solution)/shard_map/bias/pallas_call | solution.py:508
  (8 shorter events, 0.0 us)
Async XLA Ops:
  0.6 7.8 %copy-start.5 = (f32[12]{0:T(128)S(1)}, f32[12]{0:T(128)}, u32[]{:S(2)}) copy-start(f32[12]{0:T(128)} %param.18) | copy-start | bytes 148
  0.6 7.8 %copy-start.1 = (f32[2,96,12,128]{3,1,2,0:T(8,128)S(1)}, f32[2,96,12,128]{3,1,2,0:T(8,128)}, u32[]{:S(2)}) copy-start(f32[2,96,12,128]{3,1,2,0:T(8,128)} %param.17) | copy-start | bytes 3538948
  2.6 5.8 %collective-permute-start = (f32[192,128]{1,0:T(8,128)S(1)}, f32[192,128]{1,0:T(8,128)S(1)}, u32[]{:S(2)}, u32[]{:S(2)}) collective-permute-start(f32[192,128]{1,0:T(8,128)S(1)} %get-tuple-element.38), channel_id=1, source_target_pairs={{0,1},{1,0},{2,3},{3,2},{4,5},{5,4},{6,7},{7,6},{8,9},{9,8},{10,11... | collective-permute-start | bytes 294920 | tf_op jit(solution)/shard_map/ppermute | solution.py:494
  3.1 5.3 %collective-permute-start.1 = (f32[192,128]{1,0:T(8,128)S(1)}, f32[192,128]{1,0:T(8,128)S(1)}, u32[]{:S(2)}, u32[]{:S(2)}) collective-permute-start(f32[192,128]{1,0:T(8,128)S(1)} %get-tuple-element.39), channel_id=1, source_target_pairs={{1,2},{2,1},{3,4},{4,3},{5,6},{6,5},{7,8},{8,7},{9,10},{10,9},{11,... | collective-permute-start | bytes 294920 | tf_op jit(solution)/shard_map/ppermute | solution.py:490
  6.3 8.1 %copy-start.2 = (bf16[272,768]{1,0:T(8,128)(2,1)S(1)}, bf16[272,768]{1,0:T(8,128)(2,1)}, u32[]{:S(2)}) copy-start(bf16[272,768]{1,0:T(8,128)(2,1)} %constant.25.clone.waves_ref) | copy-start | bytes 1253380
  6.3 8.1 %copy-start.3 = (bf16[256,256]{1,0:T(8,128)(2,1)S(1)}, bf16[256,256]{1,0:T(8,128)(2,1)}, u32[]{:S(2)}) copy-start(bf16[256,256]{1,0:T(8,128)(2,1)} %constant.23.clone.inner_ref) | copy-start | bytes 393220
  6.4 8.1 %copy-start.4 = (bf16[256,16]{1,0:T(8,128)(2,1)S(1)}, bf16[256,16]{1,0:T(8,128)(2,1)}, u32[]{:S(2)}) copy-start(bf16[256,16]{1,0:T(8,128)(2,1)} %constant.24.clone.outer_ref) | copy-start | bytes 24580
  6.4 5.0 %collective-permute-start.4 = (f32[32,256]{1,0:T(8,128)S(1)}, f32[32,256]{1,0:T(8,128)S(1)}, u32[]{:S(2)}, u32[]{:S(2)}) collective-permute-start(f32[32,256]{1,0:T(8,128)S(1)} %get-tuple-element.45), channel_id=1, source_target_pairs={{1,2},{2,1},{3,4},{4,3},{5,6},{6,5},{7,8},{8,7},{9,10},{10,9},{11,... | collective-permute-start | bytes 98312 | tf_op jit(solution)/shard_map/ppermute | solution.py:490
  6.5 4.9 %collective-permute-start.5 = (f32[32,256]{1,0:T(8,128)S(1)}, f32[32,256]{1,0:T(8,128)S(1)}, u32[]{:S(2)}, u32[]{:S(2)}) collective-permute-start(f32[32,256]{1,0:T(8,128)S(1)} %get-tuple-element.46), channel_id=1, source_target_pairs={{0,1},{1,0},{2,3},{3,2},{4,5},{5,4},{6,7},{7,6},{8,9},{9,8},{10,11... | collective-permute-start | bytes 98312 | tf_op jit(solution)/shard_map/ppermute | solution.py:494
  9.0 5.4 %collective-permute-start.2 = (f32[8,256]{1,0:T(8,128)S(1)}, f32[8,256]{1,0:T(8,128)S(1)}, u32[]{:S(2)}, u32[]{:S(2)}) collective-permute-start(f32[8,256]{1,0:T(8,128)S(1)} %get-tuple-element.43), channel_id=1, source_target_pairs={{0,1},{1,0},{2,3},{3,2},{4,5},{5,4},{6,7},{7,6},{8,9},{9,8},{10,11... | collective-permute-start | bytes 24584 | tf_op jit(solution)/shard_map/ppermute | solution.py:494
  9.4 4.9 %collective-permute-start.3 = (f32[8,256]{1,0:T(8,128)S(1)}, f32[8,256]{1,0:T(8,128)S(1)}, u32[]{:S(2)}, u32[]{:S(2)}) collective-permute-start(f32[8,256]{1,0:T(8,128)S(1)} %get-tuple-element.44), channel_id=1, source_target_pairs={{1,2},{2,1},{3,4},{4,3},{5,6},{6,5},{7,8},{8,7},{9,10},{10,9},{11,... | collective-permute-start | bytes 24584 | tf_op jit(solution)/shard_map/ppermute | solution.py:490
  16.3 2.4 %copy-start = (bf16[768,1024]{1,0:T(8,128)(2,1)S(1)}, bf16[768,1024]{1,0:T(8,128)(2,1)}, u32[]{:S(2)}) copy-start(bf16[768,1024]{1,0:T(8,128)(2,1)} %constant.26.clone.operator_ref) | copy-start | bytes 4718596
  16.3 4.2 %collective-permute-start.7 = (f32[8,256]{1,0:T(8,128)S(1)}, f32[8,256]{1,0:T(8,128)S(1)}, u32[]{:S(2)}, u32[]{:S(2)}) collective-permute-start(f32[8,256]{1,0:T(8,128)S(1)} %get-tuple-element.63), channel_id=1, source_target_pairs={{1,2},{2,1},{3,4},{4,3},{5,6},{6,5},{7,8},{8,7},{9,10},{10,9},{11,... | collective-permute-start | bytes 24584 | tf_op jit(solution)/shard_map/ppermute | solution.py:490
  18.5 2.1 %collective-permute-start.6 = (f32[8,256]{1,0:T(8,128)S(1)}, f32[8,256]{1,0:T(8,128)S(1)}, u32[]{:S(2)}, u32[]{:S(2)}) collective-permute-start(f32[8,256]{1,0:T(8,128)S(1)} %mean_core.1), channel_id=1, source_target_pairs={{0,1},{1,0},{2,3},{3,2},{4,5},{5,4},{6,7},{7,6},{8,9},{9,8},{10,11... | collective-permute-start | bytes 24584 | tf_op jit(solution)/shard_map/ppermute | solution.py:494
  18.7 1.9 %copy-start.6 = (s32[512]{0:T(512)S(1)}, s32[512]{0:T(512)}, u32[]{:S(2)}) copy-start(s32[512]{0:T(512)} %param.22) | copy-start | bytes 6148

commit v7 on v6

--- a/solution.py
+++ b/solution.py
@@ -29,10 +29,14 @@
     return np.asarray(table, np.float32).astype(ml_dtypes.bfloat16)
 
 
-def halves(table):
-    high = rounded(table)
-    low = rounded(np.asarray(table, np.float64) - high.astype(np.float64))
-    return high, low
+def shaped(table):
+    result = np.zeros(table.shape, ml_dtypes.bfloat16)
+    carry = np.zeros(table.shape[:-1])
+    for i in range(table.shape[-1]):
+        wanted = table[..., i] + carry
+        result[..., i] = rounded(wanted)
+        carry = wanted - result[..., i].astype(np.float64)
+    return result
 
 
 def twiddle(position, frequency, period, amplitude):
@@ -99,8 +103,7 @@
     row_blur = rounded(blur_weight(row_diff, reach))
     inner = row_blur[:, reach : reach + tile_rows]
     outer = np.concatenate([row_blur[:, :reach], row_blur[:, reach + tile_rows :]], axis=1)
-    high, low = halves(spread_blur)
-    operator = np.concatenate([high, high, low], axis=0)
+    operator = np.ascontiguousarray(shaped(spread_blur.T).T)
 
     freqs = np.arange(col_freqs)
     gauss = blur_weight(np.arange(-reach, reach + 1), reach)
@@ -113,20 +116,22 @@
     imag = (-gain[:, None] * sines).reshape(-1, 8, samples)
     mid = col_freqs // 16
     above, below = slice(mid + 1, None), slice(mid - 1, 0, -1)
-    paired = [
+    sides = [
         real[above] + real[below], imag[above] - imag[below],
         imag[above] + imag[below], real[above] - real[below],
-        real[mid : mid + 1], imag[mid : mid + 1], real[:1], imag[:1],
     ]
-    paired = np.concatenate(paired, axis=0).reshape(-1, samples)
+    paired = np.concatenate(
+        [np.stack([real[mid], imag[mid], real[0], imag[0]]).reshape(-1, samples)]
+        + [np.stack(sides, axis=1).reshape(-1, samples)]
+    )
     ring = np.zeros((tile_cols, tile_cols))
     for shift in range(-reach, reach + 1):
         ring[line, (line + shift) % tile_cols] = gauss[shift + reach]
     edge = np.concatenate([line[:reach], line[tile_cols - reach :]])
     cut = (spread @ (col_blur.astype(np.float64) - ring)[:, edge]).T
     waves = np.concatenate([paired, cut], axis=0)
-    high, low = halves(waves)
-    waves = np.concatenate([high, high, low], axis=1)
+    waves = shaped(waves)
+    waves = np.concatenate([waves, waves], axis=1)
     return operator, waves, np.ascontiguousarray(inner), np.ascontiguousarray(outer)
 
 
@@ -372,32 +377,38 @@
         ends_ref[site, 32:] = jnp.maximum(1.0 - jnp.abs(position - edge), 0.0)
 
 
-def site_means(table_ref, tents_ref, spin_ref, ends_ref, middle):
+def site_means(table_ref, tents_ref, spin_ref, ends_ref, middle, beside=None):
     slots = tents_ref.shape[2]
     count = spin_ref.shape[1] // 4
     pairs = count - 1
     none = jnp.zeros((8, slots), F32)
     total = none
     for site in range(SITES):
+        if beside is not None:
+            beside(site)
         picked = jnp.dot(table_ref[...], tents_ref[site], preferred_element_type=F32)
         rows = [picked[8 * i : 8 * i + 8] for i in range(4 * pairs + 6)]
 
         def spin(i):
             return jnp.broadcast_to(spin_ref[site, i : i + 1], (8, slots))
 
-        for side in range(2):
-            first = 2 * count * side
+        def ends(i):
+            return ends_ref[site, 8 * i : 8 * i + 8]
+
+        sums = []
+        for first in (0, 2 * count):
             cosine, sine = spin(first + pairs), spin(first + count + pairs)
-            low_real, low_imag = rows[4 * pairs + 2], rows[4 * pairs + 3]
-            real = rows[4 * pairs] + low_real * cosine + low_imag * sine
-            imag = rows[4 * pairs + 1] + low_imag * cosine - low_real * sine
-            for k in range(pairs):
+            sums.append(rows[0] + rows[2] * cosine + rows[3] * sine)
+            sums.append(rows[1] + rows[3] * cosine - rows[2] * sine)
+        for k in range(pairs):
+            here = rows[4 * k + 4 : 4 * k + 8]
+            for side in range(2):
+                first = 2 * count * side
                 cosine, sine = spin(first + k), spin(first + count + k)
-                real += rows[k] * cosine - rows[pairs + k] * sine
-                imag += rows[2 * pairs + k] * cosine + rows[3 * pairs + k] * sine
-            total += real * ends_ref[site, 16 * side : 16 * side + 8]
-            total -= imag * ends_ref[site, 16 * side + 8 : 16 * side + 16]
-        total += rows[4 * pairs + 4] * ends_ref[site, 32:40] + rows[4 * pairs + 5] * ends_ref[site, 40:]
+                sums[2 * side] += here[0] * cosine - here[1] * sine
+                sums[2 * side + 1] += here[2] * cosine + here[3] * sine
+        total += (sums[0] * ends(0) - sums[1] * ends(1)) + (sums[2] * ends(2) - sums[3] * ends(3))
+        total += rows[4 * pairs + 4] * ends(4) + rows[4 * pairs + 5] * ends(5)
     mean = middle + jnp.sum(total, axis=0, keepdims=True) * (1.0 / SITES)
     return jnp.broadcast_to(mean, (8, slots))
 
@@ -419,11 +430,10 @@
     middle = middle * (1.0 / (blurred.shape[0] * blurred.shape[1]))
     high = blurred.astype(BF16)
     low = (blurred - high.astype(F32)).astype(BF16)
-    parts = jnp.concatenate([high, low, high], axis=1)
+    parts = jnp.concatenate([high, low], axis=1)
     parts_ref[...] = parts
     table = transposed_dot(waves_ref[...], parts)
-    lowest = table.shape[0] - 2 * BLUR_REACH - 16
-    first = lax.broadcasted_iota(jnp.int32, table.shape, 0) == lowest
+    first = lax.broadcasted_iota(jnp.int32, table.shape, 0) == 16
     table_ref[...] = jnp.where(first, table - middle, table).astype(BF16)
     middle_ref[...] = jnp.broadcast_to(middle, middle_ref.shape)
     mean_ref[...] = site_means(
@@ -441,13 +451,28 @@
     parts_ref, operator_ref, table_ref, tents_ref, spin_ref, ends_ref, middle_ref,
     resist_hbm, mean_ref, resist_ref, sem,
 ):
-    resist_ref[...] = jnp.dot(parts_ref[...], operator_ref[...], preferred_element_type=F32)
-    copy = pltpu.make_async_copy(resist_ref, resist_hbm, sem)
-    copy.start()
+    cols = resist_ref.shape[1] // 4
+    copies = []
+
+    def beside(site):
+        if site % 3 == 0 and len(copies) < 4:
+            lanes = pl.ds(len(copies) * cols, cols)
+            block = operator_ref[:, lanes]
+            resist_ref[:, lanes] = jnp.dot(
+                parts_ref[...], jnp.concatenate([block, block], axis=0), preferred_element_type=F32
+            )
+            copies.append(
+                pltpu.make_async_copy(
+                    resist_ref.at[:, lanes], resist_hbm.at[:, lanes], sem.at[len(copies)]
+                )
+            )
+            copies[-1].start()
+
     mean_ref[...] = site_means(
-        table_ref, tents_ref, spin_ref, ends_ref, middle_ref[:1, :1]
-    )
-    copy.wait()
+        table_ref, tents_ref, spin_ref, ends_ref, middle_ref[:1, :1], beside
+    )
+    for copy in copies:
+        copy.wait()
 
 
 def bias_kernel(level_ref, places_ref, own_ref, core_ref, chip_ref, steps_ref, out_ref):
@@ -606,7 +631,7 @@
     chip_sites, core_sites = other_sites[:3], other_sites[3:]
     parts, table, middle, mean_chip = call(
         resist_kernel,
-        [((tile_rows, 3 * samples), BF16), ((waves.shape[0], tile_rows), BF16), ((8, 128), F32), means],
+        [((tile_rows, 2 * samples), BF16), ((waves.shape[0], tile_rows), BF16), ((8, 128), F32), means],
         (intensity, edge_core, edge_chip, inner, outer, waves, *chip_sites),
         name="resist",
     )
@@ -618,7 +643,7 @@
         [((tile_rows, tile_cols), F32), means],
         (parts, operator, table, *own_sites, middle),
         hbm_outs=(0,),
-        scratch=[pltpu.VMEM((tile_rows, tile_cols), F32), pltpu.SemaphoreType.DMA],
+        scratch=[pltpu.VMEM((tile_rows, tile_cols), F32), pltpu.SemaphoreType.DMA((4,))],
         name="mean_own",
     )
     (new_bias,) = call(

time: 21.7 us -> 20.4 us (0.940); the launches traced: 21.3 us -> 20.3 us
  Pallas kernels: 13.1 us -> 11.8 us
  waiting for transfers between devices: 0.02 us -> 0.25 us
    pallas_call x10, Pallas kernels: 13.1 us -> 11.8 us  [call(): pl.pallas_call(kernel, out_shape=[jax.ShapeDtypeStruct(s, d) for s, d in...]
    ppermute x4, waiting for transfers between devices: 0.01 us -> 0.24 us  [swap_chips(): return lax.ppermute(to_chip, ('groups', 'tx'), pairs)]
  transfers between devices with their start and end apart: 8 -> 8, of which waited for: 0 -> 1; matrix products, arithmetic and copies ran while one was open for 0% -> 0% of each run, Pallas kernels for 40% -> 38%
where the time goes in v7:
time: 20.4 us; the launch traced here: 20.3 us
  Pallas kernels  11.8 us (58%)
  starting transfers between devices  6.68 us (33%)
  between operations  1.47 us (7%)
  waiting for transfers between devices  0.25 us (1%)
    pallas_call x10, Pallas kernels, call(): pl.pallas_call(kernel, out_shape=[jax.ShapeDtypeStruct(s, d) for s, d in...  11.8 us
    ppermute x4, starting transfers between devices, swap_chips(): return lax.ppermute(to_chip, ('groups', 'tx'), pairs)  5.32 us
    ppermute x4, starting transfers between devices, swap_cores(): lax.ppermute(to_core, 'tx', [(i, i ^ 1) for i in range(lax.axis_size('tx'...  1.36 us
  transfers between devices with their start and end apart: 8, of which 1 were waited for; matrix products, arithmetic and copies ran while one was open for 0% of the time, Pallas kernels for 38%

profile of v7, /device:TPU:0, one launch (start us, length us, event | category | flops | bytes accessed | tf_op | source)
XLA Modules:
  0.0 20.3 jit_solution(14102664288984950691)
XLA Ops:
  0.6 0.0 copy-start.5
  0.6 0.0 copy-start
  0.7 2.0 %front.1 = (bf16[256,256]{1,0:T(8,128)(2,1)S(1)}, f32[192,128]{1,0:T(8,128)S(1)}, f32[192,128]{1,0:T(8,128)S(1)}, s32[1,512]{1,0:T(1,128)S(1)}, f32[32,512]{1,0:T(8,128)S(1)}) custom-call(bf16[256,1024]{1,0:T(8,128)(2,1)} %mask_hbm.1, bf16[1024,256]{1,0:T(8,128)(2,1)} %constant.18.clone.forward_hbm, bf16[384,256]{1,0:T(8,128)(2,1)} %constant.19.clone.rows_hbm, ...), custom_call_target="tpu_custom_call" | custom-call | tf_op jit(solution)/shard_map/front/pallas_call | solution.py:533
  2.6 0.5 %collective-permute-start = (f32[192,128]{1,0:T(8,128)S(1)}, f32[192,128]{1,0:T(8,128)S(1)}, u32[]{:S(2)}, u32[]{:S(2)}) collective-permute-start(f32[192,128]{1,0:T(8,128)S(1)} %get-tuple-element.38), channel_id=1, source_target_pairs={{0,1},{1,0},{2,3},{3,2},{4,5},{5,4},{6,7},{7,6},{8,9},{9,8},{10,11... | collective-permute-start | bytes 294920 | tf_op jit(solution)/shard_map/ppermute | solution.py:519
  3.1 2.6 %collective-permute-start.1 = (f32[192,128]{1,0:T(8,128)S(1)}, f32[192,128]{1,0:T(8,128)S(1)}, u32[]{:S(2)}, u32[]{:S(2)}) collective-permute-start(f32[192,128]{1,0:T(8,128)S(1)} %get-tuple-element.39), channel_id=1, source_target_pairs={{1,2},{2,1},{3,4},{4,3},{5,6},{6,5},{7,8},{8,7},{9,10},{10,9},{11,... | collective-permute-start | bytes 294920 | tf_op jit(solution)/shard_map/ppermute | solution.py:515
  5.7 0.6 %pack.1 = (f32[32,256]{1,0:T(8,128)S(1)}, f32[32,256]{1,0:T(8,128)S(1)}, f32[32,256]{1,0:T(8,128)S(1)}, s32[1,512]{1,0:T(1,128)S(1)}) custom-call(bf16[256,256]{1,0:T(8,128)(2,1)S(1)} %get-tuple-element.33.after_ref.spectra_ref, s32[1,512]{1,0:T(1,128)S(1)} %get-tuple-element.34.eval_ref, f32[32,512]{1,0:T(8,128)S(1)} %get-tuple-element.35.records_ref), custom_call_target="tpu_custom_call" | custom-call | tf_op jit(solution)/shard_map/pack/pallas_call | solution.py:533
  6.3 0.0 copy-start.2
  6.3 0.0 copy-start.3
  6.4 0.0 copy-start.4
  6.4 0.1 collective-permute-start.4
  6.5 0.1 collective-permute-start.5
  7.3 1.1 %load.1 = (f32[8,128]{1,0:T(8,128)S(1)}, f32[192,128]{1,0:T(8,128)S(1)}, bf16[512,192]{1,0:T(8,128)(2,1)S(1)}, bf16[256,512]{1,0:T(8,128)(2,1)S(1)}, bf16[16,256...) custom-call(bf16[256,256]{1,0:T(8,128)(2,1)S(1)} %get-tuple-element.33.after_ref.spectra_ref, ...), custom_call_target="tpu_custom_call" | custom-call | tf_op jit(solution)/shard_map/load/pallas_call | solution.py:533
  8.4 0.0 collective-permute-done.core_ref
  8.4 0.0 collective-permute-done.1.chip_ref
  8.4 0.5 %edges.1 = (bf16[192,1536]{1,0:T(8,128)(2,1)S(1)}, f32[8,256]{1,0:T(8,128)S(1)}, f32[8,256]{1,0:T(8,128)S(1)}) custom-call(f32[1,12]{1,0:T(1,128)S(1)} %bitcast.7, f32[192,128]{1,0:T(8,128)S(1)} %get-tuple-element.37.own_ref, f32[192,128]{1,0:T(8,128)S(1)} %collective-permute-done.core_ref, f32[192,128]{1,0:T(8,128)S(1)} %collective-permute-done.1.chip_ref, ...), custom_call_target="tpu_custom_call" | custom-call | tf_op jit(solution)/shard_map/edges/pallas_call | solution.py:533
  9.0 0.5 %collective-permute-start.2 = (f32[8,256]{1,0:T(8,128)S(1)}, f32[8,256]{1,0:T(8,128)S(1)}, u32[]{:S(2)}, u32[]{:S(2)}) collective-permute-start(f32[8,256]{1,0:T(8,128)S(1)} %get-tuple-element.43), channel_id=1, source_target_pairs={{0,1},{1,0},{2,3},{3,2},{4,5},{5,4},{6,7},{7,6},{8,9},{9,8},{10,11... | collective-permute-start | bytes 24584 | tf_op jit(solution)/shard_map/ppermute | solution.py:519
  9.4 1.9 %collective-permute-start.3 = (f32[8,256]{1,0:T(8,128)S(1)}, f32[8,256]{1,0:T(8,128)S(1)}, u32[]{:S(2)}, u32[]{:S(2)}) collective-permute-start(f32[8,256]{1,0:T(8,128)S(1)} %get-tuple-element.44), channel_id=1, source_target_pairs={{1,2},{2,1},{3,4},{4,3},{5,6},{6,5},{7,8},{8,7},{9,10},{10,9},{11,... | collective-permute-start | bytes 24584 | tf_op jit(solution)/shard_map/ppermute | solution.py:515
  11.4 0.0 collective-permute-done.4.chip_coords_ref
  11.4 0.0 collective-permute-done.5.core_coords_ref
  11.4 1.6 %prepare.1 = (bf16[16,256,256]{2,1,0:T(8,128)(2,1)S(1)}, f32[16,32,256]{2,1,0:T(8,128)S(1)}, f32[16,48,256]{2,1,0:T(8,128)S(1)}, bf16[16,256,256]{2,1,0:T(8,128)...) custom-call(f32[32,256]{1,0:T(8,128)S(1)} %collective-permute-done.4.chip_coords_ref, ...), custom_call_target="tpu_custom_call" | custom-call | tf_op jit(solution)/shard_map/prepare/pallas_call | solution.py:533
  13.0 1.4 %imaging.1.intensity_ref = bf16[256,256]{1,0:T(8,128)(2,1)S(1)} custom-call(f32[1,12]{1,0:T(1,128)S(1)} %bitcast.8, bf16[192,1536]{1,0:T(8,128)(2,1)S(1)} %get-tuple-element.42.product_ref, bf16[512,192]{1,0:T(8,128)(2,1)S(1)} %get-tuple-element.40.inverse_ref, bf16[256,512]{1,0:T(8,128)(2,1)S(1)} %get-tuple-element.41.spread_ref), custom_call_target="tpu_custom_call" | custom-call | tf_op jit(solution)/shard_map/imaging/pallas_call | solution.py:533
  14.4 0.0 collective-permute-done.2.core_ref
  14.4 0.0 collective-permute-done.3.chip_ref
  14.4 1.4 %resist.1 = (bf16[256,512]{1,0:T(8,128)(2,1)S(1)}, bf16[272,256]{1,0:T(8,128)(2,1)S(1)}, f32[8,128]{1,0:T(8,128)S(1)}, f32[8,256]{1,0:T(8,128)S(1)}) custom-call(bf16[256,256]{1,0:T(8,128)(2,1)S(1)} %imaging.1.intensity_ref, f32[8,256]{1,0:T(8,128)S(1)} %collective-permute-done.2.core_ref, f32[8,256]{1,0:T(8,128)S(1)} %collective-permute-done.3.chip_ref, ...), custom_call_target="tpu_custom_call" | custom-call | tf_op jit(solution)/shard_map/resist/pallas_call | solution.py:533
  15.8 0.0 copy-start.1
  15.8 0.7 %collective-permute-start.7 = (f32[8,256]{1,0:T(8,128)S(1)}, f32[8,256]{1,0:T(8,128)S(1)}, u32[]{:S(2)}, u32[]{:S(2)}) collective-permute-start(f32[8,256]{1,0:T(8,128)S(1)} %get-tuple-element.63), channel_id=1, source_target_pairs={{1,2},{2,1},{3,4},{4,3},{5,6},{6,5},{7,8},{8,7},{9,10},{10,9},{11,... | collective-permute-start | bytes 24584 | tf_op jit(solution)/shard_map/ppermute | solution.py:515
  16.5 1.0 %mean_core.1 = f32[8,256]{1,0:T(8,128)S(1)} custom-call(bf16[272,256]{1,0:T(8,128)(2,1)S(1)} %get-tuple-element.51.table_ref, bf16[16,256,256]{2,1,0:T(8,128)(2,1)S(1)} %get-tuple-element.60.tents_ref, f32[16,32,256]{2,1,0:T(8,128)S(1)} %get-tuple-element.61.spin_ref, f32[16,48,256]{2,1,0:T(8,128)S(1)} %get-tuple-element.62.ends_ref, ...), custom_call_target="tpu_custom_call" | custom-call | tf_op jit(solution)/shard_map/mean_core/pallas_call | solution.py:533
  17.5 0.2 %collective-permute-start.6 = (f32[8,256]{1,0:T(8,128)S(1)}, f32[8,256]{1,0:T(8,128)S(1)}, u32[]{:S(2)}, u32[]{:S(2)}) collective-permute-start(f32[8,256]{1,0:T(8,128)S(1)} %mean_core.1), channel_id=1, source_target_pairs={{0,1},{1,0},{2,3},{3,2},{4,5},{5,4},{6,7},{7,6},{8,9},{9,8},{10,11... | collective-permute-start | bytes 24584 | tf_op jit(solution)/shard_map/ppermute | solution.py:519
  17.7 1.6 %mean_own.1 = (f32[256,1024]{1,0:T(8,128)}, f32[8,256]{1,0:T(8,128)S(1)}) custom-call(bf16[256,512]{1,0:T(8,128)(2,1)S(1)} %get-tuple-element.50.parts_ref, bf16[256,1024]{1,0:T(8,128)(2,1)S(1)} %copy-done.1, bf16[272,256]{1,0:T(8,128)(2,1)S(1)} %get-tuple-element.51.table_ref, bf16[16,256,256]{2,1,0:T(8,128)(2,1)S(1)} %get-tuple-element.52.tents_ref, ...), custom_call_target="tpu_custom_call" | custom-call | tf_op jit(solution)/shard_map/mean_own/pallas_call | solution.py:533
  19.3 0.2 %collective-permute-done.7.chip_ref = f32[8,256]{1,0:T(8,128)S(1)} collective-permute-done((f32[8,256]{1,0:T(8,128)S(1)}, f32[8,256]{1,0:T(8,128)S(1)}, u32[]{:S(2)}, u32[]{:S(2)}) %collective-permute-start.7) | collective-permute-done | bytes 8224 | tf_op jit(solution)/shard_map/ppermute | solution.py:515
  19.5 0.0 collective-permute-done.6.core_ref
  19.5 0.7 %bias.1 = f32[1,512]{1,0:T(1,128)} custom-call(f32[8,128]{1,0:T(8,128)S(1)} %get-tuple-element.57.level_ref, s32[1,512]{1,0:T(1,128)S(1)} %get-tuple-element.58.places_ref, f32[8,256]{1,0:T(8,128)S(1)} %get-tuple-element.59.own_ref, f32[8,256]{1,0:T(8,128)S(1)} %collective-permute-done.6.core_ref, f32[8,256]{1,0:T(8,128)S(1)} %collective-permute-done.7.chip_ref, ...), custom_call_target="tpu_custom_call" | custom-call | tf_op jit(solution)/shard_map/bias/pallas_call | solution.py:533
  (8 shorter events, 0.0 us)
Async XLA Ops:
  0.6 7.8 %copy-start.5 = (f32[12]{0:T(128)S(1)}, f32[12]{0:T(128)}, u32[]{:S(2)}) copy-start(f32[12]{0:T(128)} %param.18) | copy-start | bytes 148
  0.6 7.8 %copy-start = (f32[2,96,12,128]{3,1,2,0:T(8,128)S(1)}, f32[2,96,12,128]{3,1,2,0:T(8,128)}, u32[]{:S(2)}) copy-start(f32[2,96,12,128]{3,1,2,0:T(8,128)} %param.17) | copy-start | bytes 3538948
  2.6 5.8 %collective-permute-start = (f32[192,128]{1,0:T(8,128)S(1)}, f32[192,128]{1,0:T(8,128)S(1)}, u32[]{:S(2)}, u32[]{:S(2)}) collective-permute-start(f32[192,128]{1,0:T(8,128)S(1)} %get-tuple-element.38), channel_id=1, source_target_pairs={{0,1},{1,0},{2,3},{3,2},{4,5},{5,4},{6,7},{7,6},{8,9},{9,8},{10,11... | collective-permute-start | bytes 294920 | tf_op jit(solution)/shard_map/ppermute | solution.py:519
  3.1 5.3 %collective-permute-start.1 = (f32[192,128]{1,0:T(8,128)S(1)}, f32[192,128]{1,0:T(8,128)S(1)}, u32[]{:S(2)}, u32[]{:S(2)}) collective-permute-start(f32[192,128]{1,0:T(8,128)S(1)} %get-tuple-element.39), channel_id=1, source_target_pairs={{1,2},{2,1},{3,4},{4,3},{5,6},{6,5},{7,8},{8,7},{9,10},{10,9},{11,... | collective-permute-start | bytes 294920 | tf_op jit(solution)/shard_map/ppermute | solution.py:515
  6.3 8.1 %copy-start.2 = (bf16[272,512]{1,0:T(8,128)(2,1)S(1)}, bf16[272,512]{1,0:T(8,128)(2,1)}, u32[]{:S(2)}) copy-start(bf16[272,512]{1,0:T(8,128)(2,1)} %constant.25.clone.waves_ref) | copy-start | bytes 835588
  6.3 8.1 %copy-start.3 = (bf16[256,256]{1,0:T(8,128)(2,1)S(1)}, bf16[256,256]{1,0:T(8,128)(2,1)}, u32[]{:S(2)}) copy-start(bf16[256,256]{1,0:T(8,128)(2,1)} %constant.23.clone.inner_ref) | copy-start | bytes 393220
  6.4 8.0 %copy-start.4 = (bf16[256,16]{1,0:T(8,128)(2,1)S(1)}, bf16[256,16]{1,0:T(8,128)(2,1)}, u32[]{:S(2)}) copy-start(bf16[256,16]{1,0:T(8,128)(2,1)} %constant.24.clone.outer_ref) | copy-start | bytes 24580
  6.4 5.0 %collective-permute-start.4 = (f32[32,256]{1,0:T(8,128)S(1)}, f32[32,256]{1,0:T(8,128)S(1)}, u32[]{:S(2)}, u32[]{:S(2)}) collective-permute-start(f32[32,256]{1,0:T(8,128)S(1)} %get-tuple-element.45), channel_id=1, source_target_pairs={{1,2},{2,1},{3,4},{4,3},{5,6},{6,5},{7,8},{8,7},{9,10},{10,9},{11,... | collective-permute-start | bytes 98312 | tf_op jit(solution)/shard_map/ppermute | solution.py:515
  6.5 4.9 %collective-permute-start.5 = (f32[32,256]{1,0:T(8,128)S(1)}, f32[32,256]{1,0:T(8,128)S(1)}, u32[]{:S(2)}, u32[]{:S(2)}) collective-permute-start(f32[32,256]{1,0:T(8,128)S(1)} %get-tuple-element.46), channel_id=1, source_target_pairs={{0,1},{1,0},{2,3},{3,2},{4,5},{5,4},{6,7},{7,6},{8,9},{9,8},{10,11... | collective-permute-start | bytes 98312 | tf_op jit(solution)/shard_map/ppermute | solution.py:519
  9.0 5.4 %collective-permute-start.2 = (f32[8,256]{1,0:T(8,128)S(1)}, f32[8,256]{1,0:T(8,128)S(1)}, u32[]{:S(2)}, u32[]{:S(2)}) collective-permute-start(f32[8,256]{1,0:T(8,128)S(1)} %get-tuple-element.43), channel_id=1, source_target_pairs={{0,1},{1,0},{2,3},{3,2},{4,5},{5,4},{6,7},{7,6},{8,9},{9,8},{10,11... | collective-permute-start | bytes 24584 | tf_op jit(solution)/shard_map/ppermute | solution.py:519
  9.4 4.9 %collective-permute-start.3 = (f32[8,256]{1,0:T(8,128)S(1)}, f32[8,256]{1,0:T(8,128)S(1)}, u32[]{:S(2)}, u32[]{:S(2)}) collective-permute-start(f32[8,256]{1,0:T(8,128)S(1)} %get-tuple-element.44), channel_id=1, source_target_pairs={{1,2},{2,1},{3,4},{4,3},{5,6},{6,5},{7,8},{8,7},{9,10},{10,9},{11,... | collective-permute-start | bytes 24584 | tf_op jit(solution)/shard_map/ppermute | solution.py:515
  15.8 1.9 %copy-start.1 = (bf16[256,1024]{1,0:T(8,128)(2,1)S(1)}, bf16[256,1024]{1,0:T(8,128)(2,1)}, u32[]{:S(2)}) copy-start(bf16[256,1024]{1,0:T(8,128)(2,1)} %constant.26.clone.operator_ref) | copy-start | bytes 1572868
  15.8 3.7 %collective-permute-start.7 = (f32[8,256]{1,0:T(8,128)S(1)}, f32[8,256]{1,0:T(8,128)S(1)}, u32[]{:S(2)}, u32[]{:S(2)}) collective-permute-start(f32[8,256]{1,0:T(8,128)S(1)} %get-tuple-element.63), channel_id=1, source_target_pairs={{1,2},{2,1},{3,4},{4,3},{5,6},{6,5},{7,8},{8,7},{9,10},{10,9},{11,... | collective-permute-start | bytes 24584 | tf_op jit(solution)/shard_map/ppermute | solution.py:515
  17.5 2.1 %collective-permute-start.6 = (f32[8,256]{1,0:T(8,128)S(1)}, f32[8,256]{1,0:T(8,128)S(1)}, u32[]{:S(2)}, u32[]{:S(2)}) collective-permute-start(f32[8,256]{1,0:T(8,128)S(1)} %mean_core.1), channel_id=1, source_target_pairs={{0,1},{1,0},{2,3},{3,2},{4,5},{5,4},{6,7},{7,6},{8,9},{9,8},{10,11... | collective-permute-start | bytes 24584 | tf_op jit(solution)/shard_map/ppermute | solution.py:519
  17.7 1.9 %copy-start.6 = (s32[512]{0:T(512)S(1)}, s32[512]{0:T(512)}, u32[]{:S(2)}) copy-start(s32[512]{0:T(512)} %param.22) | copy-start | bytes 6148

commit v8 on v7

--- a/solution.py
+++ b/solution.py
@@ -68,13 +68,16 @@
     row_inverse = rounded(
         np.block([[back_cos, -back_sin], [back_sin, back_cos]])
     )
+    reach = BLUR_REACH
+    near = np.r_[:reach, tile_rows - reach : tile_rows]
+    edge_inverse = np.ascontiguousarray(row_inverse[np.concatenate([near, tile_rows + near])])
     samples = 2 * col_freqs
     step = tile_cols // samples
     out_cos, out_sin = twiddle(
         centered(col_freqs), np.arange(samples) * step, tile_cols, 1.0 / math.sqrt(col_freqs)
     )
     col_inverse = rounded(np.block([[out_cos, out_sin], [-out_sin, out_cos]]))
-    return col_forward, side_rows, own_rows, row_inverse, col_inverse
+    return col_forward, side_rows, own_rows, row_inverse, edge_inverse, col_inverse
 
 
 def blur_weight(offset, reach):
@@ -240,20 +243,21 @@
 
 
 def load_kernel(
-    cols, spectra_ref, coords_ref, threshold_ref, rows_hbm, inverse_hbm, spread_hbm,
-    level_ref, own_ref, inverse_ref, spread_ref, tents_ref, spin_ref, ends_ref,
+    cols, spectra_ref, coords_ref, threshold_ref, rows_hbm, inverse_hbm, lines_hbm, spread_hbm,
+    level_ref, own_ref, inverse_ref, lines_ref, spread_ref, tents_ref, spin_ref, ends_ref,
     rows_ref, sems,
 ):
     copies = started(
-        sems, (rows_hbm, rows_ref), (inverse_hbm, inverse_ref), (spread_hbm, spread_ref)
+        sems,
+        (rows_hbm, rows_ref), (inverse_hbm, inverse_ref), (lines_hbm, lines_ref), (spread_hbm, spread_ref),
     )
     level_ref[...] = jnp.full(level_ref.shape, threshold_ref[0], F32)
     site_tables(coords_ref[...], tents_ref, spin_ref, ends_ref, cols)
     copies[0].wait()
     product = jnp.dot(rows_ref[...], spectra_ref[...], preferred_element_type=F32)
     own_ref[...] = part_spectrum(product, own_ref.shape[0] // 2, own_ref.shape[1])
-    copies[1].wait()
-    copies[2].wait()
+    for copy in copies[1:]:
+        copy.wait()
 
 
 def stacked_pairs(half, rows, kernels, cols):
@@ -265,11 +269,10 @@
 
 
 def edge_kernel(
-    weights_ref, own_ref, core_ref, chip_ref, kern_ref, inverse_ref, spread_ref,
+    weights_ref, own_ref, core_ref, chip_ref, kern_ref, lines_ref, spread_ref,
     product_ref, edge_core_ref, edge_chip_ref,
 ):
     freqs, cols = own_ref.shape[0] // 2, own_ref.shape[1]
-    rows = inverse_ref.shape[0] // 2
     kernels = kern_ref.shape[1]
     odd = parity()
     chip = jnp.where(has_chip_side(), chip_ref[...], 0.0)
@@ -281,14 +284,7 @@
         product_ref[:freqs, lanes] = (kern_real * spec_real - kern_imag * spec_imag).astype(BF16)
         product_ref[freqs:, lanes] = (kern_real * spec_imag + kern_imag * spec_real).astype(BF16)
     reach = BLUR_REACH
-    lines = jnp.concatenate(
-        [
-            inverse_ref[:reach], inverse_ref[rows - reach : rows],
-            inverse_ref[rows : rows + reach], inverse_ref[2 * rows - reach :],
-        ],
-        axis=0,
-    )
-    half = jnp.dot(lines, product_ref[...], preferred_element_type=F32).astype(BF16)
+    half = jnp.dot(lines_ref[...], product_ref[...], preferred_element_type=F32).astype(BF16)
     pairs = stacked_pairs(half, 2 * reach, kernels, cols)
     field = jnp.dot(pairs, spread_ref[...], preferred_element_type=F32)
     total = jnp.zeros((2 * reach, 2 * cols), F32)
@@ -552,7 +548,7 @@
     samples = 2 * col_freqs
     flat = kernels * col_freqs
     records = 2 * SITES
-    col_forward, side_rows, own_rows, row_inverse, col_inverse = imaging_tables(
+    col_forward, side_rows, own_rows, row_inverse, edge_inverse, col_inverse = imaging_tables(
         tile_rows, tile_cols, row_freqs, col_freqs
     )
     operator, waves, inner, outer = blur_tables(tile_rows, tile_cols, col_freqs, BLUR_REACH)
@@ -595,14 +591,14 @@
     )
     coords_chip = swap_chips(packed_chip)
     coords_core = swap_cores(packed_core)
-    level, own, inverse, spread, *own_sites = call(
+    tables = (row_inverse, edge_inverse, col_inverse)
+    level, own, inverse, lines, spread, *own_sites = call(
         functools.partial(load_kernel, tile_cols),
-        [((8, 128), F32), spectrum, (row_inverse.shape, BF16), (col_inverse.shape, BF16)]
-        + site_shapes,
-        (spectra, packed_own, threshold, own_rows, row_inverse, col_inverse),
+        [((8, 128), F32), spectrum] + [(table.shape, BF16) for table in tables] + site_shapes,
+        (spectra, packed_own, threshold, own_rows, *tables),
         smem=(2,),
-        hbm=(3, 4, 5),
-        scratch=[pltpu.VMEM(own_rows.shape, BF16), pltpu.SemaphoreType.DMA((3,))],
+        hbm=(3, 4, 5, 6),
+        scratch=[pltpu.VMEM(own_rows.shape, BF16), pltpu.SemaphoreType.DMA((4,))],
         name="load",
     )
     kern = jnp.transpose(kernel_spectra, (0, 2, 1, 3))
@@ -610,7 +606,7 @@
         edge_kernel,
         [((2 * row_freqs, flat), BF16), edge, edge],
         (
-            weights, own, got_core, got_chip, kern, inverse, spread,
+            weights, own, got_core, got_chip, kern, lines, spread,
         ),
         name="edges",
     )

time: 20.4 us -> 20.5 us (level)
  no operation moved by 1% of the time
where the time goes in v8:
time: 20.5 us; the launch traced here: 20.3 us
  Pallas kernels  11.9 us (58%)
  starting transfers between devices  6.67 us (33%)
  between operations  1.47 us (7%)
  waiting for transfers between devices  0.23 us (1%)
    pallas_call x10, Pallas kernels, call(): pl.pallas_call(kernel, out_shape=[jax.ShapeDtypeStruct(s, d) for s, d in...  11.9 us
    ppermute x4, starting transfers between devices, swap_chips(): return lax.ppermute(to_chip, ('groups', 'tx'), pairs)  5.32 us
    ppermute x4, starting transfers between devices, swap_cores(): lax.ppermute(to_core, 'tx', [(i, i ^ 1) for i in range(lax.axis_size('tx'...  1.35 us
  transfers between devices with their start and end apart: 8, of which 1 were waited for; matrix products, arithmetic and copies ran while one was open for 0% of the time, Pallas kernels for 38%

profile of v8, /device:TPU:0, one launch (start us, length us, event | category | flops | bytes accessed | tf_op | source)
XLA Modules:
  0.0 20.3 jit_solution(2079977232922621071)
XLA Ops:
  0.6 0.0 copy-start.5
  0.6 0.0 copy-start
  0.7 2.0 %front.1 = (bf16[256,256]{1,0:T(8,128)(2,1)S(1)}, f32[192,128]{1,0:T(8,128)S(1)}, f32[192,128]{1,0:T(8,128)S(1)}, s32[1,512]{1,0:T(1,128)S(1)}, f32[32,512]{1,0:T(8,128)S(1)}) custom-call(bf16[256,1024]{1,0:T(8,128)(2,1)} %mask_hbm.1, bf16[1024,256]{1,0:T(8,128)(2,1)} %constant.20.clone.forward_hbm, bf16[384,256]{1,0:T(8,128)(2,1)} %constant.21.clone.rows_hbm, ...), custom_call_target="tpu_custom_call" | custom-call | tf_op jit(solution)/shard_map/front/pallas_call | solution.py:529
  2.6 0.0 copy-start.2
  2.6 0.0 copy-start.3
  2.6 0.0 copy-start.4
  2.7 0.5 %collective-permute-start = (f32[192,128]{1,0:T(8,128)S(1)}, f32[192,128]{1,0:T(8,128)S(1)}, u32[]{:S(2)}, u32[]{:S(2)}) collective-permute-start(f32[192,128]{1,0:T(8,128)S(1)} %get-tuple-element.39), channel_id=1, source_target_pairs={{0,1},{1,0},{2,3},{3,2},{4,5},{5,4},{6,7},{7,6},{8,9},{9,8},{10,11... | collective-permute-start | bytes 294920 | tf_op jit(solution)/shard_map/ppermute | solution.py:515
  3.2 2.6 %collective-permute-start.1 = (f32[192,128]{1,0:T(8,128)S(1)}, f32[192,128]{1,0:T(8,128)S(1)}, u32[]{:S(2)}, u32[]{:S(2)}) collective-permute-start(f32[192,128]{1,0:T(8,128)S(1)} %get-tuple-element.40), channel_id=1, source_target_pairs={{1,2},{2,1},{3,4},{4,3},{5,6},{6,5},{7,8},{8,7},{9,10},{10,9},{11,... | collective-permute-start | bytes 294920 | tf_op jit(solution)/shard_map/ppermute | solution.py:511
  5.8 0.6 %pack.1 = (f32[32,256]{1,0:T(8,128)S(1)}, f32[32,256]{1,0:T(8,128)S(1)}, f32[32,256]{1,0:T(8,128)S(1)}, s32[1,512]{1,0:T(1,128)S(1)}) custom-call(bf16[256,256]{1,0:T(8,128)(2,1)S(1)} %get-tuple-element.34.after_ref.spectra_ref, s32[1,512]{1,0:T(1,128)S(1)} %get-tuple-element.35.eval_ref, f32[32,512]{1,0:T(8,128)S(1)} %get-tuple-element.36.records_ref), custom_call_target="tpu_custom_call" | custom-call | tf_op jit(solution)/shard_map/pack/pallas_call | solution.py:529
  6.4 0.1 collective-permute-start.4
  6.5 0.1 collective-permute-start.5
  7.3 1.1 %load.1 = (f32[8,128]{1,0:T(8,128)S(1)}, f32[192,128]{1,0:T(8,128)S(1)}, bf16[512,192]{1,0:T(8,128)(2,1)S(1)}, bf16[32,192]{1,0:T(8,128)(2,1)S(1)}, bf16[256,512...) custom-call(bf16[256,256]{1,0:T(8,128)(2,1)S(1)} %get-tuple-element., ...), custom_call_target="tpu_custom_call" | custom-call | tf_op jit(solution)/shard_map/load/pallas_call | solution.py:529
  8.4 0.0 collective-permute-done.core_ref
  8.4 0.0 collective-permute-done.1.chip_ref
  8.4 0.5 %edges.1 = (bf16[192,1536]{1,0:T(8,128)(2,1)S(1)}, f32[8,256]{1,0:T(8,128)S(1)}, f32[8,256]{1,0:T(8,128)S(1)}) custom-call(f32[1,12]{1,0:T(1,128)S(1)} %bitcast.7, f32[192,128]{1,0:T(8,128)S(1)} %get-tuple-element.38.own_ref, f32[192,128]{1,0:T(8,128)S(1)} %collective-permute-done.core_ref, f32[192,128]{1,0:T(8,128)S(1)} %collective-permute-done.1.chip_ref, ...), custom_call_target="tpu_custom_call" | custom-call | tf_op jit(solution)/shard_map/edges/pallas_call | solution.py:529
  9.0 0.5 %collective-permute-start.2 = (f32[8,256]{1,0:T(8,128)S(1)}, f32[8,256]{1,0:T(8,128)S(1)}, u32[]{:S(2)}, u32[]{:S(2)}) collective-permute-start(f32[8,256]{1,0:T(8,128)S(1)} %get-tuple-element.45), channel_id=1, source_target_pairs={{0,1},{1,0},{2,3},{3,2},{4,5},{5,4},{6,7},{7,6},{8,9},{9,8},{10,11... | collective-permute-start | bytes 24584 | tf_op jit(solution)/shard_map/ppermute | solution.py:515
  9.5 1.9 %collective-permute-start.3 = (f32[8,256]{1,0:T(8,128)S(1)}, f32[8,256]{1,0:T(8,128)S(1)}, u32[]{:S(2)}, u32[]{:S(2)}) collective-permute-start(f32[8,256]{1,0:T(8,128)S(1)} %get-tuple-element.46), channel_id=1, source_target_pairs={{1,2},{2,1},{3,4},{4,3},{5,6},{6,5},{7,8},{8,7},{9,10},{10,9},{11,... | collective-permute-start | bytes 24584 | tf_op jit(solution)/shard_map/ppermute | solution.py:511
  11.4 0.0 collective-permute-done.4.chip_coords_ref
  11.4 0.0 collective-permute-done.5.core_coords_ref
  11.4 1.6 %prepare.1 = (bf16[16,256,256]{2,1,0:T(8,128)(2,1)S(1)}, f32[16,32,256]{2,1,0:T(8,128)S(1)}, f32[16,48,256]{2,1,0:T(8,128)S(1)}, bf16[16,256,256]{2,1,0:T(8,128)...) custom-call(f32[32,256]{1,0:T(8,128)S(1)} %collective-permute-done.4.chip_coords_ref, ...), custom_call_target="tpu_custom_call" | custom-call | tf_op jit(solution)/shard_map/prepare/pallas_call | solution.py:529
  13.0 1.4 %imaging.1.intensity_ref = bf16[256,256]{1,0:T(8,128)(2,1)S(1)} custom-call(f32[1,12]{1,0:T(1,128)S(1)} %bitcast.8, bf16[192,1536]{1,0:T(8,128)(2,1)S(1)} %get-tuple-element.43.product_ref, bf16[512,192]{1,0:T(8,128)(2,1)S(1)} %get-tuple-element.44.inverse_ref, bf16[256,512]{1,0:T(8,128)(2,1)S(1)} %get-tuple-element.42.spread_ref), custom_call_target="tpu_custom_call" | custom-call | tf_op jit(solution)/shard_map/imaging/pallas_call | solution.py:529
  14.4 0.0 collective-permute-done.2.core_ref
  14.4 0.0 collective-permute-done.3.chip_ref
  14.4 1.4 %resist.1 = (bf16[256,512]{1,0:T(8,128)(2,1)S(1)}, bf16[272,256]{1,0:T(8,128)(2,1)S(1)}, f32[8,128]{1,0:T(8,128)S(1)}, f32[8,256]{1,0:T(8,128)S(1)}) custom-call(bf16[256,256]{1,0:T(8,128)(2,1)S(1)} %imaging.1.intensity_ref, f32[8,256]{1,0:T(8,128)S(1)} %collective-permute-done.2.core_ref, f32[8,256]{1,0:T(8,128)S(1)} %collective-permute-done.3.chip_ref, ...), custom_call_target="tpu_custom_call" | custom-call | tf_op jit(solution)/shard_map/resist/pallas_call | solution.py:529
  15.8 0.0 copy-start.1
  15.8 0.7 %collective-permute-start.7 = (f32[8,256]{1,0:T(8,128)S(1)}, f32[8,256]{1,0:T(8,128)S(1)}, u32[]{:S(2)}, u32[]{:S(2)}) collective-permute-start(f32[8,256]{1,0:T(8,128)S(1)} %get-tuple-element.65), channel_id=1, source_target_pairs={{1,2},{2,1},{3,4},{4,3},{5,6},{6,5},{7,8},{8,7},{9,10},{10,9},{11,... | collective-permute-start | bytes 24584 | tf_op jit(solution)/shard_map/ppermute | solution.py:511
  16.5 1.0 %mean_core.1 = f32[8,256]{1,0:T(8,128)S(1)} custom-call(bf16[272,256]{1,0:T(8,128)(2,1)S(1)} %get-tuple-element.53.table_ref, bf16[16,256,256]{2,1,0:T(8,128)(2,1)S(1)} %get-tuple-element.62.tents_ref, f32[16,32,256]{2,1,0:T(8,128)S(1)} %get-tuple-element.63.spin_ref, f32[16,48,256]{2,1,0:T(8,128)S(1)} %get-tuple-element.64.ends_ref, ...), custom_call_target="tpu_custom_call" | custom-call | tf_op jit(solution)/shard_map/mean_core/pallas_call | solution.py:529
  17.5 0.2 collective-permute-start.6
  17.7 1.6 %mean_own.1 = (f32[256,1024]{1,0:T(8,128)}, f32[8,256]{1,0:T(8,128)S(1)}) custom-call(bf16[256,512]{1,0:T(8,128)(2,1)S(1)} %get-tuple-element.52.parts_ref, bf16[256,1024]{1,0:T(8,128)(2,1)S(1)} %copy-done.1, bf16[272,256]{1,0:T(8,128)(2,1)S(1)} %get-tuple-element.53.table_ref, bf16[16,256,256]{2,1,0:T(8,128)(2,1)S(1)} %get-tuple-element.54.tents_ref, ...), custom_call_target="tpu_custom_call" | custom-call | tf_op jit(solution)/shard_map/mean_own/pallas_call | solution.py:529
  19.3 0.2 %collective-permute-done.7.chip_ref = f32[8,256]{1,0:T(8,128)S(1)} collective-permute-done((f32[8,256]{1,0:T(8,128)S(1)}, f32[8,256]{1,0:T(8,128)S(1)}, u32[]{:S(2)}, u32[]{:S(2)}) %collective-permute-start.7) | collective-permute-done | bytes 8224 | tf_op jit(solution)/shard_map/ppermute | solution.py:511
  19.6 0.0 collective-permute-done.6.core_ref
  19.6 0.7 %bias.1 = f32[1,512]{1,0:T(1,128)} custom-call(f32[8,128]{1,0:T(8,128)S(1)} %get-tuple-element.59.level_ref, s32[1,512]{1,0:T(1,128)S(1)} %get-tuple-element.60.places_ref, f32[8,256]{1,0:T(8,128)S(1)} %get-tuple-element.61.own_ref, f32[8,256]{1,0:T(8,128)S(1)} %collective-permute-done.6.core_ref, f32[8,256]{1,0:T(8,128)S(1)} %collective-permute-done.7.chip_ref, ...), custom_call_target="tpu_custom_call" | custom-call | tf_op jit(solution)/shard_map/bias/pallas_call | solution.py:529
  (8 shorter events, 0.0 us)
Async XLA Ops:
  0.6 7.8 %copy-start.5 = (f32[12]{0:T(128)S(1)}, f32[12]{0:T(128)}, u32[]{:S(2)}) copy-start(f32[12]{0:T(128)} %param.19) | copy-start | bytes 148
  0.6 7.8 %copy-start = (f32[2,96,12,128]{3,1,2,0:T(8,128)S(1)}, f32[2,96,12,128]{3,1,2,0:T(8,128)}, u32[]{:S(2)}) copy-start(f32[2,96,12,128]{3,1,2,0:T(8,128)} %param.18) | copy-start | bytes 3538948
  2.6 11.8 %copy-start.2 = (bf16[272,512]{1,0:T(8,128)(2,1)S(1)}, bf16[272,512]{1,0:T(8,128)(2,1)}, u32[]{:S(2)}) copy-start(bf16[272,512]{1,0:T(8,128)(2,1)} %constant.28.clone.waves_ref) | copy-start | bytes 835588
  2.6 11.8 %copy-start.3 = (bf16[256,256]{1,0:T(8,128)(2,1)S(1)}, bf16[256,256]{1,0:T(8,128)(2,1)}, u32[]{:S(2)}) copy-start(bf16[256,256]{1,0:T(8,128)(2,1)} %constant.26.clone.inner_ref) | copy-start | bytes 393220
  2.6 11.8 %copy-start.4 = (bf16[256,16]{1,0:T(8,128)(2,1)S(1)}, bf16[256,16]{1,0:T(8,128)(2,1)}, u32[]{:S(2)}) copy-start(bf16[256,16]{1,0:T(8,128)(2,1)} %constant.27.clone.outer_ref) | copy-start | bytes 24580
  2.7 5.8 %collective-permute-start = (f32[192,128]{1,0:T(8,128)S(1)}, f32[192,128]{1,0:T(8,128)S(1)}, u32[]{:S(2)}, u32[]{:S(2)}) collective-permute-start(f32[192,128]{1,0:T(8,128)S(1)} %get-tuple-element.39), channel_id=1, source_target_pairs={{0,1},{1,0},{2,3},{3,2},{4,5},{5,4},{6,7},{7,6},{8,9},{9,8},{10,11... | collective-permute-start | bytes 294920 | tf_op jit(solution)/shard_map/ppermute | solution.py:515
  3.2 5.2 %collective-permute-start.1 = (f32[192,128]{1,0:T(8,128)S(1)}, f32[192,128]{1,0:T(8,128)S(1)}, u32[]{:S(2)}, u32[]{:S(2)}) collective-permute-start(f32[192,128]{1,0:T(8,128)S(1)} %get-tuple-element.40), channel_id=1, source_target_pairs={{1,2},{2,1},{3,4},{4,3},{5,6},{6,5},{7,8},{8,7},{9,10},{10,9},{11,... | collective-permute-start | bytes 294920 | tf_op jit(solution)/shard_map/ppermute | solution.py:511
  6.4 5.0 %collective-permute-start.4 = (f32[32,256]{1,0:T(8,128)S(1)}, f32[32,256]{1,0:T(8,128)S(1)}, u32[]{:S(2)}, u32[]{:S(2)}) collective-permute-start(f32[32,256]{1,0:T(8,128)S(1)} %get-tuple-element.47), channel_id=1, source_target_pairs={{1,2},{2,1},{3,4},{4,3},{5,6},{6,5},{7,8},{8,7},{9,10},{10,9},{11,... | collective-permute-start | bytes 98312 | tf_op jit(solution)/shard_map/ppermute | solution.py:511
  6.5 5.0 %collective-permute-start.5 = (f32[32,256]{1,0:T(8,128)S(1)}, f32[32,256]{1,0:T(8,128)S(1)}, u32[]{:S(2)}, u32[]{:S(2)}) collective-permute-start(f32[32,256]{1,0:T(8,128)S(1)} %get-tuple-element.48), channel_id=1, source_target_pairs={{0,1},{1,0},{2,3},{3,2},{4,5},{5,4},{6,7},{7,6},{8,9},{9,8},{10,11... | collective-permute-start | bytes 98312 | tf_op jit(solution)/shard_map/ppermute | solution.py:515
  9.0 5.4 %collective-permute-start.2 = (f32[8,256]{1,0:T(8,128)S(1)}, f32[8,256]{1,0:T(8,128)S(1)}, u32[]{:S(2)}, u32[]{:S(2)}) collective-permute-start(f32[8,256]{1,0:T(8,128)S(1)} %get-tuple-element.45), channel_id=1, source_target_pairs={{0,1},{1,0},{2,3},{3,2},{4,5},{5,4},{6,7},{7,6},{8,9},{9,8},{10,11... | collective-permute-start | bytes 24584 | tf_op jit(solution)/shard_map/ppermute | solution.py:515
  9.5 4.9 %collective-permute-start.3 = (f32[8,256]{1,0:T(8,128)S(1)}, f32[8,256]{1,0:T(8,128)S(1)}, u32[]{:S(2)}, u32[]{:S(2)}) collective-permute-start(f32[8,256]{1,0:T(8,128)S(1)} %get-tuple-element.46), channel_id=1, source_target_pairs={{1,2},{2,1},{3,4},{4,3},{5,6},{6,5},{7,8},{8,7},{9,10},{10,9},{11,... | collective-permute-start | bytes 24584 | tf_op jit(solution)/shard_map/ppermute | solution.py:511
  15.8 1.9 %copy-start.1 = (bf16[256,1024]{1,0:T(8,128)(2,1)S(1)}, bf16[256,1024]{1,0:T(8,128)(2,1)}, u32[]{:S(2)}) copy-start(bf16[256,1024]{1,0:T(8,128)(2,1)} %constant.29.clone.operator_ref) | copy-start | bytes 1572868
  15.8 3.7 %collective-permute-start.7 = (f32[8,256]{1,0:T(8,128)S(1)}, f32[8,256]{1,0:T(8,128)S(1)}, u32[]{:S(2)}, u32[]{:S(2)}) collective-permute-start(f32[8,256]{1,0:T(8,128)S(1)} %get-tuple-element.65), channel_id=1, source_target_pairs={{1,2},{2,1},{3,4},{4,3},{5,6},{6,5},{7,8},{8,7},{9,10},{10,9},{11,... | collective-permute-start | bytes 24584 | tf_op jit(solution)/shard_map/ppermute | solution.py:511
  17.5 2.0 %collective-permute-start.6 = (f32[8,256]{1,0:T(8,128)S(1)}, f32[8,256]{1,0:T(8,128)S(1)}, u32[]{:S(2)}, u32[]{:S(2)}) collective-permute-start(f32[8,256]{1,0:T(8,128)S(1)} %mean_core.1), channel_id=1, source_target_pairs={{0,1},{1,0},{2,3},{3,2},{4,5},{5,4},{6,7},{7,6},{8,9},{9,8},{10,11... | collective-permute-start | bytes 24584 | tf_op jit(solution)/shard_map/ppermute | solution.py:515
  17.7 1.9 %copy-start.6 = (s32[512]{0:T(512)S(1)}, s32[512]{0:T(512)}, u32[]{:S(2)}) copy-start(s32[512]{0:T(512)} %param.23) | copy-start | bytes 6148

commit v9 on v8

--- a/solution.py
+++ b/solution.py
@@ -401,8 +401,8 @@
             for side in range(2):
                 first = 2 * count * side
                 cosine, sine = spin(first + k), spin(first + count + k)
-                sums[2 * side] += here[0] * cosine - here[1] * sine
-                sums[2 * side + 1] += here[2] * cosine + here[3] * sine
+                sums[2 * side] = (sums[2 * side] + here[0] * cosine) - here[1] * sine
+                sums[2 * side + 1] = (sums[2 * side + 1] + here[2] * cosine) + here[3] * sine
         total += (sums[0] * ends(0) - sums[1] * ends(1)) + (sums[2] * ends(2) - sums[3] * ends(3))
         total += rows[4 * pairs + 4] * ends(4) + rows[4 * pairs + 5] * ends(5)
     mean = middle + jnp.sum(total, axis=0, keepdims=True) * (1.0 / SITES)

time: 20.5 us -> 20.4 us (level)
  no operation moved by 1% of the time
where the time goes in v9:
time: 20.4 us; the launch traced here: 20.2 us
  Pallas kernels  11.8 us (58%)
  starting transfers between devices  6.67 us (33%)
  between operations  1.46 us (7%)
  waiting for transfers between devices  0.27 us (1%)
    pallas_call x10, Pallas kernels, call(): pl.pallas_call(kernel, out_shape=[jax.ShapeDtypeStruct(s, d) for s, d in...  11.8 us
    ppermute x4, starting transfers between devices, swap_chips(): return lax.ppermute(to_chip, ('groups', 'tx'), pairs)  5.32 us
    ppermute x4, starting transfers between devices, swap_cores(): lax.ppermute(to_core, 'tx', [(i, i ^ 1) for i in range(lax.axis_size('tx'...  1.35 us
  transfers between devices with their start and end apart: 8, of which 1 were waited for; matrix products, arithmetic and copies ran while one was open for 0% of the time, Pallas kernels for 38%

profile of v9, /device:TPU:0, one launch (start us, length us, event | category | flops | bytes accessed | tf_op | source)
XLA Modules:
  0.0 20.2 jit_solution(17819074450981889725)
XLA Ops:
  0.7 2.0 %front.1 = (bf16[256,256]{1,0:T(8,128)(2,1)S(1)}, f32[192,128]{1,0:T(8,128)S(1)}, f32[192,128]{1,0:T(8,128)S(1)}, s32[1,512]{1,0:T(1,128)S(1)}, f32[32,512]{1,0:T(8,128)S(1)}) custom-call(bf16[256,1024]{1,0:T(8,128)(2,1)} %mask_hbm.1, bf16[1024,256]{1,0:T(8,128)(2,1)} %constant.20.clone.forward_hbm, bf16[384,256]{1,0:T(8,128)(2,1)} %constant.21.clone.rows_hbm, ...), custom_call_target="tpu_custom_call" | custom-call | tf_op jit(solution)/shard_map/front/pallas_call | solution.py:529
  2.6 0.0 copy-start.2
  2.6 0.0 copy-start.3
  2.6 0.0 copy-start.4
  2.7 0.5 %collective-permute-start = (f32[192,128]{1,0:T(8,128)S(1)}, f32[192,128]{1,0:T(8,128)S(1)}, u32[]{:S(2)}, u32[]{:S(2)}) collective-permute-start(f32[192,128]{1,0:T(8,128)S(1)} %get-tuple-element.39), channel_id=1, source_target_pairs={{0,1},{1,0},{2,3},{3,2},{4,5},{5,4},{6,7},{7,6},{8,9},{9,8},{10,11... | collective-permute-start | bytes 294920 | tf_op jit(solution)/shard_map/ppermute | solution.py:515
  3.2 2.6 %collective-permute-start.1 = (f32[192,128]{1,0:T(8,128)S(1)}, f32[192,128]{1,0:T(8,128)S(1)}, u32[]{:S(2)}, u32[]{:S(2)}) collective-permute-start(f32[192,128]{1,0:T(8,128)S(1)} %get-tuple-element.40), channel_id=1, source_target_pairs={{1,2},{2,1},{3,4},{4,3},{5,6},{6,5},{7,8},{8,7},{9,10},{10,9},{11,... | collective-permute-start | bytes 294920 | tf_op jit(solution)/shard_map/ppermute | solution.py:511
  5.8 0.6 %pack.1 = (f32[32,256]{1,0:T(8,128)S(1)}, f32[32,256]{1,0:T(8,128)S(1)}, f32[32,256]{1,0:T(8,128)S(1)}, s32[1,512]{1,0:T(1,128)S(1)}) custom-call(bf16[256,256]{1,0:T(8,128)(2,1)S(1)} %get-tuple-element.34.after_ref.spectra_ref, s32[1,512]{1,0:T(1,128)S(1)} %get-tuple-element.35.eval_ref, f32[32,512]{1,0:T(8,128)S(1)} %get-tuple-element.36.records_ref), custom_call_target="tpu_custom_call" | custom-call | tf_op jit(solution)/shard_map/pack/pallas_call | solution.py:529
  6.4 0.1 collective-permute-start.4
  6.5 0.1 collective-permute-start.5
  7.3 1.1 %load.1 = (f32[8,128]{1,0:T(8,128)S(1)}, f32[192,128]{1,0:T(8,128)S(1)}, bf16[512,192]{1,0:T(8,128)(2,1)S(1)}, bf16[32,192]{1,0:T(8,128)(2,1)S(1)}, bf16[256,512...) custom-call(bf16[256,256]{1,0:T(8,128)(2,1)S(1)} %get-tuple-element., ...), custom_call_target="tpu_custom_call" | custom-call | tf_op jit(solution)/shard_map/load/pallas_call | solution.py:529
  8.4 0.0 collective-permute-done.core_ref
  8.4 0.0 collective-permute-done.1.chip_ref
  8.4 0.0 copy-done.5
  8.4 0.0 copy-done
  8.4 0.5 %edges.1 = (bf16[192,1536]{1,0:T(8,128)(2,1)S(1)}, f32[8,256]{1,0:T(8,128)S(1)}, f32[8,256]{1,0:T(8,128)S(1)}) custom-call(f32[1,12]{1,0:T(1,128)S(1)} %bitcast.7, f32[192,128]{1,0:T(8,128)S(1)} %get-tuple-element.38.own_ref, f32[192,128]{1,0:T(8,128)S(1)} %collective-permute-done.core_ref, f32[192,128]{1,0:T(8,128)S(1)} %collective-permute-done.1.chip_ref, ...), custom_call_target="tpu_custom_call" | custom-call | tf_op jit(solution)/shard_map/edges/pallas_call | solution.py:529
  9.0 0.5 %collective-permute-start.2 = (f32[8,256]{1,0:T(8,128)S(1)}, f32[8,256]{1,0:T(8,128)S(1)}, u32[]{:S(2)}, u32[]{:S(2)}) collective-permute-start(f32[8,256]{1,0:T(8,128)S(1)} %get-tuple-element.45), channel_id=1, source_target_pairs={{0,1},{1,0},{2,3},{3,2},{4,5},{5,4},{6,7},{7,6},{8,9},{9,8},{10,11... | collective-permute-start | bytes 24584 | tf_op jit(solution)/shard_map/ppermute | solution.py:515
  9.5 1.9 %collective-permute-start.3 = (f32[8,256]{1,0:T(8,128)S(1)}, f32[8,256]{1,0:T(8,128)S(1)}, u32[]{:S(2)}, u32[]{:S(2)}) collective-permute-start(f32[8,256]{1,0:T(8,128)S(1)} %get-tuple-element.46), channel_id=1, source_target_pairs={{1,2},{2,1},{3,4},{4,3},{5,6},{6,5},{7,8},{8,7},{9,10},{10,9},{11,... | collective-permute-start | bytes 24584 | tf_op jit(solution)/shard_map/ppermute | solution.py:511
  11.4 0.0 collective-permute-done.4.chip_coords_ref
  11.4 0.0 collective-permute-done.5.core_coords_ref
  11.4 1.6 %prepare.1 = (bf16[16,256,256]{2,1,0:T(8,128)(2,1)S(1)}, f32[16,32,256]{2,1,0:T(8,128)S(1)}, f32[16,48,256]{2,1,0:T(8,128)S(1)}, bf16[16,256,256]{2,1,0:T(8,128)...) custom-call(f32[32,256]{1,0:T(8,128)S(1)} %collective-permute-done.4.chip_coords_ref, ...), custom_call_target="tpu_custom_call" | custom-call | tf_op jit(solution)/shard_map/prepare/pallas_call | solution.py:529
  13.0 1.4 %imaging.1.intensity_ref = bf16[256,256]{1,0:T(8,128)(2,1)S(1)} custom-call(f32[1,12]{1,0:T(1,128)S(1)} %bitcast.8, bf16[192,1536]{1,0:T(8,128)(2,1)S(1)} %get-tuple-element.43.product_ref, bf16[512,192]{1,0:T(8,128)(2,1)S(1)} %get-tuple-element.44.inverse_ref, bf16[256,512]{1,0:T(8,128)(2,1)S(1)} %get-tuple-element.42.spread_ref), custom_call_target="tpu_custom_call" | custom-call | tf_op jit(solution)/shard_map/imaging/pallas_call | solution.py:529
  14.4 0.0 collective-permute-done.2.core_ref
  14.4 0.0 collective-permute-done.3.chip_ref
  14.4 1.4 %resist.1 = (bf16[256,512]{1,0:T(8,128)(2,1)S(1)}, bf16[272,256]{1,0:T(8,128)(2,1)S(1)}, f32[8,128]{1,0:T(8,128)S(1)}, f32[8,256]{1,0:T(8,128)S(1)}) custom-call(bf16[256,256]{1,0:T(8,128)(2,1)S(1)} %imaging.1.intensity_ref, f32[8,256]{1,0:T(8,128)S(1)} %collective-permute-done.2.core_ref, f32[8,256]{1,0:T(8,128)S(1)} %collective-permute-done.3.chip_ref, ...), custom_call_target="tpu_custom_call" | custom-call | tf_op jit(solution)/shard_map/resist/pallas_call | solution.py:529
  15.8 0.0 copy-start.1
  15.8 0.7 %collective-permute-start.7 = (f32[8,256]{1,0:T(8,128)S(1)}, f32[8,256]{1,0:T(8,128)S(1)}, u32[]{:S(2)}, u32[]{:S(2)}) collective-permute-start(f32[8,256]{1,0:T(8,128)S(1)} %get-tuple-element.65), channel_id=1, source_target_pairs={{1,2},{2,1},{3,4},{4,3},{5,6},{6,5},{7,8},{8,7},{9,10},{10,9},{11,... | collective-permute-start | bytes 24584 | tf_op jit(solution)/shard_map/ppermute | solution.py:511
  16.5 0.9 %mean_core.1 = f32[8,256]{1,0:T(8,128)S(1)} custom-call(bf16[272,256]{1,0:T(8,128)(2,1)S(1)} %get-tuple-element.53.table_ref, bf16[16,256,256]{2,1,0:T(8,128)(2,1)S(1)} %get-tuple-element.62.tents_ref, f32[16,32,256]{2,1,0:T(8,128)S(1)} %get-tuple-element.63.spin_ref, f32[16,48,256]{2,1,0:T(8,128)S(1)} %get-tuple-element.64.ends_ref, ...), custom_call_target="tpu_custom_call" | custom-call | tf_op jit(solution)/shard_map/mean_core/pallas_call | solution.py:529
  17.4 0.2 collective-permute-start.6
  17.6 1.6 %mean_own.1 = (f32[256,1024]{1,0:T(8,128)}, f32[8,256]{1,0:T(8,128)S(1)}) custom-call(bf16[256,512]{1,0:T(8,128)(2,1)S(1)} %get-tuple-element.52.parts_ref, bf16[256,1024]{1,0:T(8,128)(2,1)S(1)} %copy-done.1, bf16[272,256]{1,0:T(8,128)(2,1)S(1)} %get-tuple-element.53.table_ref, bf16[16,256,256]{2,1,0:T(8,128)(2,1)S(1)} %get-tuple-element.54.tents_ref, ...), custom_call_target="tpu_custom_call" | custom-call | tf_op jit(solution)/shard_map/mean_own/pallas_call | solution.py:529
  19.3 0.3 %collective-permute-done.7.chip_ref = f32[8,256]{1,0:T(8,128)S(1)} collective-permute-done((f32[8,256]{1,0:T(8,128)S(1)}, f32[8,256]{1,0:T(8,128)S(1)}, u32[]{:S(2)}, u32[]{:S(2)}) %collective-permute-start.7) | collective-permute-done | bytes 8224 | tf_op jit(solution)/shard_map/ppermute | solution.py:511
  19.5 0.0 collective-permute-done.6.core_ref
  19.5 0.7 %bias.1 = f32[1,512]{1,0:T(1,128)} custom-call(f32[8,128]{1,0:T(8,128)S(1)} %get-tuple-element.59.level_ref, s32[1,512]{1,0:T(1,128)S(1)} %get-tuple-element.60.places_ref, f32[8,256]{1,0:T(8,128)S(1)} %get-tuple-element.61.own_ref, f32[8,256]{1,0:T(8,128)S(1)} %collective-permute-done.6.core_ref, f32[8,256]{1,0:T(8,128)S(1)} %collective-permute-done.7.chip_ref, ...), custom_call_target="tpu_custom_call" | custom-call | tf_op jit(solution)/shard_map/bias/pallas_call | solution.py:529
  (8 shorter events, 0.0 us)
Async XLA Ops:
  0.6 7.8 %copy-start.5 = (f32[12]{0:T(128)S(1)}, f32[12]{0:T(128)}, u32[]{:S(2)}) copy-start(f32[12]{0:T(128)} %param.19) | copy-start | bytes 148
  0.6 7.8 %copy-start = (f32[2,96,12,128]{3,1,2,0:T(8,128)S(1)}, f32[2,96,12,128]{3,1,2,0:T(8,128)}, u32[]{:S(2)}) copy-start(f32[2,96,12,128]{3,1,2,0:T(8,128)} %param.18) | copy-start | bytes 3538948
  2.6 11.8 %copy-start.2 = (bf16[272,512]{1,0:T(8,128)(2,1)S(1)}, bf16[272,512]{1,0:T(8,128)(2,1)}, u32[]{:S(2)}) copy-start(bf16[272,512]{1,0:T(8,128)(2,1)} %constant.28.clone.waves_ref) | copy-start | bytes 835588
  2.6 11.8 %copy-start.3 = (bf16[256,256]{1,0:T(8,128)(2,1)S(1)}, bf16[256,256]{1,0:T(8,128)(2,1)}, u32[]{:S(2)}) copy-start(bf16[256,256]{1,0:T(8,128)(2,1)} %constant.26.clone.inner_ref) | copy-start | bytes 393220
  2.6 11.8 %copy-start.4 = (bf16[256,16]{1,0:T(8,128)(2,1)S(1)}, bf16[256,16]{1,0:T(8,128)(2,1)}, u32[]{:S(2)}) copy-start(bf16[256,16]{1,0:T(8,128)(2,1)} %constant.27.clone.outer_ref) | copy-start | bytes 24580
  2.7 5.8 %collective-permute-start = (f32[192,128]{1,0:T(8,128)S(1)}, f32[192,128]{1,0:T(8,128)S(1)}, u32[]{:S(2)}, u32[]{:S(2)}) collective-permute-start(f32[192,128]{1,0:T(8,128)S(1)} %get-tuple-element.39), channel_id=1, source_target_pairs={{0,1},{1,0},{2,3},{3,2},{4,5},{5,4},{6,7},{7,6},{8,9},{9,8},{10,11... | collective-permute-start | bytes 294920 | tf_op jit(solution)/shard_map/ppermute | solution.py:515
  3.2 5.2 %collective-permute-start.1 = (f32[192,128]{1,0:T(8,128)S(1)}, f32[192,128]{1,0:T(8,128)S(1)}, u32[]{:S(2)}, u32[]{:S(2)}) collective-permute-start(f32[192,128]{1,0:T(8,128)S(1)} %get-tuple-element.40), channel_id=1, source_target_pairs={{1,2},{2,1},{3,4},{4,3},{5,6},{6,5},{7,8},{8,7},{9,10},{10,9},{11,... | collective-permute-start | bytes 294920 | tf_op jit(solution)/shard_map/ppermute | solution.py:511
  6.4 5.0 %collective-permute-start.4 = (f32[32,256]{1,0:T(8,128)S(1)}, f32[32,256]{1,0:T(8,128)S(1)}, u32[]{:S(2)}, u32[]{:S(2)}) collective-permute-start(f32[32,256]{1,0:T(8,128)S(1)} %get-tuple-element.47), channel_id=1, source_target_pairs={{1,2},{2,1},{3,4},{4,3},{5,6},{6,5},{7,8},{8,7},{9,10},{10,9},{11,... | collective-permute-start | bytes 98312 | tf_op jit(solution)/shard_map/ppermute | solution.py:511
  6.5 5.0 %collective-permute-start.5 = (f32[32,256]{1,0:T(8,128)S(1)}, f32[32,256]{1,0:T(8,128)S(1)}, u32[]{:S(2)}, u32[]{:S(2)}) collective-permute-start(f32[32,256]{1,0:T(8,128)S(1)} %get-tuple-element.48), channel_id=1, source_target_pairs={{0,1},{1,0},{2,3},{3,2},{4,5},{5,4},{6,7},{7,6},{8,9},{9,8},{10,11... | collective-permute-start | bytes 98312 | tf_op jit(solution)/shard_map/ppermute | solution.py:515
  9.0 5.4 %collective-permute-start.2 = (f32[8,256]{1,0:T(8,128)S(1)}, f32[8,256]{1,0:T(8,128)S(1)}, u32[]{:S(2)}, u32[]{:S(2)}) collective-permute-start(f32[8,256]{1,0:T(8,128)S(1)} %get-tuple-element.45), channel_id=1, source_target_pairs={{0,1},{1,0},{2,3},{3,2},{4,5},{5,4},{6,7},{7,6},{8,9},{9,8},{10,11... | collective-permute-start | bytes 24584 | tf_op jit(solution)/shard_map/ppermute | solution.py:515
  9.5 4.9 %collective-permute-start.3 = (f32[8,256]{1,0:T(8,128)S(1)}, f32[8,256]{1,0:T(8,128)S(1)}, u32[]{:S(2)}, u32[]{:S(2)}) collective-permute-start(f32[8,256]{1,0:T(8,128)S(1)} %get-tuple-element.46), channel_id=1, source_target_pairs={{1,2},{2,1},{3,4},{4,3},{5,6},{6,5},{7,8},{8,7},{9,10},{10,9},{11,... | collective-permute-start | bytes 24584 | tf_op jit(solution)/shard_map/ppermute | solution.py:511
  15.8 1.9 %copy-start.1 = (bf16[256,1024]{1,0:T(8,128)(2,1)S(1)}, bf16[256,1024]{1,0:T(8,128)(2,1)}, u32[]{:S(2)}) copy-start(bf16[256,1024]{1,0:T(8,128)(2,1)} %constant.29.clone.operator_ref) | copy-start | bytes 1572868
  15.8 3.7 %collective-permute-start.7 = (f32[8,256]{1,0:T(8,128)S(1)}, f32[8,256]{1,0:T(8,128)S(1)}, u32[]{:S(2)}, u32[]{:S(2)}) collective-permute-start(f32[8,256]{1,0:T(8,128)S(1)} %get-tuple-element.65), channel_id=1, source_target_pairs={{1,2},{2,1},{3,4},{4,3},{5,6},{6,5},{7,8},{8,7},{9,10},{10,9},{11,... | collective-permute-start | bytes 24584 | tf_op jit(solution)/shard_map/ppermute | solution.py:511
  17.4 2.1 %collective-permute-start.6 = (f32[8,256]{1,0:T(8,128)S(1)}, f32[8,256]{1,0:T(8,128)S(1)}, u32[]{:S(2)}, u32[]{:S(2)}) collective-permute-start(f32[8,256]{1,0:T(8,128)S(1)} %mean_core.1), channel_id=1, source_target_pairs={{0,1},{1,0},{2,3},{3,2},{4,5},{5,4},{6,7},{7,6},{8,9},{9,8},{10,11... | collective-permute-start | bytes 24584 | tf_op jit(solution)/shard_map/ppermute | solution.py:515
  17.6 1.9 %copy-start.6 = (s32[512]{0:T(512)S(1)}, s32[512]{0:T(512)}, u32[]{:S(2)}) copy-start(s32[512]{0:T(512)} %param.23) | copy-start | bytes 6148

commit v10 on v9

--- a/solution.py
+++ b/solution.py
@@ -180,8 +180,6 @@
     spectra_ref, core_ref, chip_ref, eval_ref, records_ref,
     mask_ref, forward_ref, rows_ref, sems,
 ):
-    depth = mask_ref.shape[1] // 2
-    parts = [pl.ds(i * depth, depth) for i in range(2)]
     copies = started(
         sems,
         (mask_hbm, mask_ref),
@@ -406,7 +404,7 @@
         total += (sums[0] * ends(0) - sums[1] * ends(1)) + (sums[2] * ends(2) - sums[3] * ends(3))
         total += rows[4 * pairs + 4] * ends(4) + rows[4 * pairs + 5] * ends(5)
     mean = middle + jnp.sum(total, axis=0, keepdims=True) * (1.0 / SITES)
-    return jnp.broadcast_to(mean, (8, slots))
+    return mean
 
 
 def resist_kernel(
@@ -475,7 +473,11 @@
     odd = parity() == 1
     core, chip = core_ref[...], chip_ref[...]
     means = (jnp.where(odd, core, chip), own_ref[...], jnp.where(odd, chip, core))
-    means = [part[:, i : i + 128] for part in means for i in range(0, part.shape[1], 128)]
+    means = [
+        jnp.broadcast_to(part[:, i : i + 128], (8, 128))
+        for part in means
+        for i in range(0, part.shape[1], 128)
+    ]
     found = []
     for start in range(0, out_ref.shape[1], 128):
         place = jnp.broadcast_to(places_ref[:, start : start + 128], (8, 128))
@@ -555,7 +557,7 @@
     spectrum = ((2 * row_freqs, col_freqs), F32)
     packed = ((records, capacity), F32)
     edge = ((BLUR_REACH, samples), F32)
-    means = ((8, capacity), F32)
+    means = ((1, capacity), F32)
     site_shapes = [
         ((SITES, tile_rows, capacity), BF16),
         ((SITES, col_freqs // 4, capacity), F32),

time: 20.4 us -> 20.4 us (level)
  no operation moved by 1% of the time
where the time goes in v10:
time: 20.4 us; the launch traced here: 20.1 us
  Pallas kernels  11.8 us (58%)
  starting transfers between devices  6.67 us (33%)
  between operations  1.46 us (7%)
  waiting for transfers between devices  0.22 us (1%)
    pallas_call x10, Pallas kernels, call(): pl.pallas_call(kernel, out_shape=[jax.ShapeDtypeStruct(s, d) for s, d in...  11.8 us
    ppermute x4, starting transfers between devices, swap_chips(): return lax.ppermute(to_chip, ('groups', 'tx'), pairs)  5.32 us
    ppermute x4, starting transfers between devices, swap_cores(): lax.ppermute(to_core, 'tx', [(i, i ^ 1) for i in range(lax.axis_size('tx'...  1.35 us
  transfers between devices with their start and end apart: 8, of which 1 were waited for; matrix products, arithmetic and copies ran while one was open for 0% of the time, Pallas kernels for 38%

profile of v10, /device:TPU:0, one launch (start us, length us, event | category | flops | bytes accessed | tf_op | source)
XLA Modules:
  0.0 20.1 jit_solution(1596863838377707460)
XLA Ops:
  0.6 0.0 copy-start.5
  0.6 0.0 copy-start
  0.7 2.0 %front.1 = (bf16[256,256]{1,0:T(8,128)(2,1)S(1)}, f32[192,128]{1,0:T(8,128)S(1)}, f32[192,128]{1,0:T(8,128)S(1)}, s32[1,512]{1,0:T(1,128)S(1)}, f32[32,512]{1,0:T(8,128)S(1)}) custom-call(bf16[256,1024]{1,0:T(8,128)(2,1)} %mask_hbm.1, bf16[1024,256]{1,0:T(8,128)(2,1)} %constant.20.clone.forward_hbm, bf16[384,256]{1,0:T(8,128)(2,1)} %constant.21.clone.rows_hbm, ...), custom_call_target="tpu_custom_call" | custom-call | tf_op jit(solution)/shard_map/front/pallas_call | solution.py:531
  2.6 0.0 copy-start.2
  2.6 0.0 copy-start.3
  2.6 0.0 copy-start.4
  2.7 0.5 %collective-permute-start = (f32[192,128]{1,0:T(8,128)S(1)}, f32[192,128]{1,0:T(8,128)S(1)}, u32[]{:S(2)}, u32[]{:S(2)}) collective-permute-start(f32[192,128]{1,0:T(8,128)S(1)} %get-tuple-element.39), channel_id=1, source_target_pairs={{0,1},{1,0},{2,3},{3,2},{4,5},{5,4},{6,7},{7,6},{8,9},{9,8},{10,11... | collective-permute-start | bytes 294920 | tf_op jit(solution)/shard_map/ppermute | solution.py:517
  3.2 2.6 %collective-permute-start.1 = (f32[192,128]{1,0:T(8,128)S(1)}, f32[192,128]{1,0:T(8,128)S(1)}, u32[]{:S(2)}, u32[]{:S(2)}) collective-permute-start(f32[192,128]{1,0:T(8,128)S(1)} %get-tuple-element.40), channel_id=1, source_target_pairs={{1,2},{2,1},{3,4},{4,3},{5,6},{6,5},{7,8},{8,7},{9,10},{10,9},{11,... | collective-permute-start | bytes 294920 | tf_op jit(solution)/shard_map/ppermute | solution.py:513
  5.8 0.6 %pack.1 = (f32[32,256]{1,0:T(8,128)S(1)}, f32[32,256]{1,0:T(8,128)S(1)}, f32[32,256]{1,0:T(8,128)S(1)}, s32[1,512]{1,0:T(1,128)S(1)}) custom-call(bf16[256,256]{1,0:T(8,128)(2,1)S(1)} %get-tuple-element.34.after_ref.spectra_ref, s32[1,512]{1,0:T(1,128)S(1)} %get-tuple-element.35.eval_ref, f32[32,512]{1,0:T(8,128)S(1)} %get-tuple-element.36.records_ref), custom_call_target="tpu_custom_call" | custom-call | tf_op jit(solution)/shard_map/pack/pallas_call | solution.py:531
  6.4 0.1 collective-permute-start.4
  6.5 0.1 collective-permute-start.5
  7.3 1.1 %load.1 = (f32[8,128]{1,0:T(8,128)S(1)}, f32[192,128]{1,0:T(8,128)S(1)}, bf16[512,192]{1,0:T(8,128)(2,1)S(1)}, bf16[32,192]{1,0:T(8,128)(2,1)S(1)}, bf16[256,512...) custom-call(bf16[256,256]{1,0:T(8,128)(2,1)S(1)} %get-tuple-element., ...), custom_call_target="tpu_custom_call" | custom-call | tf_op jit(solution)/shard_map/load/pallas_call | solution.py:531
  8.4 0.0 collective-permute-done.core_ref
  8.4 0.0 collective-permute-done.1.chip_ref
  8.4 0.5 %edges.1 = (bf16[192,1536]{1,0:T(8,128)(2,1)S(1)}, f32[8,256]{1,0:T(8,128)S(1)}, f32[8,256]{1,0:T(8,128)S(1)}) custom-call(f32[1,12]{1,0:T(1,128)S(1)} %bitcast.7, f32[192,128]{1,0:T(8,128)S(1)} %get-tuple-element.38.own_ref, f32[192,128]{1,0:T(8,128)S(1)} %collective-permute-done.core_ref, f32[192,128]{1,0:T(8,128)S(1)} %collective-permute-done.1.chip_ref, ...), custom_call_target="tpu_custom_call" | custom-call | tf_op jit(solution)/shard_map/edges/pallas_call | solution.py:531
  9.0 0.5 %collective-permute-start.2 = (f32[8,256]{1,0:T(8,128)S(1)}, f32[8,256]{1,0:T(8,128)S(1)}, u32[]{:S(2)}, u32[]{:S(2)}) collective-permute-start(f32[8,256]{1,0:T(8,128)S(1)} %get-tuple-element.45), channel_id=1, source_target_pairs={{0,1},{1,0},{2,3},{3,2},{4,5},{5,4},{6,7},{7,6},{8,9},{9,8},{10,11... | collective-permute-start | bytes 24584 | tf_op jit(solution)/shard_map/ppermute | solution.py:517
  9.5 1.9 %collective-permute-start.3 = (f32[8,256]{1,0:T(8,128)S(1)}, f32[8,256]{1,0:T(8,128)S(1)}, u32[]{:S(2)}, u32[]{:S(2)}) collective-permute-start(f32[8,256]{1,0:T(8,128)S(1)} %get-tuple-element.46), channel_id=1, source_target_pairs={{1,2},{2,1},{3,4},{4,3},{5,6},{6,5},{7,8},{8,7},{9,10},{10,9},{11,... | collective-permute-start | bytes 24584 | tf_op jit(solution)/shard_map/ppermute | solution.py:513
  11.4 0.0 collective-permute-done.4.chip_coords_ref
  11.4 0.0 collective-permute-done.5.core_coords_ref
  11.4 1.6 %prepare.1 = (bf16[16,256,256]{2,1,0:T(8,128)(2,1)S(1)}, f32[16,32,256]{2,1,0:T(8,128)S(1)}, f32[16,48,256]{2,1,0:T(8,128)S(1)}, bf16[16,256,256]{2,1,0:T(8,128)...) custom-call(f32[32,256]{1,0:T(8,128)S(1)} %collective-permute-done.4.chip_coords_ref, ...), custom_call_target="tpu_custom_call" | custom-call | tf_op jit(solution)/shard_map/prepare/pallas_call | solution.py:531
  13.0 1.4 %imaging.1.intensity_ref = bf16[256,256]{1,0:T(8,128)(2,1)S(1)} custom-call(f32[1,12]{1,0:T(1,128)S(1)} %bitcast.8, bf16[192,1536]{1,0:T(8,128)(2,1)S(1)} %get-tuple-element.43.product_ref, bf16[512,192]{1,0:T(8,128)(2,1)S(1)} %get-tuple-element.44.inverse_ref, bf16[256,512]{1,0:T(8,128)(2,1)S(1)} %get-tuple-element.42.spread_ref), custom_call_target="tpu_custom_call" | custom-call | tf_op jit(solution)/shard_map/imaging/pallas_call | solution.py:531
  14.4 0.0 collective-permute-done.2.core_ref
  14.4 0.0 collective-permute-done.3.chip_ref
  14.4 1.3 %resist.1 = (bf16[256,512]{1,0:T(8,128)(2,1)S(1)}, bf16[272,256]{1,0:T(8,128)(2,1)S(1)}, f32[8,128]{1,0:T(8,128)S(1)}, f32[1,256]{1,0:T(1,128)S(1)}) custom-call(bf16[256,256]{1,0:T(8,128)(2,1)S(1)} %imaging.1.intensity_ref, f32[8,256]{1,0:T(8,128)S(1)} %collective-permute-done.2.core_ref, f32[8,256]{1,0:T(8,128)S(1)} %collective-permute-done.3.chip_ref, ...), custom_call_target="tpu_custom_call" | custom-call | tf_op jit(solution)/shard_map/resist/pallas_call | solution.py:531
  15.8 0.0 copy-start.1
  15.8 0.7 %collective-permute-start.7 = (f32[1,256]{1,0:T(1,128)S(1)}, f32[1,256]{1,0:T(1,128)S(1)}, u32[]{:S(2)}, u32[]{:S(2)}) collective-permute-start(f32[1,256]{1,0:T(1,128)S(1)} %get-tuple-element.65), channel_id=1, source_target_pairs={{1,2},{2,1},{3,4},{4,3},{5,6},{6,5},{7,8},{8,7},{9,10},{10,9},{11,... | collective-permute-start | bytes 3080 | tf_op jit(solution)/shard_map/ppermute | solution.py:513
  16.5 0.9 %mean_core.1 = f32[1,256]{1,0:T(1,128)S(1)} custom-call(bf16[272,256]{1,0:T(8,128)(2,1)S(1)} %get-tuple-element.53.table_ref, bf16[16,256,256]{2,1,0:T(8,128)(2,1)S(1)} %get-tuple-element.62.tents_ref, f32[16,32,256]{2,1,0:T(8,128)S(1)} %get-tuple-element.63.spin_ref, f32[16,48,256]{2,1,0:T(8,128)S(1)} %get-tuple-element.64.ends_ref, ...), custom_call_target="tpu_custom_call" | custom-call | tf_op jit(solution)/shard_map/mean_core/pallas_call | solution.py:531
  17.4 0.2 collective-permute-start.6
  17.6 1.6 %mean_own.1 = (f32[256,1024]{1,0:T(8,128)}, f32[1,256]{1,0:T(1,128)S(1)}) custom-call(bf16[256,512]{1,0:T(8,128)(2,1)S(1)} %get-tuple-element.52.parts_ref, bf16[256,1024]{1,0:T(8,128)(2,1)S(1)} %copy-done.1, bf16[272,256]{1,0:T(8,128)(2,1)S(1)} %get-tuple-element.53.table_ref, bf16[16,256,256]{2,1,0:T(8,128)(2,1)S(1)} %get-tuple-element.54.tents_ref, ...), custom_call_target="tpu_custom_call" | custom-call | tf_op jit(solution)/shard_map/mean_own/pallas_call | solution.py:531
  19.2 0.2 %collective-permute-done.7.chip_ref = f32[1,256]{1,0:T(1,128)S(1)} collective-permute-done((f32[1,256]{1,0:T(1,128)S(1)}, f32[1,256]{1,0:T(1,128)S(1)}, u32[]{:S(2)}, u32[]{:S(2)}) %collective-permute-start.7) | collective-permute-done | bytes 1056 | tf_op jit(solution)/shard_map/ppermute | solution.py:513
  19.4 0.0 collective-permute-done.6.core_ref
  19.4 0.7 %bias.1 = f32[1,512]{1,0:T(1,128)} custom-call(f32[8,128]{1,0:T(8,128)S(1)} %get-tuple-element.59.level_ref, s32[1,512]{1,0:T(1,128)S(1)} %get-tuple-element.60.places_ref, f32[1,256]{1,0:T(1,128)S(1)} %get-tuple-element.61.own_ref, f32[1,256]{1,0:T(1,128)S(1)} %collective-permute-done.6.core_ref, f32[1,256]{1,0:T(1,128)S(1)} %collective-permute-done.7.chip_ref, ...), custom_call_target="tpu_custom_call" | custom-call | tf_op jit(solution)/shard_map/bias/pallas_call | solution.py:531
  (8 shorter events, 0.0 us)
Async XLA Ops:
  0.6 7.8 %copy-start.5 = (f32[12]{0:T(128)S(1)}, f32[12]{0:T(128)}, u32[]{:S(2)}) copy-start(f32[12]{0:T(128)} %param.19) | copy-start | bytes 148
  0.6 7.8 %copy-start = (f32[2,96,12,128]{3,1,2,0:T(8,128)S(1)}, f32[2,96,12,128]{3,1,2,0:T(8,128)}, u32[]{:S(2)}) copy-start(f32[2,96,12,128]{3,1,2,0:T(8,128)} %param.18) | copy-start | bytes 3538948
  2.6 11.8 %copy-start.2 = (bf16[272,512]{1,0:T(8,128)(2,1)S(1)}, bf16[272,512]{1,0:T(8,128)(2,1)}, u32[]{:S(2)}) copy-start(bf16[272,512]{1,0:T(8,128)(2,1)} %constant.28.clone.waves_ref) | copy-start | bytes 835588
  2.6 11.8 %copy-start.3 = (bf16[256,256]{1,0:T(8,128)(2,1)S(1)}, bf16[256,256]{1,0:T(8,128)(2,1)}, u32[]{:S(2)}) copy-start(bf16[256,256]{1,0:T(8,128)(2,1)} %constant.26.clone.inner_ref) | copy-start | bytes 393220
  2.6 11.8 %copy-start.4 = (bf16[256,16]{1,0:T(8,128)(2,1)S(1)}, bf16[256,16]{1,0:T(8,128)(2,1)}, u32[]{:S(2)}) copy-start(bf16[256,16]{1,0:T(8,128)(2,1)} %constant.27.clone.outer_ref) | copy-start | bytes 24580
  2.7 5.8 %collective-permute-start = (f32[192,128]{1,0:T(8,128)S(1)}, f32[192,128]{1,0:T(8,128)S(1)}, u32[]{:S(2)}, u32[]{:S(2)}) collective-permute-start(f32[192,128]{1,0:T(8,128)S(1)} %get-tuple-element.39), channel_id=1, source_target_pairs={{0,1},{1,0},{2,3},{3,2},{4,5},{5,4},{6,7},{7,6},{8,9},{9,8},{10,11... | collective-permute-start | bytes 294920 | tf_op jit(solution)/shard_map/ppermute | solution.py:517
  3.2 5.2 %collective-permute-start.1 = (f32[192,128]{1,0:T(8,128)S(1)}, f32[192,128]{1,0:T(8,128)S(1)}, u32[]{:S(2)}, u32[]{:S(2)}) collective-permute-start(f32[192,128]{1,0:T(8,128)S(1)} %get-tuple-element.40), channel_id=1, source_target_pairs={{1,2},{2,1},{3,4},{4,3},{5,6},{6,5},{7,8},{8,7},{9,10},{10,9},{11,... | collective-permute-start | bytes 294920 | tf_op jit(solution)/shard_map/ppermute | solution.py:513
  6.4 5.0 %collective-permute-start.4 = (f32[32,256]{1,0:T(8,128)S(1)}, f32[32,256]{1,0:T(8,128)S(1)}, u32[]{:S(2)}, u32[]{:S(2)}) collective-permute-start(f32[32,256]{1,0:T(8,128)S(1)} %get-tuple-element.47), channel_id=1, source_target_pairs={{1,2},{2,1},{3,4},{4,3},{5,6},{6,5},{7,8},{8,7},{9,10},{10,9},{11,... | collective-permute-start | bytes 98312 | tf_op jit(solution)/shard_map/ppermute | solution.py:513
  6.5 5.0 %collective-permute-start.5 = (f32[32,256]{1,0:T(8,128)S(1)}, f32[32,256]{1,0:T(8,128)S(1)}, u32[]{:S(2)}, u32[]{:S(2)}) collective-permute-start(f32[32,256]{1,0:T(8,128)S(1)} %get-tuple-element.48), channel_id=1, source_target_pairs={{0,1},{1,0},{2,3},{3,2},{4,5},{5,4},{6,7},{7,6},{8,9},{9,8},{10,11... | collective-permute-start | bytes 98312 | tf_op jit(solution)/shard_map/ppermute | solution.py:517
  9.0 5.4 %collective-permute-start.2 = (f32[8,256]{1,0:T(8,128)S(1)}, f32[8,256]{1,0:T(8,128)S(1)}, u32[]{:S(2)}, u32[]{:S(2)}) collective-permute-start(f32[8,256]{1,0:T(8,128)S(1)} %get-tuple-element.45), channel_id=1, source_target_pairs={{0,1},{1,0},{2,3},{3,2},{4,5},{5,4},{6,7},{7,6},{8,9},{9,8},{10,11... | collective-permute-start | bytes 24584 | tf_op jit(solution)/shard_map/ppermute | solution.py:517
  9.5 4.9 %collective-permute-start.3 = (f32[8,256]{1,0:T(8,128)S(1)}, f32[8,256]{1,0:T(8,128)S(1)}, u32[]{:S(2)}, u32[]{:S(2)}) collective-permute-start(f32[8,256]{1,0:T(8,128)S(1)} %get-tuple-element.46), channel_id=1, source_target_pairs={{1,2},{2,1},{3,4},{4,3},{5,6},{6,5},{7,8},{8,7},{9,10},{10,9},{11,... | collective-permute-start | bytes 24584 | tf_op jit(solution)/shard_map/ppermute | solution.py:513
  15.8 1.8 %copy-start.1 = (bf16[256,1024]{1,0:T(8,128)(2,1)S(1)}, bf16[256,1024]{1,0:T(8,128)(2,1)}, u32[]{:S(2)}) copy-start(bf16[256,1024]{1,0:T(8,128)(2,1)} %constant.29.clone.operator_ref) | copy-start | bytes 1572868
  15.8 3.6 %collective-permute-start.7 = (f32[1,256]{1,0:T(1,128)S(1)}, f32[1,256]{1,0:T(1,128)S(1)}, u32[]{:S(2)}, u32[]{:S(2)}) collective-permute-start(f32[1,256]{1,0:T(1,128)S(1)} %get-tuple-element.65), channel_id=1, source_target_pairs={{1,2},{2,1},{3,4},{4,3},{5,6},{6,5},{7,8},{8,7},{9,10},{10,9},{11,... | collective-permute-start | bytes 3080 | tf_op jit(solution)/shard_map/ppermute | solution.py:513
  17.4 2.0 %collective-permute-start.6 = (f32[1,256]{1,0:T(1,128)S(1)}, f32[1,256]{1,0:T(1,128)S(1)}, u32[]{:S(2)}, u32[]{:S(2)}) collective-permute-start(f32[1,256]{1,0:T(1,128)S(1)} %mean_core.1), channel_id=1, source_target_pairs={{0,1},{1,0},{2,3},{3,2},{4,5},{5,4},{6,7},{7,6},{8,9},{9,8},{10,11... | collective-permute-start | bytes 3080 | tf_op jit(solution)/shard_map/ppermute | solution.py:517
  17.6 1.8 %copy-start.6 = (s32[512]{0:T(512)S(1)}, s32[512]{0:T(512)}, u32[]{:S(2)}) copy-start(s32[512]{0:T(512)} %param.23) | copy-start | bytes 6148

commit v11 on v10

--- a/solution.py
+++ b/solution.py
@@ -21,7 +21,7 @@
 F32 = jnp.float32
 BF16 = jnp.bfloat16
 SINE = (1.57079628989, -0.645963358138, 0.0796884742403, -0.0046722194159, 0.000150816735945)
-COSINE = (0.99999999978, -1.23370053428, 0.253669322509, -0.0208626876045, 0.000917723911039, -2.38245358719e-05)
+COSINE = (0.999999953341, -1.23369820859, 0.25365071182, -0.0208105729184, 0.000858162571361)
 VMEM_BYTES = 32 * 1024 * 1024
 
 

time: 20.4 us -> 20.3 us (level)
  no operation moved by 1% of the time
where the time goes in v11:
time: 20.3 us; the launch traced here: 20.1 us
  Pallas kernels  11.7 us (58%)
  starting transfers between devices  6.7 us (33%)
  between operations  1.46 us (7%)
    pallas_call x10, Pallas kernels, call(): pl.pallas_call(kernel, out_shape=[jax.ShapeDtypeStruct(s, d) for s, d in...  11.7 us
    ppermute x4, starting transfers between devices, swap_chips(): return lax.ppermute(to_chip, ('groups', 'tx'), pairs)  5.35 us
    ppermute x4, starting transfers between devices, swap_cores(): lax.ppermute(to_core, 'tx', [(i, i ^ 1) for i in range(lax.axis_size('tx'...  1.35 us
  transfers between devices with their start and end apart: 8, of which 1 were waited for; matrix products, arithmetic and copies ran while one was open for 0% of the time, Pallas kernels for 38%

profile of v11, /device:TPU:0, one launch (start us, length us, event | category | flops | bytes accessed | tf_op | source)
XLA Modules:
  0.0 20.1 jit_solution(8675831028314070603)
XLA Ops:
  0.6 0.0 copy-start.5
  0.6 0.0 copy-start
  0.7 2.0 %front.1 = (bf16[256,256]{1,0:T(8,128)(2,1)S(1)}, f32[192,128]{1,0:T(8,128)S(1)}, f32[192,128]{1,0:T(8,128)S(1)}, s32[1,512]{1,0:T(1,128)S(1)}, f32[32,512]{1,0:T(8,128)S(1)}) custom-call(bf16[256,1024]{1,0:T(8,128)(2,1)} %mask_hbm.1, bf16[1024,256]{1,0:T(8,128)(2,1)} %constant.20.clone.forward_hbm, bf16[384,256]{1,0:T(8,128)(2,1)} %constant.21.clone.rows_hbm, ...), custom_call_target="tpu_custom_call" | custom-call | tf_op jit(solution)/shard_map/front/pallas_call | solution.py:531
  2.6 0.0 copy-start.2
  2.6 0.0 copy-start.3
  2.6 0.0 copy-start.4
  2.7 0.5 %collective-permute-start = (f32[192,128]{1,0:T(8,128)S(1)}, f32[192,128]{1,0:T(8,128)S(1)}, u32[]{:S(2)}, u32[]{:S(2)}) collective-permute-start(f32[192,128]{1,0:T(8,128)S(1)} %get-tuple-element.39), channel_id=1, source_target_pairs={{0,1},{1,0},{2,3},{3,2},{4,5},{5,4},{6,7},{7,6},{8,9},{9,8},{10,11... | collective-permute-start | bytes 294920 | tf_op jit(solution)/shard_map/ppermute | solution.py:517
  3.2 2.6 %collective-permute-start.1 = (f32[192,128]{1,0:T(8,128)S(1)}, f32[192,128]{1,0:T(8,128)S(1)}, u32[]{:S(2)}, u32[]{:S(2)}) collective-permute-start(f32[192,128]{1,0:T(8,128)S(1)} %get-tuple-element.40), channel_id=1, source_target_pairs={{1,2},{2,1},{3,4},{4,3},{5,6},{6,5},{7,8},{8,7},{9,10},{10,9},{11,... | collective-permute-start | bytes 294920 | tf_op jit(solution)/shard_map/ppermute | solution.py:513
  5.8 0.6 %pack.1 = (f32[32,256]{1,0:T(8,128)S(1)}, f32[32,256]{1,0:T(8,128)S(1)}, f32[32,256]{1,0:T(8,128)S(1)}, s32[1,512]{1,0:T(1,128)S(1)}) custom-call(bf16[256,256]{1,0:T(8,128)(2,1)S(1)} %get-tuple-element.34.after_ref.spectra_ref, s32[1,512]{1,0:T(1,128)S(1)} %get-tuple-element.35.eval_ref, f32[32,512]{1,0:T(8,128)S(1)} %get-tuple-element.36.records_ref), custom_call_target="tpu_custom_call" | custom-call | tf_op jit(solution)/shard_map/pack/pallas_call | solution.py:531
  6.4 0.1 collective-permute-start.4
  6.5 0.1 collective-permute-start.5
  7.3 1.1 %load.1 = (f32[8,128]{1,0:T(8,128)S(1)}, f32[192,128]{1,0:T(8,128)S(1)}, bf16[512,192]{1,0:T(8,128)(2,1)S(1)}, bf16[32,192]{1,0:T(8,128)(2,1)S(1)}, bf16[256,512...) custom-call(bf16[256,256]{1,0:T(8,128)(2,1)S(1)} %get-tuple-element., ...), custom_call_target="tpu_custom_call" | custom-call | tf_op jit(solution)/shard_map/load/pallas_call | solution.py:531
  8.4 0.0 collective-permute-done.core_ref
  8.4 0.0 collective-permute-done.1.chip_ref
  8.4 0.5 %edges.1 = (bf16[192,1536]{1,0:T(8,128)(2,1)S(1)}, f32[8,256]{1,0:T(8,128)S(1)}, f32[8,256]{1,0:T(8,128)S(1)}) custom-call(f32[1,12]{1,0:T(1,128)S(1)} %bitcast.7, f32[192,128]{1,0:T(8,128)S(1)} %get-tuple-element.38.own_ref, f32[192,128]{1,0:T(8,128)S(1)} %collective-permute-done.core_ref, f32[192,128]{1,0:T(8,128)S(1)} %collective-permute-done.1.chip_ref, ...), custom_call_target="tpu_custom_call" | custom-call | tf_op jit(solution)/shard_map/edges/pallas_call | solution.py:531
  9.0 0.5 %collective-permute-start.2 = (f32[8,256]{1,0:T(8,128)S(1)}, f32[8,256]{1,0:T(8,128)S(1)}, u32[]{:S(2)}, u32[]{:S(2)}) collective-permute-start(f32[8,256]{1,0:T(8,128)S(1)} %get-tuple-element.45), channel_id=1, source_target_pairs={{0,1},{1,0},{2,3},{3,2},{4,5},{5,4},{6,7},{7,6},{8,9},{9,8},{10,11... | collective-permute-start | bytes 24584 | tf_op jit(solution)/shard_map/ppermute | solution.py:517
  9.5 1.9 %collective-permute-start.3 = (f32[8,256]{1,0:T(8,128)S(1)}, f32[8,256]{1,0:T(8,128)S(1)}, u32[]{:S(2)}, u32[]{:S(2)}) collective-permute-start(f32[8,256]{1,0:T(8,128)S(1)} %get-tuple-element.46), channel_id=1, source_target_pairs={{1,2},{2,1},{3,4},{4,3},{5,6},{6,5},{7,8},{8,7},{9,10},{10,9},{11,... | collective-permute-start | bytes 24584 | tf_op jit(solution)/shard_map/ppermute | solution.py:513
  11.4 0.0 collective-permute-done.4.chip_coords_ref
  11.4 0.0 collective-permute-done.5.core_coords_ref
  11.4 1.5 %prepare.1 = (bf16[16,256,256]{2,1,0:T(8,128)(2,1)S(1)}, f32[16,32,256]{2,1,0:T(8,128)S(1)}, f32[16,48,256]{2,1,0:T(8,128)S(1)}, bf16[16,256,256]{2,1,0:T(8,128)...) custom-call(f32[32,256]{1,0:T(8,128)S(1)} %collective-permute-done.4.chip_coords_ref, ...), custom_call_target="tpu_custom_call" | custom-call | tf_op jit(solution)/shard_map/prepare/pallas_call | solution.py:531
  13.0 1.4 %imaging.1.intensity_ref = bf16[256,256]{1,0:T(8,128)(2,1)S(1)} custom-call(f32[1,12]{1,0:T(1,128)S(1)} %bitcast.8, bf16[192,1536]{1,0:T(8,128)(2,1)S(1)} %get-tuple-element.43.product_ref, bf16[512,192]{1,0:T(8,128)(2,1)S(1)} %get-tuple-element.44.inverse_ref, bf16[256,512]{1,0:T(8,128)(2,1)S(1)} %get-tuple-element.42.spread_ref), custom_call_target="tpu_custom_call" | custom-call | tf_op jit(solution)/shard_map/imaging/pallas_call | solution.py:531
  14.3 0.0 collective-permute-done.2.core_ref
  14.4 0.0 collective-permute-done.3.chip_ref
  14.4 1.3 %resist.1 = (bf16[256,512]{1,0:T(8,128)(2,1)S(1)}, bf16[272,256]{1,0:T(8,128)(2,1)S(1)}, f32[8,128]{1,0:T(8,128)S(1)}, f32[1,256]{1,0:T(1,128)S(1)}) custom-call(bf16[256,256]{1,0:T(8,128)(2,1)S(1)} %imaging.1.intensity_ref, f32[8,256]{1,0:T(8,128)S(1)} %collective-permute-done.2.core_ref, f32[8,256]{1,0:T(8,128)S(1)} %collective-permute-done.3.chip_ref, ...), custom_call_target="tpu_custom_call" | custom-call | tf_op jit(solution)/shard_map/resist/pallas_call | solution.py:531
  15.7 0.0 copy-start.1
  15.8 0.7 %collective-permute-start.7 = (f32[1,256]{1,0:T(1,128)S(1)}, f32[1,256]{1,0:T(1,128)S(1)}, u32[]{:S(2)}, u32[]{:S(2)}) collective-permute-start(f32[1,256]{1,0:T(1,128)S(1)} %get-tuple-element.65), channel_id=1, source_target_pairs={{1,2},{2,1},{3,4},{4,3},{5,6},{6,5},{7,8},{8,7},{9,10},{10,9},{11,... | collective-permute-start | bytes 3080 | tf_op jit(solution)/shard_map/ppermute | solution.py:513
  16.5 0.9 %mean_core.1 = f32[1,256]{1,0:T(1,128)S(1)} custom-call(bf16[272,256]{1,0:T(8,128)(2,1)S(1)} %get-tuple-element.53.table_ref, bf16[16,256,256]{2,1,0:T(8,128)(2,1)S(1)} %get-tuple-element.62.tents_ref, f32[16,32,256]{2,1,0:T(8,128)S(1)} %get-tuple-element.63.spin_ref, f32[16,48,256]{2,1,0:T(8,128)S(1)} %get-tuple-element.64.ends_ref, ...), custom_call_target="tpu_custom_call" | custom-call | tf_op jit(solution)/shard_map/mean_core/pallas_call | solution.py:531
  17.4 0.2 collective-permute-start.6
  17.6 1.6 %mean_own.1 = (f32[256,1024]{1,0:T(8,128)}, f32[1,256]{1,0:T(1,128)S(1)}) custom-call(bf16[256,512]{1,0:T(8,128)(2,1)S(1)} %get-tuple-element.52.parts_ref, bf16[256,1024]{1,0:T(8,128)(2,1)S(1)} %copy-done.1, bf16[272,256]{1,0:T(8,128)(2,1)S(1)} %get-tuple-element.53.table_ref, bf16[16,256,256]{2,1,0:T(8,128)(2,1)S(1)} %get-tuple-element.54.tents_ref, ...), custom_call_target="tpu_custom_call" | custom-call | tf_op jit(solution)/shard_map/mean_own/pallas_call | solution.py:531
  19.2 0.2 collective-permute-done.7.chip_ref
  19.4 0.0 collective-permute-done.6.core_ref
  19.4 0.7 %bias.1 = f32[1,512]{1,0:T(1,128)} custom-call(f32[8,128]{1,0:T(8,128)S(1)} %get-tuple-element.59.level_ref, s32[1,512]{1,0:T(1,128)S(1)} %get-tuple-element.60.places_ref, f32[1,256]{1,0:T(1,128)S(1)} %get-tuple-element.61.own_ref, f32[1,256]{1,0:T(1,128)S(1)} %collective-permute-done.6.core_ref, f32[1,256]{1,0:T(1,128)S(1)} %collective-permute-done.7.chip_ref, ...), custom_call_target="tpu_custom_call" | custom-call | tf_op jit(solution)/shard_map/bias/pallas_call | solution.py:531
  (8 shorter events, 0.0 us)
Async XLA Ops:
  0.6 7.8 %copy-start.5 = (f32[12]{0:T(128)S(1)}, f32[12]{0:T(128)}, u32[]{:S(2)}) copy-start(f32[12]{0:T(128)} %param.19) | copy-start | bytes 148
  0.6 7.8 %copy-start = (f32[2,96,12,128]{3,1,2,0:T(8,128)S(1)}, f32[2,96,12,128]{3,1,2,0:T(8,128)}, u32[]{:S(2)}) copy-start(f32[2,96,12,128]{3,1,2,0:T(8,128)} %param.18) | copy-start | bytes 3538948
  2.6 11.8 %copy-start.2 = (bf16[272,512]{1,0:T(8,128)(2,1)S(1)}, bf16[272,512]{1,0:T(8,128)(2,1)}, u32[]{:S(2)}) copy-start(bf16[272,512]{1,0:T(8,128)(2,1)} %constant.28.clone.waves_ref) | copy-start | bytes 835588
  2.6 11.7 %copy-start.3 = (bf16[256,256]{1,0:T(8,128)(2,1)S(1)}, bf16[256,256]{1,0:T(8,128)(2,1)}, u32[]{:S(2)}) copy-start(bf16[256,256]{1,0:T(8,128)(2,1)} %constant.26.clone.inner_ref) | copy-start | bytes 393220
  2.6 11.7 %copy-start.4 = (bf16[256,16]{1,0:T(8,128)(2,1)S(1)}, bf16[256,16]{1,0:T(8,128)(2,1)}, u32[]{:S(2)}) copy-start(bf16[256,16]{1,0:T(8,128)(2,1)} %constant.27.clone.outer_ref) | copy-start | bytes 24580
  2.7 5.8 %collective-permute-start = (f32[192,128]{1,0:T(8,128)S(1)}, f32[192,128]{1,0:T(8,128)S(1)}, u32[]{:S(2)}, u32[]{:S(2)}) collective-permute-start(f32[192,128]{1,0:T(8,128)S(1)} %get-tuple-element.39), channel_id=1, source_target_pairs={{0,1},{1,0},{2,3},{3,2},{4,5},{5,4},{6,7},{7,6},{8,9},{9,8},{10,11... | collective-permute-start | bytes 294920 | tf_op jit(solution)/shard_map/ppermute | solution.py:517
  3.2 5.2 %collective-permute-start.1 = (f32[192,128]{1,0:T(8,128)S(1)}, f32[192,128]{1,0:T(8,128)S(1)}, u32[]{:S(2)}, u32[]{:S(2)}) collective-permute-start(f32[192,128]{1,0:T(8,128)S(1)} %get-tuple-element.40), channel_id=1, source_target_pairs={{1,2},{2,1},{3,4},{4,3},{5,6},{6,5},{7,8},{8,7},{9,10},{10,9},{11,... | collective-permute-start | bytes 294920 | tf_op jit(solution)/shard_map/ppermute | solution.py:513
  6.4 5.0 %collective-permute-start.4 = (f32[32,256]{1,0:T(8,128)S(1)}, f32[32,256]{1,0:T(8,128)S(1)}, u32[]{:S(2)}, u32[]{:S(2)}) collective-permute-start(f32[32,256]{1,0:T(8,128)S(1)} %get-tuple-element.47), channel_id=1, source_target_pairs={{1,2},{2,1},{3,4},{4,3},{5,6},{6,5},{7,8},{8,7},{9,10},{10,9},{11,... | collective-permute-start | bytes 98312 | tf_op jit(solution)/shard_map/ppermute | solution.py:513
  6.5 5.0 %collective-permute-start.5 = (f32[32,256]{1,0:T(8,128)S(1)}, f32[32,256]{1,0:T(8,128)S(1)}, u32[]{:S(2)}, u32[]{:S(2)}) collective-permute-start(f32[32,256]{1,0:T(8,128)S(1)} %get-tuple-element.48), channel_id=1, source_target_pairs={{0,1},{1,0},{2,3},{3,2},{4,5},{5,4},{6,7},{7,6},{8,9},{9,8},{10,11... | collective-permute-start | bytes 98312 | tf_op jit(solution)/shard_map/ppermute | solution.py:517
  9.0 5.4 %collective-permute-start.2 = (f32[8,256]{1,0:T(8,128)S(1)}, f32[8,256]{1,0:T(8,128)S(1)}, u32[]{:S(2)}, u32[]{:S(2)}) collective-permute-start(f32[8,256]{1,0:T(8,128)S(1)} %get-tuple-element.45), channel_id=1, source_target_pairs={{0,1},{1,0},{2,3},{3,2},{4,5},{5,4},{6,7},{7,6},{8,9},{9,8},{10,11... | collective-permute-start | bytes 24584 | tf_op jit(solution)/shard_map/ppermute | solution.py:517
  9.5 4.9 %collective-permute-start.3 = (f32[8,256]{1,0:T(8,128)S(1)}, f32[8,256]{1,0:T(8,128)S(1)}, u32[]{:S(2)}, u32[]{:S(2)}) collective-permute-start(f32[8,256]{1,0:T(8,128)S(1)} %get-tuple-element.46), channel_id=1, source_target_pairs={{1,2},{2,1},{3,4},{4,3},{5,6},{6,5},{7,8},{8,7},{9,10},{10,9},{11,... | collective-permute-start | bytes 24584 | tf_op jit(solution)/shard_map/ppermute | solution.py:513
  15.7 1.9 %copy-start.1 = (bf16[256,1024]{1,0:T(8,128)(2,1)S(1)}, bf16[256,1024]{1,0:T(8,128)(2,1)}, u32[]{:S(2)}) copy-start(bf16[256,1024]{1,0:T(8,128)(2,1)} %constant.29.clone.operator_ref) | copy-start | bytes 1572868
  15.8 3.6 %collective-permute-start.7 = (f32[1,256]{1,0:T(1,128)S(1)}, f32[1,256]{1,0:T(1,128)S(1)}, u32[]{:S(2)}, u32[]{:S(2)}) collective-permute-start(f32[1,256]{1,0:T(1,128)S(1)} %get-tuple-element.65), channel_id=1, source_target_pairs={{1,2},{2,1},{3,4},{4,3},{5,6},{6,5},{7,8},{8,7},{9,10},{10,9},{11,... | collective-permute-start | bytes 3080 | tf_op jit(solution)/shard_map/ppermute | solution.py:513
  17.4 2.0 %collective-permute-start.6 = (f32[1,256]{1,0:T(1,128)S(1)}, f32[1,256]{1,0:T(1,128)S(1)}, u32[]{:S(2)}, u32[]{:S(2)}) collective-permute-start(f32[1,256]{1,0:T(1,128)S(1)} %mean_core.1), channel_id=1, source_target_pairs={{0,1},{1,0},{2,3},{3,2},{4,5},{5,4},{6,7},{7,6},{8,9},{9,8},{10,11... | collective-permute-start | bytes 3080 | tf_op jit(solution)/shard_map/ppermute | solution.py:517
  17.6 1.8 %copy-start.6 = (s32[512]{0:T(512)S(1)}, s32[512]{0:T(512)}, u32[]{:S(2)}) copy-start(s32[512]{0:T(512)} %param.23) | copy-start | bytes 6148
